TPU v7x, 32 devices: a whole 2x2x4 slice. The times are simulated.
32 devices in a mesh: groups: 2 (over y), expert: 4 (over x, core), replica: 4 (over z).
Axes of the slice: x: 2, y: 2, z: 4, core: 2. Of those that a mesh axis runs over, the one named last changes fastest.
Arguments:
- grad_rows: bfloat16 [4096, 3584], P(('groups', 'expert', 'replica')), parts along dimension 0, may hold values from -6 to 6
- grad_scale: float32 [4096], P(('groups', 'expert', 'replica')), parts along dimension 0, may hold values from 0.25 to 4
- route_probs: float32 [4096, 8], P(('groups', 'expert', 'replica')), parts along dimension 0, may hold values from 0.1 to 0.6
- expert_ids: int32 [4096, 8], P(('groups', 'expert', 'replica')), parts along dimension 0, may hold values from 0 to 15, all different within a row; in each aligned block of 128 rows (0 to 127, 128 to 255, ...) at most 72 rows name the same one
- saved_hidden: bfloat16 [8, 16, 4, 72, 1024], P(('groups', 'replica'), 'expert'), parts along dimension 0, may hold values from -6 to 6
Outputs:
- weight_grad: bfloat16 [2048, 16, 3584], P(('groups', 'replica'), 'expert'), parts along dimension 0
There are 2 independent parts, one for each index of `groups`. A program takes and returns all parts, laid end to end along the dimension named above; each array names one. Nothing has to cross between parts.
Inputs may be any that keep to these rules, and one draw needn't show every extreme that they name: `expert_ids`: each token names 8 different experts. The 128 tokens of one device name one expert at most 72 times, and in every draw some device names some expert exactly 72 times.
All inputs are finite; a program needn't handle non-finite values.
Results may differ from a plain program's by a relative error of at most 0.0095.
Values may be sent and summed in bfloat16 or wider, within the bound.
No kernel may reach another device: no remote copies, remote signals or barrier semaphores. Data moves between devices by JAX's collectives and lax.ppermute only.
A program may use at most 128 MiB of HBM per device.

v0:
```python
import math

import jax
import jax.numpy as jnp
from jax import lax
from jax.sharding import PartitionSpec as P

EXPERTS = 16


def slot_positions(expert_ids):
    flat_ids = expert_ids.reshape(-1)
    onehot = (flat_ids[:, None] == jnp.arange(EXPERTS, dtype=jnp.int32)[None, :]).astype(jnp.int32)
    running = jnp.cumsum(onehot, axis=0)
    return (flat_ids, jnp.sum(onehot * running, axis=1) - 1)


def shards(grad_rows, grad_scale, route_probs, expert_ids, saved_hidden):
    tok_rows, row_width = grad_rows.shape
    top_count = expert_ids.shape[1]
    n_expert = lax.axis_size("expert")
    n_replica = lax.axis_size("replica")
    per_device = EXPERTS // n_expert
    hidden = saved_hidden[0]
    capacity = hidden.shape[2]
    hidden_units = hidden.shape[3]
    scale_norm = 1.0 / math.sqrt(n_replica * n_expert * tok_rows * top_count / EXPERTS)
    flat_ids, position = slot_positions(expert_ids)
    pair_coef = grad_scale[:, None] * route_probs
    gathered_ids, gathered_pos = (
        lax.all_gather(expert_ids, "expert", axis=0, tiled=True),
        lax.all_gather(position.reshape(tok_rows, top_count), "expert", axis=0, tiled=True),
    )
    gathered_coef = lax.all_gather(pair_coef, "expert", axis=0, tiled=True)
    first_expert = lax.axis_index("expert") * per_device
    local_ids = first_expert + jnp.arange(per_device, dtype=jnp.int32)
    hidden_flat = hidden.reshape(per_device, n_expert * capacity, hidden_units)
    token_piece = lax.all_gather(grad_rows, "expert", axis=0, tiled=True)
    row_count = token_piece.shape[0]
    source = jnp.arange(row_count, dtype=jnp.int32) // tok_rows
    matches = gathered_ids[None, :, :] == local_ids[:, None, None]
    row_coef = jnp.sum(jnp.where(matches, gathered_coef[None], 0.0), axis=2)
    row_index = jnp.sum(
        jnp.where(matches, source[None, :, None] * capacity + gathered_pos[None], 0), axis=2
    )
    chosen = jax.vmap(lambda hidden_table, row_pick: jnp.take(hidden_table, row_pick, axis=0))(
        hidden_flat, row_index
    )
    scaled = (row_coef[:, :, None] * token_piece[None]).astype(jnp.bfloat16)
    summed = jnp.einsum("lif,lid->fld", chosen, scaled, preferred_element_type=jnp.float32)
    reduced = lax.psum_scatter(
        (summed * scale_norm).astype(jnp.bfloat16), "replica", scatter_dimension=0, tiled=True
    )
    return reduced


def solution(mesh):
    placed = (
        P(("groups", "expert", "replica"), None),
        P(("groups", "expert", "replica")),
        P(("groups", "expert", "replica"), None),
        P(("groups", "expert", "replica"), None),
        P(("groups", "replica"), "expert", None, None, None),
    )
    return jax.shard_map(
        shards,
        mesh=mesh,
        in_specs=placed,
        out_specs=P(("groups", "replica"), "expert", None),
        check_vma=False,
    )
```

profile of v0, /device:TPU:0, one launch (start us, length us, event | category | flops | bytes accessed | tf_op | source)
XLA Modules:
  0.0 592.8 jit_solution(14116124883881741759)
XLA Ops:
  6.5 0.0 copy-start
  6.5 0.0 all-gather.2.cloned.1.call-start
  6.5 0.7 all-gather.2.cloned.1.call-update
  7.3 0.0 reduce-scatter.2.cloned.1.call-start
  7.3 0.8 copy.28
  8.1 0.1 eq.45
  8.2 0.1 eq.41
  8.3 4.5 reduce-window.6
  12.8 0.1 slice.10
  12.9 0.1 copy.30
  13.1 0.1 copy.31
  13.1 0.1 broadcast_add_fusion
  13.3 0.1 sub.14
  13.4 6.3 %all_gather.12 = s32[512,8]{0,1:T(8,128)S(1)} all-gather(s32[128,8]{0,1:T(8,128)} %param.8), channel_id=1, replica_groups=mesh['groups'=2,'expert'=4,'replica'=4] {'expert'}, dimensions={0}, use_global_device_ids=true | all-gather | bytes 20480 | tf_op jit(solution)/shard_map/all_gather | solution.py:31
  19.7 5.4 all_gather.15
  25.2 0.1 fusion.7
  25.3 0.0 copy-done
  25.3 0.0 copy-start.1
  25.3 0.0 copy-start.2
  25.3 30.2 %gather_fusion = bf16[2048,1024]{1,0:T(8,128)(2,1)} fusion(bf16[4,288,1024]{2,1,0:T(8,128)(2,1)S(1)} %bitcast.24, s32[2048]{0:T(1024)S(1)} %bitcast.25), kind=kCustom, calls=%fused_computation | custom fusion | bytes 8404992 | tf_op jit(solution)/shard_map/vmap(jit(_take))/gather | solution.py:46
  55.5 0.0 copy-done.1
  55.5 0.0 copy-done.2
  55.5 5.2 all_gather.13
  60.7 0.1 fusion.6
  60.8 0.0 all-gather.2.cloned.1.call-done
  60.8 6.2 %copy.27 = f32[512,3584]{0,1:T(8,128)} copy(bf16[512,3584]{1,0:T(8,128)(2,1)} %all-gather.2.cloned.1.call-done) | data formatting | bytes 11010048 | tf_op jit(solution)/shard_map/convert_element_type | solution.py:49
  67.0 22.8 %fusion = bf16[1024,4,3584]{0,2,1:T(8,128)(2,1)} fusion(f32[512,3584]{0,1:T(8,128)} %copy.27, f32[4,512]{1,0:T(4,128)S(1)} %fusion.6, bf16[4,512,1024]{2,1,0:T(8,128)(2,1)} %bitcast.26, pred[4,512]{1,0:T(4,128)(4,1)S(1)} %compare_and_fusion), kind=kOutput, calls=%fused_computation.3 | convolution fusion | flops 15078522880 | bytes 40904704 | tf_op jit(solution)/shard_map/lif,lid->fld/dot_general | solution.py:50
  89.8 0.0 reduce-scatter.2.cloned.1.call-update
  89.8 483.3 %reduce-scatter.2.cloned.1.call-done = bf16[256,4,3584]{0,2,1:T(8,128)(2,1)} async-done(((bf16[1024,4,3584]{0,2,1:T(8,128)(2,1)}), bf16[256,4,3584]{0,2,1:T(8,128)(2,1)}) %reduce-scatter.2.cloned.1.call-update) | async-done | bytes 7340048 | tf_op jit(solution)/shard_map/reduce_scatter | solution.py:51
  573.1 12.8 %copy.33 = bf16[256,4,3584]{2,1,0:T(4,128)(2,1)} copy(bf16[256,4,3584]{0,2,1:T(8,128)(2,1)} %reduce-scatter.2.cloned.1.call-done) | data formatting | bytes 14680064 | tf_op jit(solution)/shard_map/reduce_scatter | solution.py:51
  (13 shorter events, 0.2 us)
Async XLA Ops:
  6.5 18.8 %copy-start = (bf16[1,4,4,72,1024]{4,3,2,1,0:T(8,128)(2,1)S(1)}, bf16[1,4,4,72,1024]{4,3,2,1,0:T(8,128)(2,1)}, u32[]{:S(2)}) copy-start(bf16[1,4,4,72,1024]{4,3,2,1,0:T(8,128)(2,1)} %param.9) | copy-start | bytes 7077892
  6.5 54.3 %all-gather.2.cloned.1.call-start = ((), (), s32[]{:S(2)}) async-start(), calls=%async_computation.1 | async-start | bytes 4587520 | tf_op jit(solution)/shard_map/all_gather | solution.py:38
  7.3 565.9 %reduce-scatter.2.cloned.1.call-start = ((), (), s32[]{:S(2)}) async-start(), calls=%async_computation.2 | async-start | bytes 36700160 | tf_op jit(solution)/shard_map/reduce_scatter | solution.py:51
  25.3 30.2 %copy-start.1 = (f32[128,8]{0,1:T(8,128)S(1)}, f32[128,8]{0,1:T(8,128)}, u32[]{:S(2)}) copy-start(f32[128,8]{0,1:T(8,128)} %param.7) | copy-start | bytes 12292
  25.3 30.2 %copy-start.2 = (f32[128]{0:T(128)S(1)}, f32[128]{0:T(128)}, u32[]{:S(2)}) copy-start(f32[128]{0:T(128)} %param.6) | copy-start | bytes 1540
Sparse Core Ops, SparseCore 0:
  8.9 34.2 all-gather.1
  89.9 483.1 reduce-scatter.1
where the time goes:
time: 594 us; the launch traced here: 593 us
  waiting for transfers between devices  484 us (81%)
  local copies, waits for them, and re-layouts  50.6 us (9%)
  matrix products  22.8 us (4%)
  blocking collectives  16.9 us (3%)
  between operations  13.5 us (2%)
    reduce_scatter x1, waiting for transfers between devices, shards(): lax.psum_scatter((summed * scale_norm).astype(jnp.bfloat16), 'replica', s...  483 us
    gather x1, local copies, waits for them, and re-layouts, shards(): jnp.take(hidden_table, row_pick, axis=0)  30.2 us
    dot_general x1, matrix products, shards(): jnp.einsum('lif,lid->fld', chosen, scaled, preferred_element_type=jnp.flo...  22.8 us
    reduce_scatter x1, local copies, waits for them, and re-layouts, shards(): lax.psum_scatter((summed * scale_norm).astype(jnp.bfloat16), 'replica', s...  12.8 us
  transfers between devices with their start and end apart: 2, of which 1 were waited for; matrix products, arithmetic and copies ran while one was open for 6% of the time, Pallas kernels for 0%

commit v1 on v0

--- a/solution.py
+++ b/solution.py
@@ -3,6 +3,8 @@
 import jax
 import jax.numpy as jnp
 from jax import lax
+from jax.experimental import pallas as pl
+from jax.experimental.pallas import tpu as pltpu
 from jax.sharding import PartitionSpec as P
 
 EXPERTS = 16
@@ -15,7 +17,7 @@
     return (flat_ids, jnp.sum(onehot * running, axis=1) - 1)
 
 
-def shards(grad_rows, grad_scale, route_probs, expert_ids, saved_hidden):
+def summed_shards(grad_rows, grad_scale, route_probs, expert_ids, saved_hidden):
     tok_rows, row_width = grad_rows.shape
     top_count = expert_ids.shape[1]
     n_expert = lax.axis_size("expert")
@@ -48,10 +50,193 @@
     )
     scaled = (row_coef[:, :, None] * token_piece[None]).astype(jnp.bfloat16)
     summed = jnp.einsum("lif,lid->fld", chosen, scaled, preferred_element_type=jnp.float32)
-    reduced = lax.psum_scatter(
+    return lax.psum_scatter(
         (summed * scale_norm).astype(jnp.bfloat16), "replica", scatter_dimension=0, tiled=True
     )
-    return reduced
+
+
+def spread_kernel(where_ref, hidden_ref, meta_ref, out_ref, rows_ref):
+    experts, sources, capacity, units = hidden_ref.shape
+    tok = meta_ref.shape[2]
+    me, replica = where_ref[0], where_ref[1]
+    for q in range(sources):
+        src = me ^ q
+        block = src * sources + replica
+        for j in range(experts):
+            pos = meta_ref[block, pl.ds(j, 1), :]
+            coef = meta_ref[block, pl.ds(experts + j, 1), :]
+            slot = lax.broadcasted_iota(jnp.int32, (capacity, tok), 0).astype(jnp.float32)
+            pick = jnp.where(slot == pos, 1.0, 0.0).astype(jnp.bfloat16)
+            rows = lax.dot_general(
+                hidden_ref[j, src],
+                pick,
+                (((0,), (0,)), ((), ())),
+                preferred_element_type=jnp.float32,
+            )
+            rows_ref[pl.ds(j, units, stride=experts), :] = rows * coef
+        out_ref[:, q * tok : (q + 1) * tok] = rows_ref[...].astype(out_ref.dtype)
+
+
+def spread(where, hidden, meta):
+    experts, sources, capacity, units = hidden.shape
+    tok = meta.shape[2]
+    vmem = pl.BlockSpec(memory_space=pltpu.VMEM)
+    return pl.pallas_call(
+        spread_kernel,
+        out_shape=jax.ShapeDtypeStruct((units * experts, sources * tok), jnp.bfloat16),
+        in_specs=[pl.BlockSpec(memory_space=pltpu.SMEM), vmem, vmem],
+        out_specs=vmem,
+        scratch_shapes=[pltpu.VMEM((units * experts, tok), jnp.float32)],
+        compiler_params=pltpu.CompilerParams(vmem_limit_bytes=16 << 20),
+        cost_estimate=pl.CostEstimate(
+            flops=2 * sources * experts * units * tok * capacity * 2,
+            bytes_accessed=hidden.size * 2 + units * experts * sources * tok * 2,
+            transcendentals=0,
+        ),
+    )(where, hidden, meta)
+
+
+def product(flag, spreads, rows, other=None, acc=None, last=False, experts=4, tile=512):
+    n_tok, width = rows[0].shape
+    m = spreads[0].shape[0]
+    steps = width // tile
+    sets = [rows] + ([other] if other is not None else [])
+
+    def body(flag_ref, *refs):
+        refs = list(refs)
+        lhs = [refs.pop(0) for _ in spreads]
+        held = [[refs.pop(0) for _ in group] for group in sets]
+        before = refs.pop(0) if acc is not None else None
+        out = refs.pop(0)
+        k = jnp.concatenate([r[...] for r in held[0]], axis=0)
+        if other is not None:
+            k2 = jnp.concatenate([r[...] for r in held[1]], axis=0)
+            k = jnp.where(flag_ref[0] == 1, k, k2)
+        left = jnp.concatenate([r[...] for r in lhs], axis=1) if len(lhs) > 1 else lhs[0][...]
+        total = jnp.dot(left, k, preferred_element_type=jnp.float32)
+        if before is not None:
+            total = total + before[...]
+        if last:
+            out[...] = total.reshape(m // experts, experts, tile).astype(out.dtype)
+        else:
+            out[...] = total
+
+    in_specs = [pl.BlockSpec(s.shape, lambda i, f: (0, 0)) for s in spreads]
+    for n, group in enumerate(sets):
+        if other is None:
+            pick = lambda i, f: (0, i)
+        elif n == 0:
+            pick = lambda i, f: (0, i * f[0])
+        else:
+            pick = lambda i, f: (0, i * (1 - f[0]))
+        in_specs += [pl.BlockSpec((n_tok, tile), pick) for _ in group]
+    args = list(spreads) + [r for group in sets for r in group]
+    aliases = {}
+    if acc is not None:
+        in_specs.append(pl.BlockSpec((m, tile), lambda i, f: (0, i)))
+        if not last:
+            aliases = {1 + len(args): 0}
+        args.append(acc)
+    if last:
+        out_shape = jax.ShapeDtypeStruct((m // experts, experts, width), jnp.bfloat16)
+        out_spec = pl.BlockSpec((m // experts, experts, tile), lambda i, f: (0, 0, i))
+    else:
+        out_shape = jax.ShapeDtypeStruct((m, width), jnp.float32)
+        out_spec = pl.BlockSpec((m, tile), lambda i, f: (0, i))
+    k = sum(s.shape[1] for s in spreads)
+    return pl.pallas_call(
+        body,
+        grid_spec=pltpu.PrefetchScalarGridSpec(
+            num_scalar_prefetch=1, grid=(steps,), in_specs=in_specs, out_specs=out_spec
+        ),
+        out_shape=out_shape,
+        input_output_aliases=aliases,
+        compiler_params=pltpu.CompilerParams(vmem_limit_bytes=40 << 20),
+        cost_estimate=pl.CostEstimate(
+            flops=2 * m * k * width,
+            bytes_accessed=m * width * 4 + k * width * 2,
+            transcendentals=0,
+        ),
+    )(flag, *args)
+
+
+def gathered_shards(grad_rows, grad_scale, route_probs, expert_ids, saved_hidden):
+    tok, width = grad_rows.shape
+    top_count = expert_ids.shape[1]
+    n_expert = lax.axis_size("expert")
+    n_replica = lax.axis_size("replica")
+    per_device = EXPERTS // n_expert
+    hidden = saved_hidden[0]
+    units = hidden.shape[3] // n_replica
+    scale_norm = 1.0 / math.sqrt(n_replica * n_expert * tok * top_count / EXPERTS)
+    e = lax.axis_index("expert")
+    z = lax.axis_index("replica")
+    both = ("expert", "replica")
+
+    def send(array, expert_to, moves):
+        pairs = [
+            (a * n_replica + i, expert_to(a) * n_replica + j)
+            for a in range(n_expert)
+            for i, j in moves
+        ]
+        return lax.ppermute(array, both, pairs)
+
+    stay = [(i, i) for i in range(4)]
+    near = [(0, 1), (1, 0), (2, 3), (3, 2)]
+    middle = [(1, 2), (2, 1)]
+    outward = [(1, 0), (2, 3)]
+    same = lambda a: a
+    inner = (z == 1) | (z == 2)
+
+    own = grad_rows
+    pair = send(own, same, near)
+    mid_a = send(own, same, middle)
+    mid_b = send(pair, same, middle)
+    end_a = send(mid_a, same, outward)
+    end_b = send(mid_b, same, outward)
+    far_a = jnp.where(inner, mid_a, end_a)
+    far_b = jnp.where(inner, mid_b, end_b)
+
+    def around(rows):
+        across = send(rows, lambda a: a ^ 2, stay)
+        return [rows, send(rows, lambda a: a ^ 1, stay), across, send(across, lambda a: a ^ 1, stay)]
+
+    ids = expert_ids.T
+    named = ids[None, :, :] == jnp.arange(EXPERTS, dtype=jnp.int32)[:, None, None]
+    mask = jnp.any(named, axis=1)
+    coef = jnp.sum(jnp.where(named, (route_probs.T * grad_scale[None, :])[None], 0.0), axis=1)
+    before = jnp.arange(tok)[:, None] < jnp.arange(tok)[None, :]
+    place = jnp.dot(
+        mask.astype(jnp.bfloat16), before.astype(jnp.bfloat16), preferred_element_type=jnp.float32
+    )
+    place = jnp.where(mask, place, -1.0)
+    meta = jnp.stack([place, coef * scale_norm]).reshape(2, n_expert, per_device, tok)
+    meta = lax.all_gather(meta, both, axis=0, tiled=False)
+    meta = lax.dynamic_index_in_dim(meta, e, 2, keepdims=False)
+    meta = meta.reshape(n_expert * n_replica, 2 * per_device, tok)
+
+    def units_of(replica):
+        return lax.dynamic_slice_in_dim(hidden, replica * units, units, 3)
+
+    h_own = units_of(z)
+    h_pair = send(units_of(z ^ 1), same, near)
+    h_two = send(units_of(z ^ 2), same, [(i, i ^ 2) for i in range(4)])
+    h_flip = send(units_of(z ^ 3), same, [(i, i ^ 3) for i in range(4)])
+
+    def place_of(replica):
+        return jnp.stack([e, replica]).astype(jnp.int32)
+
+    s_own = spread(place_of(z), h_own, meta)
+    s_pair = spread(place_of(z ^ 1), h_pair, meta)
+    s_two = spread(place_of(z ^ 2), h_two, meta)
+    s_flip = spread(place_of(z ^ 3), h_flip, meta)
+
+    near_rows = around(own) + around(pair)
+    rows_a, rows_b = around(far_a), around(far_b)
+    ends = jnp.where(inner, 0, 1).astype(jnp.int32)[None]
+    acc = product(ends, [s_own, s_pair], near_rows)
+    acc = product(ends, [s_two], rows_a, rows_b, acc)
+    return product(1 - ends, [s_flip], rows_a, rows_b, acc, last=True, experts=per_device)
 
 
 def solution(mesh):
@@ -62,8 +247,9 @@
         P(("groups", "expert", "replica"), None),
         P(("groups", "replica"), "expert", None, None, None),
     )
+    small = mesh.shape["expert"] == 4 and mesh.shape["replica"] == 4
     return jax.shard_map(
-        shards,
+        gathered_shards if small else summed_shards,
         mesh=mesh,
         in_specs=placed,
         out_specs=P(("groups", "replica"), "expert", None),

time: 594 us -> 222 us (0.37)
  waiting for transfers between devices: 484 us -> 91.4 us
  Pallas kernels: 0 us -> 48.2 us
  local copies, waits for them, and re-layouts: 50.6 us -> 9.76 us
  starting transfers between devices: 0.04 us -> 33.1 us
  matrix products: 22.8 us -> 0.13 us
  blocking collectives: 16.9 us -> 34.5 us
  between operations: 13.5 us -> 0.21 us
    reduce_scatter x1 -> x0, waiting for transfers between devices: 483 us -> none  [shards(): lax.psum_scatter((summed * scale_norm).astype(jnp.bfloat16), 'replica', s...]
    ppermute x0 -> x20, waiting for transfers between devices: none -> 91.4 us  [send(): return lax.ppermute(array, both, pairs)]
    pallas_call x0 -> x7, Pallas kernels: none -> 48.2 us  [the longest x3 43.7 us: product(): pl.pallas_call(body, grid_spec=pltpu.PrefetchScalarGridSpec(num_scalar_pr...]
    ppermute x0 -> x20, starting transfers between devices: none -> 33.1 us  [send(): return lax.ppermute(array, both, pairs)]
    gather x1 -> x0, local copies, waits for them, and re-layouts: 30.2 us -> none  [shards(): jnp.take(hidden_table, row_pick, axis=0)]
    dot_general x1, matrix products: 22.8 us -> 0.13 us  [gathered_shards(): jnp.dot(mask.astype(jnp.bfloat16), before.astype(jnp.bfloat16), preferred...]
    all_gather x3 -> x1, blocking collectives: 16.9 us -> 34.5 us  [gathered_shards(): meta = lax.all_gather(meta, both, axis=0, tiled=False)]
    reduce_scatter x1 -> x0, local copies, waits for them, and re-layouts: 12.8 us -> none  [shards(): lax.psum_scatter((summed * scale_norm).astype(jnp.bfloat16), 'replica', s...]
  transfers between devices with their start and end apart: 2 -> 20, of which waited for: 1 -> 6; matrix products, arithmetic and copies ran while one was open for 6% -> 3% of each run, Pallas kernels for 0% -> 8%
where the time goes in v1:
time: 222 us; the launch traced here: 221 us
  waiting for transfers between devices  91.4 us (41%)
  Pallas kernels  48.2 us (22%)
  blocking collectives  34.5 us (16%)
  starting transfers between devices  33.1 us (15%)
  local copies, waits for them, and re-layouts  9.76 us (4%)
  other arithmetic  3.82 us (2%)
    ppermute x20, waiting for transfers between devices, send(): return lax.ppermute(array, both, pairs)  91.4 us
    pallas_call x3, Pallas kernels, product(): pl.pallas_call(body, grid_spec=pltpu.PrefetchScalarGridSpec(num_scalar_pr...  43.7 us
    all_gather x1, blocking collectives, gathered_shards(): meta = lax.all_gather(meta, both, axis=0, tiled=False)  34.5 us
    ppermute x20, starting transfers between devices, send(): return lax.ppermute(array, both, pairs)  33.1 us
    unnamed x16, local copies, waits for them, and re-layouts  6.84 us
    pallas_call x4, Pallas kernels, spread(): pl.pallas_call(spread_kernel, out_shape=jax.ShapeDtypeStruct((units * exp...  4.55 us
  transfers between devices with their start and end apart: 20, of which 6 were waited for; matrix products, arithmetic and copies ran while one was open for 3% of the time, Pallas kernels for 8%

profile of v1, /device:TPU:0, one launch (start us, length us, event | category | flops | bytes accessed | tf_op | source)
XLA Modules:
  0.0 221.2 jit_solution(8261075917675651760)
XLA Ops:
  0.0 3.0 %collective-permute-start.6 = (bf16[128,3584]{1,0:T(8,128)(2,1)}, bf16[128,3584]{1,0:T(8,128)(2,1)}, u32[]{:S(2)}, u32[]{:S(2)}) collective-permute-start(bf16[128,3584]{1,0:T(8,128)(2,1)} %refs_2_.1), channel_id=1, source_target_pairs={{0,1},{1,0},{2,3},{3,2},{4,5},{5,4},{6,7},{7,6},{8,9},{9,8},{10,11... | collective-permute-start | bytes 2752520 | tf_op jit(solution)/shard_map/ppermute | solution.py:182
  3.7 19.9 %collective-permute-done.6.refs_6_ = bf16[128,3584]{1,0:T(8,128)(2,1)} collective-permute-done((bf16[128,3584]{1,0:T(8,128)(2,1)}, bf16[128,3584]{1,0:T(8,128)(2,1)}, u32[]{:S(2)}, u32[]{:S(2)}) %collective-permute-start.6) | collective-permute-done | bytes 917536 | tf_op jit(solution)/shard_map/ppermute | solution.py:182
  24.4 1.3 collective-permute-start.2
  25.7 1.7 collective-permute-start.15
  27.5 2.9 %dynamic-slice_bitcast_fusion = (bf16[4,4,72,256]{3,2,1,0:T(8,128)(2,1)}, bf16[4,4,72,256]{3,2,1,0:T(8,128)(2,1)}, bf16[4,4,72,256]{3,2,1,0:T(8,128)(2,1)}, bf16[4,4,72,256]{3,2,1,0:T(8,128)(2,1)S(1)}) fusion(bf16[1,4,4,72,1024]{4,3,2,1,0:T(8,128)(2,1)} %param.9, s32[]{:T(128)S(6)} %select_n.50, s32[]{:T(128)S(6)} %select_n.48, s32[]{:T(128)S(6)} %select_n.41, ...), kind=kLoop, calls=%fused_computation.3 | loop fusion | bytes 4718608 | tf_op jit(solution)/shard_map/dynamic_slice | solution.py:219
  30.4 5.2 %collective-permute-start.13 = (bf16[4,4,72,256]{3,2,1,0:T(8,128)(2,1)}, bf16[4,4,72,256]{3,2,1,0:T(8,128)(2,1)S(1)}, u32[]{:S(2)}, u32[]{:S(2)}) collective-permute-start(bf16[4,4,72,256]{3,2,1,0:T(8,128)(2,1)} %get-tuple-element.5), channel_id=1, source_target_pairs={{0,1},{1,0},{2,3},{3,2},{4,5},{5,4},{6,7},{7,6},{8,9},{9,8},{10,11... | collective-permute-start | bytes 1769480 | tf_op jit(solution)/shard_map/ppermute | solution.py:182
  37.7 12.3 %collective-permute-start.12 = (bf16[4,4,72,256]{3,2,1,0:T(8,128)(2,1)}, bf16[4,4,72,256]{3,2,1,0:T(8,128)(2,1)S(1)}, u32[]{:S(2)}, u32[]{:S(2)}) collective-permute-start(bf16[4,4,72,256]{3,2,1,0:T(8,128)(2,1)} %get-tuple-element.6), channel_id=1, source_target_pairs={{0,2},{1,3},{2,0},{3,1},{4,6},{5,7},{6,4},{7,5},{8,10},{9,11},{10,... | collective-permute-start | bytes 1769480 | tf_op jit(solution)/shard_map/ppermute | solution.py:182
  50.0 4.2 %collective-permute-done.2 = bf16[128,3584]{1,0:T(8,128)(2,1)} collective-permute-done((bf16[128,3584]{1,0:T(8,128)(2,1)S(1)}, bf16[128,3584]{1,0:T(8,128)(2,1)}, u32[]{:S(2)}, u32[]{:S(2)}) %collective-permute-start.2) | collective-permute-done | bytes 917536 | tf_op jit(solution)/shard_map/ppermute | solution.py:182
  54.2 1.3 collective-permute-start.8
  55.5 1.3 broadcast_select_fusion.1.refs_1_
  56.8 26.2 %collective-permute-done.13.hidden_ref = bf16[4,4,72,256]{3,2,1,0:T(8,128)(2,1)S(1)} collective-permute-done((bf16[4,4,72,256]{3,2,1,0:T(8,128)(2,1)}, bf16[4,4,72,256]{3,2,1,0:T(8,128)(2,1)S(1)}, u32[]{:S(2)}, u32[]{:S(2)}) %collective-permute-start.13) | collective-permute-done | bytes 589856 | tf_op jit(solution)/shard_map/ppermute | solution.py:182
  83.0 0.8 copy-done
  83.8 2.1 collective-permute-start
  85.9 21.0 %collective-permute-done.8 = bf16[128,3584]{1,0:T(8,128)(2,1)S(1)} collective-permute-done((bf16[128,3584]{1,0:T(8,128)(2,1)S(1)}, bf16[128,3584]{1,0:T(8,128)(2,1)S(1)}, u32[]{:S(2)}, u32[]{:S(2)}) %collective-permute-start.8) | collective-permute-done | bytes 917536 | tf_op jit(solution)/shard_map/ppermute | solution.py:182
  107.0 1.5 collective-permute-start.18
  108.6 0.8 copy-done.2
  110.0 0.8 copy-done.4
  111.3 1.5 collective-permute-start.10
  113.0 17.6 %collective-permute-done.18.refs_8_ = bf16[128,3584]{1,0:T(8,128)(2,1)} collective-permute-done((bf16[128,3584]{1,0:T(8,128)(2,1)}, bf16[128,3584]{1,0:T(8,128)(2,1)}, u32[]{:S(2)}, u32[]{:S(2)}) %collective-permute-start.18) | collective-permute-done | bytes 917536 | tf_op jit(solution)/shard_map/ppermute | solution.py:182
  130.7 34.5 %all_gather.3 = f32[16,2,4,4,128]{4,3,1,0,2:T(4,128)S(1)} all-gather(f32[1,2,4,4,128]{4,3,1,0,2:T(4,128)S(1)} %pad_maximum_fusion), channel_id=1, replica_groups=mesh['groups'=2,'expert'=4,'replica'=4] {'expert','replica'}, dimensions={0}, use_global_device_ids=true | all-gather | bytes 278528 | tf_op jit(solution)/shard_map/all_gather | solution.py:214
  165.9 2.4 %collective-permute-done.10.refs_7_ = bf16[128,3584]{1,0:T(8,128)(2,1)} collective-permute-done((bf16[128,3584]{1,0:T(8,128)(2,1)S(1)}, bf16[128,3584]{1,0:T(8,128)(2,1)}, u32[]{:S(2)}, u32[]{:S(2)}) %collective-permute-start.10) | collective-permute-done | bytes 917536 | tf_op jit(solution)/shard_map/ppermute | solution.py:182
  168.4 1.1 shard_map.57.refs_0_
  169.6 1.1 copy-done.1
  170.7 1.1 shard_map.58.refs_1_
  171.9 1.1 copy-done.3
  172.9 1.1 shard_map.56.refs_0_
  174.1 1.1 copy-done.5
  175.1 1.1 shard_map.55.refs_0_
  176.3 1.2 copy-done.6
  177.5 13.7 %shard_map.59.refs_9_ = f32[1024,3584]{1,0:T(8,128)} custom-call(s32[1]{0:T(128)} %bitcast.flag_ref, bf16[1024,512]{1,0:T(8,128)(2,1)S(1)} %shard_map.57.refs_0_, bf16[1024,512]{1,0:T(8,128)(2,1)S(1)} %shard_map.58.refs_1_, bf16[128,3584]{1,0:T(8,128)(2,1)S(1)} %copy-done.6, bf16[128,3584]{1,0:T(8,128)(2,1)} %collective-permute-done.14.refs_3_, ...), custom_call_target="tpu_custom_call" | custom-call | flops 7516192768 | bytes 22020096 | tf_op jit(solution)/shard_map/pallas_call | solution.py:147
  191.2 16.0 %shard_map.60.refs_9_ = f32[1024,3584]{1,0:T(8,128)} custom-call(s32[1]{0:T(128)} %bitcast.flag_ref, bf16[1024,512]{1,0:T(8,128)(2,1)S(1)} %shard_map.56.refs_0_, bf16[128,3584]{1,0:T(8,128)(2,1)S(1)} %broadcast_select_fusion.1.refs_1_, bf16[128,3584]{1,0:T(8,128)(2,1)} %collective-permute-done.3.refs_2_, ...), custom_call_target="tpu_custom_call", output_to_operand_aliasing={{}: (10, {})} | custom-call | flops 3758096384 | bytes 18350080 | tf_op jit(solution)/shard_map/pallas_call | solution.py:147
  207.2 14.0 %shard_map.61 = bf16[256,4,3584]{2,1,0:T(4,128)(2,1)} custom-call(s32[1]{0:T(128)S(6)} %sub.3.flag_ref, bf16[1024,512]{1,0:T(8,128)(2,1)S(1)} %shard_map.55.refs_0_, bf16[128,3584]{1,0:T(8,128)(2,1)S(1)} %broadcast_select_fusion.1.refs_1_, bf16[128,3584]{1,0:T(8,128)(2,1)} %collective-permute-done.3.refs_2_, ...), custom_call_target="tpu_custom_call" | custom-call | flops 3758096384 | bytes 18350080 | tf_op jit(solution)/shard_map/pallas_call | solution.py:147
  (46 shorter events, 5.8 us)
Async XLA Ops:
  0.0 23.7 %collective-permute-start.6 = (bf16[128,3584]{1,0:T(8,128)(2,1)}, bf16[128,3584]{1,0:T(8,128)(2,1)}, u32[]{:S(2)}, u32[]{:S(2)}) collective-permute-start(bf16[128,3584]{1,0:T(8,128)(2,1)} %refs_2_.1), channel_id=1, source_target_pairs={{0,1},{1,0},{2,3},{3,2},{4,5},{5,4},{6,7},{7,6},{8,9},{9,8},{10,11... | collective-permute-start | bytes 2752520 | tf_op jit(solution)/shard_map/ppermute | solution.py:182
  3.0 21.4 %collective-permute-start.1 = (bf16[128,3584]{1,0:T(8,128)(2,1)}, bf16[128,3584]{1,0:T(8,128)(2,1)S(1)}, u32[]{:S(2)}, u32[]{:S(2)}) collective-permute-start(bf16[128,3584]{1,0:T(8,128)(2,1)} %refs_2_.1), channel_id=1, source_target_pairs={{1,2},{2,1},{5,6},{6,5},{9,10},{10,9},{13,14},{14,13},{17,18},{18,... | collective-permute-start | bytes 2752520 | tf_op jit(solution)/shard_map/ppermute | solution.py:182
  23.7 14.0 %collective-permute-start.7 = (bf16[128,3584]{1,0:T(8,128)(2,1)}, bf16[128,3584]{1,0:T(8,128)(2,1)S(1)}, u32[]{:S(2)}, u32[]{:S(2)}) collective-permute-start(bf16[128,3584]{1,0:T(8,128)(2,1)} %collective-permute-done.6.refs_6_), channel_id=1, source_target_pairs={{1,2},{2,1},{5,6},{6,5},{9,10},{10,9},{13,14},{14,13},{17,18},{18,... | collective-permute-start | bytes 2752520 | tf_op jit(solution)/shard_map/ppermute | solution.py:182
  24.4 29.8 %copy-start.7 = (bf16[128,3584]{1,0:T(8,128)(2,1)}, bf16[128,3584]{1,0:T(8,128)(2,1)S(1)}, u32[]{:S(2)}) copy-start(bf16[128,3584]{1,0:T(8,128)(2,1)S(1)} %collective-permute-done.1) | copy-start | bytes 2752516
  24.4 29.8 %collective-permute-start.2 = (bf16[128,3584]{1,0:T(8,128)(2,1)S(1)}, bf16[128,3584]{1,0:T(8,128)(2,1)}, u32[]{:S(2)}, u32[]{:S(2)}) collective-permute-start(bf16[128,3584]{1,0:T(8,128)(2,1)S(1)} %collective-permute-done.1), channel_id=1, source_target_pairs={{1,0},{2,3},{5,4},{6,7},{9,8},{10,11},{13,12},{14,15},{17,16},{18,... | collective-permute-start | bytes 2752520 | tf_op jit(solution)/shard_map/ppermute | solution.py:182
  25.7 83.7 %collective-permute-start.15 = (bf16[128,3584]{1,0:T(8,128)(2,1)}, bf16[128,3584]{1,0:T(8,128)(2,1)}, u32[]{:S(2)}, u32[]{:S(2)}) collective-permute-start(bf16[128,3584]{1,0:T(8,128)(2,1)} %refs_2_.1), channel_id=1, source_target_pairs={{0,8},{1,9},{2,10},{3,11},{4,12},{5,13},{6,14},{7,15},{8,0},{9,1},... | collective-permute-start | bytes 2752520 | tf_op jit(solution)/shard_map/ppermute | solution.py:182
  27.4 83.9 %collective-permute-start.14 = (bf16[128,3584]{1,0:T(8,128)(2,1)}, bf16[128,3584]{1,0:T(8,128)(2,1)}, u32[]{:S(2)}, u32[]{:S(2)}) collective-permute-start(bf16[128,3584]{1,0:T(8,128)(2,1)} %refs_2_.1), channel_id=1, source_target_pairs={{0,4},{1,5},{2,6},{3,7},{4,0},{5,1},{6,2},{7,3},{8,12},{9,13},{10,... | collective-permute-start | bytes 2752520 | tf_op jit(solution)/shard_map/ppermute | solution.py:182
  30.4 52.6 %collective-permute-start.13 = (bf16[4,4,72,256]{3,2,1,0:T(8,128)(2,1)}, bf16[4,4,72,256]{3,2,1,0:T(8,128)(2,1)S(1)}, u32[]{:S(2)}, u32[]{:S(2)}) collective-permute-start(bf16[4,4,72,256]{3,2,1,0:T(8,128)(2,1)} %get-tuple-element.5), channel_id=1, source_target_pairs={{0,1},{1,0},{2,3},{3,2},{4,5},{5,4},{6,7},{7,6},{8,9},{9,8},{10,11... | collective-permute-start | bytes 1769480 | tf_op jit(solution)/shard_map/ppermute | solution.py:182
  37.7 70.9 %collective-permute-start.12 = (bf16[4,4,72,256]{3,2,1,0:T(8,128)(2,1)}, bf16[4,4,72,256]{3,2,1,0:T(8,128)(2,1)S(1)}, u32[]{:S(2)}, u32[]{:S(2)}) collective-permute-start(bf16[4,4,72,256]{3,2,1,0:T(8,128)(2,1)} %get-tuple-element.6), channel_id=1, source_target_pairs={{0,2},{1,3},{2,0},{3,1},{4,6},{5,7},{6,4},{7,5},{8,10},{9,11},{10,... | collective-permute-start | bytes 1769480 | tf_op jit(solution)/shard_map/ppermute | solution.py:182
  54.2 52.8 %collective-permute-start.8 = (bf16[128,3584]{1,0:T(8,128)(2,1)S(1)}, bf16[128,3584]{1,0:T(8,128)(2,1)S(1)}, u32[]{:S(2)}, u32[]{:S(2)}) collective-permute-start(bf16[128,3584]{1,0:T(8,128)(2,1)S(1)} %collective-permute-done.7), channel_id=1, source_target_pairs={{1,0},{2,3},{5,4},{6,7},{9,8},{10,11},{13,12},{14,15},{17,16},{18,... | collective-permute-start | bytes 2752520 | tf_op jit(solution)/shard_map/ppermute | solution.py:182
  83.0 0.8 copy-start
  83.8 26.2 %collective-permute-start = (bf16[4,4,72,256]{3,2,1,0:T(8,128)(2,1)}, bf16[4,4,72,256]{3,2,1,0:T(8,128)(2,1)S(1)}, u32[]{:S(2)}, u32[]{:S(2)}) collective-permute-start(bf16[4,4,72,256]{3,2,1,0:T(8,128)(2,1)} %get-tuple-element.7), channel_id=1, source_target_pairs={{0,3},{1,2},{2,1},{3,0},{4,7},{5,6},{6,5},{7,4},{8,11},{9,10},{10,... | collective-permute-start | bytes 1769480 | tf_op jit(solution)/shard_map/ppermute | solution.py:182
  107.0 23.6 %collective-permute-start.18 = (bf16[128,3584]{1,0:T(8,128)(2,1)}, bf16[128,3584]{1,0:T(8,128)(2,1)}, u32[]{:S(2)}, u32[]{:S(2)}) collective-permute-start(bf16[128,3584]{1,0:T(8,128)(2,1)} %collective-permute-done.6.refs_6_), channel_id=1, source_target_pairs={{0,8},{1,9},{2,10},{3,11},{4,12},{5,13},{6,14},{7,15},{8,0},{9,1},... | collective-permute-start | bytes 2752520 | tf_op jit(solution)/shard_map/ppermute | solution.py:182
  108.6 0.8 copy-start.2
  109.4 55.8 %collective-permute-start.17 = (bf16[128,3584]{1,0:T(8,128)(2,1)}, bf16[128,3584]{1,0:T(8,128)(2,1)}, u32[]{:S(2)}, u32[]{:S(2)}) collective-permute-start(bf16[128,3584]{1,0:T(8,128)(2,1)} %collective-permute-done.6.refs_6_), channel_id=1, source_target_pairs={{0,4},{1,5},{2,6},{3,7},{4,0},{5,1},{6,2},{7,3},{8,12},{9,13},{10,... | collective-permute-start | bytes 2752520 | tf_op jit(solution)/shard_map/ppermute | solution.py:182
  109.4 55.9 %collective-permute-start.16 = (bf16[128,3584]{1,0:T(8,128)(2,1)}, bf16[128,3584]{1,0:T(8,128)(2,1)}, u32[]{:S(2)}, u32[]{:S(2)}) collective-permute-start(bf16[128,3584]{1,0:T(8,128)(2,1)} %collective-permute-done.15.refs_4_), channel_id=1, source_target_pairs={{0,4},{1,5},{2,6},{3,7},{4,0},{5,1},{6,2},{7,3},{8,12},{9,13},{10,... | collective-permute-start | bytes 2752520 | tf_op jit(solution)/shard_map/ppermute | solution.py:182
  110.0 0.8 copy-start.4
  110.8 55.0 %collective-permute-start.4 = (bf16[128,3584]{1,0:T(8,128)(2,1)S(1)}, bf16[128,3584]{1,0:T(8,128)(2,1)S(1)}, u32[]{:S(2)}, u32[]{:S(2)}) collective-permute-start(bf16[128,3584]{1,0:T(8,128)(2,1)S(1)} %broadcast_select_fusion.1.refs_1_), channel_id=1, source_target_pairs={{0,8},{1,9},{2,10},{3,11},{4,12},{5,13},{6,14},{7,15},{8,0},{9,1},... | collective-permute-start | bytes 2752520 | tf_op jit(solution)/shard_map/ppermute | solution.py:182
  111.3 57.0 %collective-permute-start.10 = (bf16[128,3584]{1,0:T(8,128)(2,1)S(1)}, bf16[128,3584]{1,0:T(8,128)(2,1)}, u32[]{:S(2)}, u32[]{:S(2)}) collective-permute-start(bf16[128,3584]{1,0:T(8,128)(2,1)S(1)} %broadcast_select_fusion.refs_5_), channel_id=1, source_target_pairs={{0,8},{1,9},{2,10},{3,11},{4,12},{5,13},{6,14},{7,15},{8,0},{9,1},... | collective-permute-start | bytes 2752520 | tf_op jit(solution)/shard_map/ppermute | solution.py:182
  130.6 45.7 %collective-permute-start.19 = (bf16[128,3584]{1,0:T(8,128)(2,1)}, bf16[128,3584]{1,0:T(8,128)(2,1)}, u32[]{:S(2)}, u32[]{:S(2)}) collective-permute-start(bf16[128,3584]{1,0:T(8,128)(2,1)} %collective-permute-done.18.refs_8_), channel_id=1, source_target_pairs={{0,4},{1,5},{2,6},{3,7},{4,0},{5,1},{6,2},{7,3},{8,12},{9,13},{10,... | collective-permute-start | bytes 2752520 | tf_op jit(solution)/shard_map/ppermute | solution.py:182
  165.2 25.9 %collective-permute-start.3 = (bf16[128,3584]{1,0:T(8,128)(2,1)S(1)}, bf16[128,3584]{1,0:T(8,128)(2,1)}, u32[]{:S(2)}, u32[]{:S(2)}) collective-permute-start(bf16[128,3584]{1,0:T(8,128)(2,1)S(1)} %broadcast_select_fusion.1.refs_1_), channel_id=1, source_target_pairs={{0,4},{1,5},{2,6},{3,7},{4,0},{5,1},{6,2},{7,3},{8,12},{9,13},{10,... | collective-permute-start | bytes 2752520 | tf_op jit(solution)/shard_map/ppermute | solution.py:182
  165.3 25.8 %collective-permute-start.9 = (bf16[128,3584]{1,0:T(8,128)(2,1)S(1)}, bf16[128,3584]{1,0:T(8,128)(2,1)}, u32[]{:S(2)}, u32[]{:S(2)}) collective-permute-start(bf16[128,3584]{1,0:T(8,128)(2,1)S(1)} %broadcast_select_fusion.refs_5_), channel_id=1, source_target_pairs={{0,4},{1,5},{2,6},{3,7},{4,0},{5,1},{6,2},{7,3},{8,12},{9,13},{10,... | collective-permute-start | bytes 2752520 | tf_op jit(solution)/shard_map/ppermute | solution.py:182
  165.8 25.3 %collective-permute-start.5 = (bf16[128,3584]{1,0:T(8,128)(2,1)S(1)}, bf16[128,3584]{1,0:T(8,128)(2,1)}, u32[]{:S(2)}, u32[]{:S(2)}) collective-permute-start(bf16[128,3584]{1,0:T(8,128)(2,1)S(1)} %collective-permute-done.4.refs_3_), channel_id=1, source_target_pairs={{0,4},{1,5},{2,6},{3,7},{4,0},{5,1},{6,2},{7,3},{8,12},{9,13},{10,... | collective-permute-start | bytes 2752520 | tf_op jit(solution)/shard_map/ppermute | solution.py:182
  168.3 22.8 %collective-permute-start.11 = (bf16[128,3584]{1,0:T(8,128)(2,1)}, bf16[128,3584]{1,0:T(8,128)(2,1)}, u32[]{:S(2)}, u32[]{:S(2)}) collective-permute-start(bf16[128,3584]{1,0:T(8,128)(2,1)} %collective-permute-done.10.refs_7_), channel_id=1, source_target_pairs={{0,4},{1,5},{2,6},{3,7},{4,0},{5,1},{6,2},{7,3},{8,12},{9,13},{10,... | collective-permute-start | bytes 2752520 | tf_op jit(solution)/shard_map/ppermute | solution.py:182
  169.6 1.1 copy-start.1
  171.8 1.1 copy-start.3
  174.1 1.1 copy-start.5
  176.3 1.2 copy-start.6

commit v2 on v0

--- a/solution.py
+++ b/solution.py
@@ -1,11 +1,15 @@
+import functools
 import math
 
 import jax
 import jax.numpy as jnp
 from jax import lax
+from jax.experimental import pallas as pl
+from jax.experimental.pallas import tpu as pltpu
 from jax.sharding import PartitionSpec as P
 
 EXPERTS = 16
+ACC = jnp.bfloat16
 
 
 def slot_positions(expert_ids):
@@ -15,7 +19,7 @@
     return (flat_ids, jnp.sum(onehot * running, axis=1) - 1)
 
 
-def shards(grad_rows, grad_scale, route_probs, expert_ids, saved_hidden):
+def summed_shards(grad_rows, grad_scale, route_probs, expert_ids, saved_hidden):
     tok_rows, row_width = grad_rows.shape
     top_count = expert_ids.shape[1]
     n_expert = lax.axis_size("expert")
@@ -48,10 +52,276 @@
     )
     scaled = (row_coef[:, :, None] * token_piece[None]).astype(jnp.bfloat16)
     summed = jnp.einsum("lif,lid->fld", chosen, scaled, preferred_element_type=jnp.float32)
-    reduced = lax.psum_scatter(
+    return lax.psum_scatter(
         (summed * scale_norm).astype(jnp.bfloat16), "replica", scatter_dimension=0, tiled=True
     )
-    return reduced
+
+
+def label_kernel(scale_norm, rows_ref, scale_ref, probs_ref, ids_ref, out_ref):
+    tok, width = rows_ref.shape
+    out_ref[:, :width] = rows_ref[...]
+    coef = probs_ref[...] * scale_ref[...] * scale_norm
+    ids = ids_ref[...]
+    masks, coefs = [], []
+    for j in range(EXPERTS):
+        named = ids == j
+        masks.append(jnp.sum(jnp.where(named, 1.0, 0.0), axis=0, keepdims=True))
+        coefs.append(jnp.sum(jnp.where(named, coef, 0.0), axis=0, keepdims=True))
+    mask = jnp.concatenate(masks, axis=0)
+    coef = jnp.concatenate(coefs, axis=0)
+    row = lax.broadcasted_iota(jnp.int32, (tok, tok), 0)
+    col = lax.broadcasted_iota(jnp.int32, (tok, tok), 1)
+    before = jnp.where(row < col, 1.0, 0.0).astype(jnp.bfloat16)
+    place = jnp.dot(mask.astype(jnp.bfloat16), before, preferred_element_type=jnp.float32)
+    place = jnp.where(mask > 0.0, place, -1.0)
+    high = coef.astype(jnp.bfloat16).astype(jnp.float32)
+    mid = (coef - high).astype(jnp.bfloat16).astype(jnp.float32)
+    low = coef - high - mid
+    rest = jnp.zeros((tok - 4 * EXPERTS, tok), jnp.float32)
+    labels = jnp.concatenate([place, high, mid, low, rest], axis=0)
+    out_ref[:, width:] = labels.T.astype(out_ref.dtype)
+
+
+def labelled(grad_rows, grad_scale, route_probs, expert_ids, scale_norm):
+    tok, width = grad_rows.shape
+    return pl.pallas_call(
+        functools.partial(label_kernel, scale_norm),
+        out_shape=jax.ShapeDtypeStruct((tok, width + tok), grad_rows.dtype),
+        compiler_params=pltpu.CompilerParams(vmem_limit_bytes=60 << 20),
+    )(grad_rows, grad_scale[None, :], route_probs.T, expert_ids.T)
+
+
+def spread_rows(me, hidden_ref, label_refs, out_ref, table_ref, rows_ref):
+    experts, sources, capacity, units = hidden_ref.shape
+    tok = label_refs[0].shape[0]
+    slot = lax.broadcasted_iota(jnp.int32, (capacity, tok), 0).astype(jnp.float32)
+    for q in range(sources):
+        src = me ^ q
+        table_ref[...] = label_refs[q][...].astype(jnp.float32).T
+        for j in range(experts):
+            line = lambda part: table_ref[pl.ds(part * EXPERTS + me * experts + j, 1), :]
+            pos = line(0)
+            coef = line(1) + line(2) + line(3)
+            pick = jnp.where(slot == pos, 1.0, 0.0).astype(jnp.bfloat16)
+            rows = lax.dot_general(
+                hidden_ref[j, src],
+                pick,
+                (((0,), (0,)), ((), ())),
+                preferred_element_type=jnp.float32,
+            )
+            rows_ref[pl.ds(j, units, stride=experts), :] = rows * coef
+        out_ref[:, q * tok : (q + 1) * tok] = rows_ref[...].astype(out_ref.dtype)
+
+
+def spread_call(body, where, hiddens, unit_blocks, labels, n_out):
+    experts, sources, capacity = hiddens[0].shape[:3]
+    tok = labels[0].shape[0]
+    units = hiddens[0].shape[3] // unit_blocks
+    last = labels[0].shape[1] // tok - 1
+    out = jax.ShapeDtypeStruct((units * experts, sources * tok), jnp.bfloat16)
+    out_spec = pl.BlockSpec(out.shape, lambda i, w: (0, 0))
+    return pl.pallas_call(
+        body,
+        grid_spec=pltpu.PrefetchScalarGridSpec(
+            num_scalar_prefetch=1,
+            grid=(1,),
+            in_specs=[
+                pl.BlockSpec(
+                    (experts, sources, capacity, units),
+                    (lambda i, w: (0, 0, 0, w[1])) if unit_blocks > 1 else (lambda i, w: (0, 0, 0, 0)),
+                )
+                for _ in hiddens
+            ]
+            + [pl.BlockSpec((tok, tok), lambda i, w: (0, last)) for _ in labels],
+            out_specs=[out_spec] * n_out,
+            scratch_shapes=[
+                pltpu.VMEM((tok, tok), jnp.float32),
+                pltpu.VMEM((units * experts, tok), jnp.float32),
+            ],
+        ),
+        out_shape=[out] * n_out,
+        compiler_params=pltpu.CompilerParams(vmem_limit_bytes=16 << 20),
+        cost_estimate=pl.CostEstimate(
+            flops=4 * n_out * sources * tok * units * experts * capacity,
+            bytes_accessed=n_out * (hiddens[0].size * 2 + out.size * 2),
+            transcendentals=0,
+        ),
+    )(where, *hiddens, *labels)
+
+
+def spread(where, hidden, unit_blocks, labels):
+    def body(where_ref, hidden_ref, *refs):
+        *label_refs, out_ref, table_ref, rows_ref = refs
+        spread_rows(where_ref[0], hidden_ref, label_refs, out_ref, table_ref, rows_ref)
+
+    return spread_call(body, where, [hidden], unit_blocks, labels, 1)[0]
+
+
+def spread_far(where, hidden_ends, hidden_inner, labels_a, labels_b):
+    def body(where_ref, ends_a, ends_b, inner_a, inner_b, *refs):
+        *label_refs, out_a, out_b, table_ref, rows_ref = refs
+        n = len(label_refs) // 2
+
+        def both(hidden_a, hidden_b):
+            spread_rows(where_ref[0], hidden_a, label_refs[:n], out_a, table_ref, rows_ref)
+            spread_rows(where_ref[0], hidden_b, label_refs[n:], out_b, table_ref, rows_ref)
+
+        @pl.when(where_ref[2] == 1)
+        def _():
+            both(ends_a, ends_b)
+
+        @pl.when(where_ref[2] == 0)
+        def _():
+            both(inner_a, inner_b)
+
+    return spread_call(
+        body, where, [*hidden_ends, *hidden_inner], 1, [*labels_a, *labels_b], 2
+    )
+
+
+def product(spreads, rows, width, acc=None, last=False, experts=4, tile=512):
+    n_tok = rows[0].shape[0]
+    m = spreads[0].shape[0]
+    k = sum(s.shape[1] for s in spreads)
+
+    def body(*refs):
+        refs = list(refs)
+        lhs = [refs.pop(0) for _ in spreads]
+        held = [refs.pop(0) for _ in rows]
+        before = refs.pop(0) if acc is not None else None
+        out = refs.pop(0)
+        right = jnp.concatenate([r[...] for r in held], axis=0)
+        left = jnp.concatenate([r[...] for r in lhs], axis=1) if len(lhs) > 1 else lhs[0][...]
+        total = jnp.dot(left, right, preferred_element_type=jnp.float32)
+        if before is not None:
+            total = total + before[...].astype(jnp.float32)
+        if last:
+            out[...] = total.reshape(m // experts, experts, tile).astype(out.dtype)
+        else:
+            out[...] = total.astype(out.dtype)
+
+    in_specs = [
+        pl.BlockSpec(s.shape, lambda i: (0, 0), pipeline_mode=pl.Buffered(1)) for s in spreads
+    ]
+    in_specs += [pl.BlockSpec((n_tok, tile), lambda i: (0, i)) for _ in rows]
+    args = [*spreads, *rows]
+    if acc is not None:
+        in_specs.append(pl.BlockSpec((m, tile), lambda i: (0, i)))
+        args.append(acc)
+    if last:
+        out_shape = jax.ShapeDtypeStruct((m // experts, experts, width), jnp.bfloat16)
+        out_spec = pl.BlockSpec((m // experts, experts, tile), lambda i: (0, 0, i))
+    else:
+        out_shape = jax.ShapeDtypeStruct((m, width), ACC)
+        out_spec = pl.BlockSpec((m, tile), lambda i: (0, i))
+    return pl.pallas_call(
+        body,
+        grid=(width // tile,),
+        in_specs=in_specs,
+        out_specs=out_spec,
+        out_shape=out_shape,
+        compiler_params=pltpu.CompilerParams(vmem_limit_bytes=20 << 20),
+        cost_estimate=pl.CostEstimate(
+            flops=2 * m * k * width,
+            bytes_accessed=m * width * 4 + k * width * 2,
+            transcendentals=0,
+        ),
+    )(*args)
+
+
+def gathered_shards(grad_rows, grad_scale, route_probs, expert_ids, saved_hidden):
+    tok, width = grad_rows.shape
+    top_count = expert_ids.shape[1]
+    n_expert = lax.axis_size("expert")
+    n_replica = lax.axis_size("replica")
+    per_device = EXPERTS // n_expert
+    hidden = saved_hidden[0]
+    units = hidden.shape[3] // n_replica
+    scale_norm = 1.0 / math.sqrt(n_replica * n_expert * tok * top_count / EXPERTS)
+    e = lax.axis_index("expert")
+    z = lax.axis_index("replica")
+    both = ("expert", "replica")
+
+    def send(name, array, expert_to, moves):
+        pairs = [
+            (a * n_replica + i, expert_to(a) * n_replica + j)
+            for a in range(n_expert)
+            for i, j in moves
+        ]
+        with jax.named_scope(name):
+            return lax.ppermute(array, both, pairs)
+
+    stay = [(i, i) for i in range(4)]
+    near = [(0, 1), (1, 0), (2, 3), (3, 2)]
+    middle = [(1, 2), (2, 1)]
+    outward = [(1, 0), (2, 3)]
+    outer = [(0, 3), (3, 0)]
+    cross_in = [(2, 0), (1, 3)]
+    cross_out = [(0, 2), (3, 1)]
+    same = lambda a: a
+    core = lambda a: a ^ 1
+    side = lambda a: a ^ 2
+    inner = (z == 1) | (z == 2)
+
+    def units_of(replica):
+        return lax.dynamic_slice_in_dim(hidden, replica * units, units, 3)
+
+    own = labelled(grad_rows, grad_scale, route_probs, expert_ids, scale_norm)
+
+    tie = lax.optimization_barrier
+    h_near, h_cross, h_flip = (units_of(z ^ i) for i in range(1, 4))
+
+    where = jnp.stack([e, z, jnp.where(inner, 0, 1)]).astype(jnp.int32)
+
+    c_own = send("c_own", own, core, stay)
+    mid_a = send("mid_a", own, same, middle)
+    x_own = send("x_own", own, side, stay)
+    pair = send("pair", own, same, near)
+    c_own, h_near, own, where, mid_a, h_flip, x_own, h_cross, pair = tie(
+        (c_own, h_near, own, where, mid_a, h_flip, x_own, h_cross, pair)
+    )
+
+    end_a = send("end_a", mid_a, same, outward)
+    mid_b = send("mid_b", pair, same, middle)
+    x_pair = send("x_pair", pair, side, stay)
+    g_near = send("g_near", h_near, same, near)
+    g_inner = send("g_inner", h_flip, same, middle)
+    far_a = jnp.where(inner, mid_a, end_a)
+    x_pair, g_near, c_own, h_cross, x_own, pair, far_a, h_flip, g_inner, own, mid_b = tie(
+        (x_pair, g_near, c_own, h_cross, x_own, pair, far_a, h_flip, g_inner, own, mid_b)
+    )
+
+    end_b = send("end_b", mid_b, same, outward)
+    g_out = send("g_out", h_cross, same, cross_out)
+    x_far_a = send("x_far_a", far_a, side, stay)
+    c_xown = send("c_xown", x_own, core, stay)
+    c_pair = send("c_pair", pair, core, stay)
+    far_b = jnp.where(inner, mid_b, end_b)
+    x_far_a, g_out, far_b, h_flip, far_a, pair, x_pair, c_xown, x_own, own, c_own, c_pair, h_cross = tie(
+        (x_far_a, g_out, far_b, h_flip, far_a, pair, x_pair, c_xown, x_own, own, c_own, c_pair, h_cross)
+    )
+
+    g_outer = send("g_outer", h_flip, same, outer)
+    g_in = send("g_in", h_cross, same, cross_in)
+    x_far_b = send("x_far_b", far_b, side, stay)
+    c_xpair = send("c_xpair", x_pair, core, stay)
+    c_far_a = send("c_far_a", far_a, core, stay)
+    rows_own = [own, c_own, x_own, c_xown]
+    rows_near = [pair, c_pair, x_pair, c_xpair]
+    s_own = spread(where, hidden, n_replica, rows_own)
+    s_near = spread(where, g_near, 1, rows_near)
+    acc = product([s_own, s_near], rows_own + rows_near, width)
+    c_far_a, g_outer, x_far_b, acc, x_far_a, far_b, g_in = tie(
+        (c_far_a, g_outer, x_far_b, acc, x_far_a, far_b, g_in)
+    )
+
+    c_xfar_a = send("c_xfar_a", x_far_a, core, stay)
+    c_far_b = send("c_far_b", far_b, core, stay)
+    c_xfar_b = send("c_xfar_b", x_far_b, core, stay)
+    rows_a = [far_a, c_far_a, x_far_a, c_xfar_a]
+    rows_b = [far_b, c_far_b, x_far_b, c_xfar_b]
+    s_a, s_b = spread_far(where, (g_in, g_outer), (g_inner, g_out), rows_a, rows_b)
+    return product([s_a, s_b], rows_a + rows_b, width, acc, last=True, experts=per_device)
 
 
 def solution(mesh):
@@ -62,8 +332,9 @@
         P(("groups", "expert", "replica"), None),
         P(("groups", "replica"), "expert", None, None, None),
     )
+    small = mesh.shape["expert"] == 4 and mesh.shape["replica"] == 4
     return jax.shard_map(
-        shards,
+        gathered_shards if small else summed_shards,
         mesh=mesh,
         in_specs=placed,
         out_specs=P(("groups", "replica"), "expert", None),

time: 594 us -> 149 us (0.25)
  waiting for transfers between devices: 484 us -> 80.7 us
  local copies, waits for them, and re-layouts: 50.6 us -> 1.56 us
  Pallas kernels: 0 us -> 33.4 us
  starting transfers between devices: 0.04 us -> 32.2 us
  matrix products: 22.8 us -> 0 us
  blocking collectives: 16.9 us -> 0 us
  between operations: 13.5 us -> 0.17 us
    reduce_scatter x1 -> x0, waiting for transfers between devices: 483 us -> none  [shards(): lax.psum_scatter((summed * scale_norm).astype(jnp.bfloat16), 'replica', s...]
    ppermute x0 -> x22, waiting for transfers between devices: none -> 80.7 us  [send(): return lax.ppermute(array, both, pairs)]
    pallas_call x0 -> x6, Pallas kernels: none -> 33.4 us  [the longest x2 25 us: product(): pl.pallas_call(body, grid=(width // tile,), in_specs=in_specs, out_specs=...]
    ppermute x0 -> x22, starting transfers between devices: none -> 32.2 us  [send(): return lax.ppermute(array, both, pairs)]
    gather x1 -> x0, local copies, waits for them, and re-layouts: 30.2 us -> none  [shards(): jnp.take(hidden_table, row_pick, axis=0)]
    dot_general x1 -> x0, matrix products: 22.8 us -> none  [shards(): jnp.einsum('lif,lid->fld', chosen, scaled, preferred_element_type=jnp.flo...]
    all_gather x3 -> x0, blocking collectives: 16.9 us -> none  [the longest x1 6.33 us: shards(): lax.all_gather(expert_ids, 'expert', axis=0, tiled=True)]
    reduce_scatter x1 -> x0, local copies, waits for them, and re-layouts: 12.8 us -> none  [shards(): lax.psum_scatter((summed * scale_norm).astype(jnp.bfloat16), 'replica', s...]
  transfers between devices with their start and end apart: 2 -> 22, of which waited for: 1 -> 10; matrix products, arithmetic and copies ran while one was open for 6% -> 1% of each run, Pallas kernels for 0% -> 10%
where the time goes in v2:
time: 149 us; the launch traced here: 148 us
  waiting for transfers between devices  80.7 us (54%)
  Pallas kernels  33.4 us (22%)
  starting transfers between devices  32.2 us (22%)
  local copies, waits for them, and re-layouts  1.56 us (1%)
    ppermute x22, waiting for transfers between devices, send(): return lax.ppermute(array, both, pairs)  80.7 us
    ppermute x22, starting transfers between devices, send(): return lax.ppermute(array, both, pairs)  32.2 us
    pallas_call x2, Pallas kernels, product(): pl.pallas_call(body, grid=(width // tile,), in_specs=in_specs, out_specs=...  25 us
    pallas_call x3, Pallas kernels, spread_call(): pl.pallas_call(body, grid_spec=pltpu.PrefetchScalarGridSpec(num_scalar_pr...  5.86 us
  transfers between devices with their start and end apart: 22, of which 10 were waited for; matrix products, arithmetic and copies ran while one was open for 1% of the time, Pallas kernels for 10%

profile of v2, /device:TPU:0, one launch (start us, length us, event | category | flops | bytes accessed | tf_op | source)
XLA Modules:
  0.0 148.3 jit_solution(17944659071106571663)
XLA Ops:
  0.0 2.5 %shard_map.55.refs_0_.refs_2_ = bf16[128,3712]{1,0:T(8,128)(2,1)} custom-call(bf16[128,3584]{1,0:T(8,128)(2,1)} %rows_ref.1, f32[1,128]{1,0:T(1,128)} %bitcast.16, f32[8,128]{1,0:T(8,128)} %bitcast.14, s32[8,128]{1,0:T(8,128)} %bitcast.15), custom_call_target="tpu_custom_call" | custom-call | tf_op jit(solution)/shard_map/pallas_call | solution.py:87
  2.5 3.0 %collective-permute-start.3 = (bf16[128,3712]{1,0:T(8,128)(2,1)}, bf16[128,3712]{1,0:T(8,128)(2,1)}, u32[]{:S(2)}, u32[]{:S(2)}) collective-permute-start(bf16[128,3712]{1,0:T(8,128)(2,1)} %shard_map.55.refs_0_.refs_2_), channel_id=1, source_target_pairs={{0,1},{1,0},{2,3},{3,2},{4,5},{5,4},{6,7},{7,6},{8,9},{9,8},{10,11... | collective-permute-start | bytes 2850824 | tf_op jit(solution)/shard_map/pair/ppermute | solution.py:252
  5.6 1.5 %collective-permute-start.2 = (bf16[128,3712]{1,0:T(8,128)(2,1)}, bf16[128,3712]{1,0:T(8,128)(2,1)}, u32[]{:S(2)}, u32[]{:S(2)}) collective-permute-start(bf16[128,3712]{1,0:T(8,128)(2,1)} %shard_map.55.refs_0_.refs_2_), channel_id=1, source_target_pairs={{0,8},{1,9},{2,10},{3,11},{4,12},{5,13},{6,14},{7,15},{8,0},{9,1},... | collective-permute-start | bytes 2850824 | tf_op jit(solution)/shard_map/x_own/ppermute | solution.py:252
  7.0 1.6 %collective-permute-start.1 = (bf16[128,3712]{1,0:T(8,128)(2,1)}, bf16[128,3712]{1,0:T(8,128)(2,1)}, u32[]{:S(2)}, u32[]{:S(2)}) collective-permute-start(bf16[128,3712]{1,0:T(8,128)(2,1)} %shard_map.55.refs_0_.refs_2_), channel_id=1, source_target_pairs={{1,2},{2,1},{5,6},{6,5},{9,10},{10,9},{13,14},{14,13},{17,18},{18,... | collective-permute-start | bytes 2850824 | tf_op jit(solution)/shard_map/mid_a/ppermute | solution.py:252
  8.7 1.6 %dynamic-slice_bitcast_fusion = (bf16[4,4,72,256]{3,2,1,0:T(8,128)(2,1)S(1)}, bf16[4,4,72,256]{3,2,1,0:T(8,128)(2,1)S(1)}, bf16[4,4,72,256]{3,2,1,0:T(8,128)(2,1)S(1)}) fusion(bf16[1,4,4,72,1024]{4,3,2,1,0:T(8,128)(2,1)} %param.9, s32[]{:T(128)S(6)} %select_n.28, s32[]{:T(128)S(6)} %select_n.27, s32[]{:T(128)S(6)} %select_n.25), kind=kLoop, calls=%fused_computation.2 | loop fusion | bytes 3538956 | tf_op jit(solution)/shard_map/dynamic_slice | solution.py:267
  10.3 16.7 %collective-permute-done.3.refs_0_.refs_6_ = bf16[128,3712]{1,0:T(8,128)(2,1)} collective-permute-done((bf16[128,3712]{1,0:T(8,128)(2,1)}, bf16[128,3712]{1,0:T(8,128)(2,1)}, u32[]{:S(2)}, u32[]{:S(2)}) %collective-permute-start.3) | collective-permute-done | bytes 950304 | tf_op jit(solution)/shard_map/pair/ppermute | solution.py:252
  27.0 1.4 collective-permute-done.2.refs_2_.refs_4_
  28.4 1.3 collective-permute-start.6
  29.7 0.7 collective-permute-start.8
  30.4 1.6 %collective-permute-start.4 = (bf16[128,3712]{1,0:T(8,128)(2,1)}, bf16[128,3712]{1,0:T(8,128)(2,1)S(1)}, u32[]{:S(2)}, u32[]{:S(2)}) collective-permute-start(bf16[128,3712]{1,0:T(8,128)(2,1)} %collective-permute-done.3.refs_0_.refs_6_), channel_id=1, source_target_pairs={{0,8},{1,9},{2,10},{3,11},{4,12},{5,13},{6,14},{7,15},{8,0},{9,1},... | collective-permute-start | bytes 2850824 | tf_op jit(solution)/shard_map/x_pair/ppermute | solution.py:252
  32.0 6.5 %collective-permute-start.5 = (bf16[4,4,72,256]{3,2,1,0:T(8,128)(2,1)S(1)}, bf16[4,4,72,256]{3,2,1,0:T(8,128)(2,1)S(1)}, u32[]{:S(2)}, u32[]{:S(2)}) collective-permute-start(bf16[4,4,72,256]{3,2,1,0:T(8,128)(2,1)S(1)} %get-tuple-element.49), channel_id=1, source_target_pairs={{0,1},{1,0},{2,3},{3,2},{4,5},{5,4},{6,7},{7,6},{8,9},{9,8},{10,11... | collective-permute-start | bytes 1769480 | tf_op jit(solution)/shard_map/g_near/ppermute | solution.py:252
  38.5 0.7 collective-permute-start.7
  39.2 17.2 %collective-permute-done.6 = bf16[128,3712]{1,0:T(8,128)(2,1)S(1)} collective-permute-done((bf16[128,3712]{1,0:T(8,128)(2,1)}, bf16[128,3712]{1,0:T(8,128)(2,1)S(1)}, u32[]{:S(2)}, u32[]{:S(2)}) %collective-permute-start.6) | collective-permute-done | bytes 950304 | tf_op jit(solution)/shard_map/end_a/ppermute | solution.py:252
  56.5 10.4 %collective-permute-done.5.hidden_ref = bf16[4,4,72,256]{3,2,1,0:T(8,128)(2,1)S(1)} collective-permute-done((bf16[4,4,72,256]{3,2,1,0:T(8,128)(2,1)S(1)}, bf16[4,4,72,256]{3,2,1,0:T(8,128)(2,1)S(1)}, u32[]{:S(2)}, u32[]{:S(2)}) %collective-permute-start.5) | collective-permute-done | bytes 589856 | tf_op jit(solution)/shard_map/g_near/ppermute | solution.py:252
  66.9 1.3 collective-permute-start.11
  68.2 6.6 %collective-permute-start.10 = (bf16[4,4,72,256]{3,2,1,0:T(8,128)(2,1)S(1)}, bf16[4,4,72,256]{3,2,1,0:T(8,128)(2,1)S(1)}, u32[]{:S(2)}, u32[]{:S(2)}) collective-permute-start(bf16[4,4,72,256]{3,2,1,0:T(8,128)(2,1)S(1)} %get-tuple-element.77), channel_id=1, source_target_pairs={{0,2},{3,1},{4,6},{7,5},{8,10},{11,9},{12,14},{15,13},{16,18},{19,... | collective-permute-start | bytes 1769480 | tf_op jit(solution)/shard_map/g_out/ppermute | solution.py:252
  74.8 0.6 collective-permute-start.9
  75.4 0.5 collective-permute-start.12
  75.9 14.9 %collective-permute-done.11 = bf16[128,3712]{1,0:T(8,128)(2,1)S(1)} collective-permute-done((bf16[128,3712]{1,0:T(8,128)(2,1)S(1)}, bf16[128,3712]{1,0:T(8,128)(2,1)S(1)}, u32[]{:S(2)}, u32[]{:S(2)}) %collective-permute-start.11) | collective-permute-done | bytes 950304 | tf_op jit(solution)/shard_map/end_b/ppermute | solution.py:252
  90.9 4.0 %collective-permute-done.9.refs_2_.refs_4_ = bf16[128,3712]{1,0:T(8,128)(2,1)S(1)} collective-permute-done((bf16[128,3712]{1,0:T(8,128)(2,1)S(1)}, bf16[128,3712]{1,0:T(8,128)(2,1)S(1)}, u32[]{:S(2)}, u32[]{:S(2)}) %collective-permute-start.9) | collective-permute-done | bytes 950304 | tf_op jit(solution)/shard_map/x_far_a/ppermute | solution.py:252
  95.0 0.6 collective-permute-start.16
  95.7 3.7 %collective-permute-start.15 = (bf16[4,4,72,256]{3,2,1,0:T(8,128)(2,1)S(1)}, bf16[4,4,72,256]{3,2,1,0:T(8,128)(2,1)S(1)}, u32[]{:S(2)}, u32[]{:S(2)}) collective-permute-start(bf16[4,4,72,256]{3,2,1,0:T(8,128)(2,1)S(1)} %get-tuple-element.66), channel_id=1, source_target_pairs={{0,3},{3,0},{4,7},{7,4},{8,11},{11,8},{12,15},{15,12},{16,19},{19,... | collective-permute-start | bytes 1769480 | tf_op jit(solution)/shard_map/g_outer/ppermute | solution.py:252
  99.4 1.3 collective-permute-start.18
  100.7 2.1 %shard_map.56.refs_0_ = bf16[1024,512]{1,0:T(8,128)(2,1)S(1)} custom-call(s32[3]{0:T(128)S(1)} %pad_add_fusion.where_ref, bf16[4,4,72,1024]{3,2,1,0:T(8,128)(2,1)S(1)} %bitcast.13, bf16[128,3712]{1,0:T(8,128)(2,1)S(1)} %copy-done.1, bf16[128,3712]{1,0:T(8,128)(2,1)} %collective-permute-done.refs_1_.refs_3_, ...), custom_call_target="tpu_custom_call" | custom-call | flops 150994944 | bytes 3407872 | tf_op jit(solution)/shard_map/pallas_call | solution.py:123
  102.8 2.0 %shard_map.57.refs_1_ = bf16[1024,512]{1,0:T(8,128)(2,1)S(1)} custom-call(s32[3]{0:T(128)S(1)} %pad_add_fusion.where_ref, bf16[4,4,72,256]{3,2,1,0:T(8,128)(2,1)S(1)} %collective-permute-done.5.hidden_ref, bf16[128,3712]{1,0:T(8,128)(2,1)} %collective-permute-done.3.refs_0_.refs_6_, bf16[128,3712]{1,0:T(8,128)(2,1)S(1)} %collective-permute-done.13.refs_1_.refs_7_, ...), custom_call_target="tpu_custom_call" | custom-call | flops 150994944 | bytes 1638400 | tf_op jit(solution)/shard_map/pallas_call | solution.py:123
  104.8 11.4 %shard_map.58.refs_10_ = bf16[1024,3584]{1,0:T(8,128)(2,1)S(1)} custom-call(bf16[1024,512]{1,0:T(8,128)(2,1)S(1)} %shard_map.56.refs_0_, bf16[1024,512]{1,0:T(8,128)(2,1)S(1)} %shard_map.57.refs_1_, bf16[128,3712]{1,0:T(8,128)(2,1)S(1)} %copy-done.1, bf16[128,3712]{1,0:T(8,128)(2,1)} %collective-permute-done.refs_1_.refs_3_, ...), custom_call_target="tpu_custom_call" | custom-call | flops 7516192768 | bytes 22020096 | tf_op jit(solution)/shard_map/pallas_call | solution.py:217
  116.2 11.4 %collective-permute-done.18.ends_a = bf16[4,4,72,256]{3,2,1,0:T(8,128)(2,1)S(1)} collective-permute-done((bf16[4,4,72,256]{3,2,1,0:T(8,128)(2,1)S(1)}, bf16[4,4,72,256]{3,2,1,0:T(8,128)(2,1)S(1)}, u32[]{:S(2)}, u32[]{:S(2)}) %collective-permute-start.18) | collective-permute-done | bytes 589856 | tf_op jit(solution)/shard_map/g_in/ppermute | solution.py:252
  128.2 1.9 %collective-permute-done.19.refs_3_.refs_5_ = bf16[128,3712]{1,0:T(8,128)(2,1)S(1)} collective-permute-done((bf16[128,3712]{1,0:T(8,128)(2,1)S(1)}, bf16[128,3712]{1,0:T(8,128)(2,1)S(1)}, u32[]{:S(2)}, u32[]{:S(2)}) %collective-permute-start.19) | collective-permute-done | bytes 950304 | tf_op jit(solution)/shard_map/c_xfar_a/ppermute | solution.py:252
  130.1 1.4 collective-permute-done.20.refs_5_.refs_7_
  131.5 1.4 collective-permute-done.21.refs_7_.refs_9_
  132.9 1.8 %shard_map.59 = (bf16[1024,512]{1,0:T(8,128)(2,1)S(1)}, bf16[1024,512]{1,0:T(8,128)(2,1)S(1)}) custom-call(s32[3]{0:T(128)S(1)} %pad_add_fusion.where_ref, bf16[4,4,72,256]{3,2,1,0:T(8,128)(2,1)S(1)} %collective-permute-done.18.ends_a, bf16[4,4,72,256]{3,2,1,0:T(8,128)(2,1)S(1)} %collective-permute-done.15.ends_b, ...), custom_call_target="tpu_custom_call" | custom-call | flops 301989888 | bytes 3276800 | tf_op jit(solution)/shard_map/pallas_call | solution.py:123
  134.7 13.7 %shard_map.60 = bf16[256,4,3584]{2,1,0:T(4,128)(2,1)} custom-call(bf16[1024,512]{1,0:T(8,128)(2,1)S(1)} %get-tuple-element.86.refs_0_, bf16[1024,512]{1,0:T(8,128)(2,1)S(1)} %get-tuple-element.87.refs_1_, bf16[128,3712]{1,0:T(8,128)(2,1)S(1)} %broadcast_select_fusion.1.refs_0_.refs_2_, bf16[128,3712]{1,0:T(8,128)(2,1)S(1)} %collective-permute-done.14.refs_1_.refs_3_, ...), custom_call_target="tpu_custom_call" | custom-call | flops 7516192768 | bytes 22020096 | tf_op jit(solution)/shard_map/pallas_call | solution.py:217
  (26 shorter events, 1.1 us)
Async XLA Ops:
  0.0 100.7 %copy-start = (bf16[1,4,4,72,1024]{4,3,2,1,0:T(8,128)(2,1)S(1)}, bf16[1,4,4,72,1024]{4,3,2,1,0:T(8,128)(2,1)}, u32[]{:S(2)}) copy-start(bf16[1,4,4,72,1024]{4,3,2,1,0:T(8,128)(2,1)} %param.9) | copy-start | bytes 7077892
  2.5 98.2 %copy-start.1 = (bf16[128,3712]{1,0:T(8,128)(2,1)S(1)}, bf16[128,3712]{1,0:T(8,128)(2,1)}, u32[]{:S(2)}) copy-start(bf16[128,3712]{1,0:T(8,128)(2,1)} %shard_map.55.refs_0_.refs_2_) | copy-start | bytes 2850820
  2.5 24.5 %collective-permute-start.3 = (bf16[128,3712]{1,0:T(8,128)(2,1)}, bf16[128,3712]{1,0:T(8,128)(2,1)}, u32[]{:S(2)}, u32[]{:S(2)}) collective-permute-start(bf16[128,3712]{1,0:T(8,128)(2,1)} %shard_map.55.refs_0_.refs_2_), channel_id=1, source_target_pairs={{0,1},{1,0},{2,3},{3,2},{4,5},{5,4},{6,7},{7,6},{8,9},{9,8},{10,11... | collective-permute-start | bytes 2850824 | tf_op jit(solution)/shard_map/pair/ppermute | solution.py:252
  5.6 22.8 %collective-permute-start.2 = (bf16[128,3712]{1,0:T(8,128)(2,1)}, bf16[128,3712]{1,0:T(8,128)(2,1)}, u32[]{:S(2)}, u32[]{:S(2)}) collective-permute-start(bf16[128,3712]{1,0:T(8,128)(2,1)} %shard_map.55.refs_0_.refs_2_), channel_id=1, source_target_pairs={{0,8},{1,9},{2,10},{3,11},{4,12},{5,13},{6,14},{7,15},{8,0},{9,1},... | collective-permute-start | bytes 2850824 | tf_op jit(solution)/shard_map/x_own/ppermute | solution.py:252
  7.0 21.3 %collective-permute-start.1 = (bf16[128,3712]{1,0:T(8,128)(2,1)}, bf16[128,3712]{1,0:T(8,128)(2,1)}, u32[]{:S(2)}, u32[]{:S(2)}) collective-permute-start(bf16[128,3712]{1,0:T(8,128)(2,1)} %shard_map.55.refs_0_.refs_2_), channel_id=1, source_target_pairs={{1,2},{2,1},{5,6},{6,5},{9,10},{10,9},{13,14},{14,13},{17,18},{18,... | collective-permute-start | bytes 2850824 | tf_op jit(solution)/shard_map/mid_a/ppermute | solution.py:252
  8.7 19.7 %collective-permute-start = (bf16[128,3712]{1,0:T(8,128)(2,1)}, bf16[128,3712]{1,0:T(8,128)(2,1)}, u32[]{:S(2)}, u32[]{:S(2)}) collective-permute-start(bf16[128,3712]{1,0:T(8,128)(2,1)} %shard_map.55.refs_0_.refs_2_), channel_id=1, source_target_pairs={{0,4},{1,5},{2,6},{3,7},{4,0},{5,1},{6,2},{7,3},{8,12},{9,13},{10,... | collective-permute-start | bytes 2850824 | tf_op jit(solution)/shard_map/c_own/ppermute | solution.py:252
  28.4 28.0 %collective-permute-start.6 = (bf16[128,3712]{1,0:T(8,128)(2,1)}, bf16[128,3712]{1,0:T(8,128)(2,1)S(1)}, u32[]{:S(2)}, u32[]{:S(2)}) collective-permute-start(bf16[128,3712]{1,0:T(8,128)(2,1)} %collective-permute-done.1), channel_id=1, source_target_pairs={{1,0},{2,3},{5,4},{6,7},{9,8},{10,11},{13,12},{14,15},{17,16},{18,... | collective-permute-start | bytes 2850824 | tf_op jit(solution)/shard_map/end_a/ppermute | solution.py:252
  29.7 37.2 %collective-permute-start.8 = (bf16[128,3712]{1,0:T(8,128)(2,1)}, bf16[128,3712]{1,0:T(8,128)(2,1)S(1)}, u32[]{:S(2)}, u32[]{:S(2)}) collective-permute-start(bf16[128,3712]{1,0:T(8,128)(2,1)} %collective-permute-done.3.refs_0_.refs_6_), channel_id=1, source_target_pairs={{1,2},{2,1},{5,6},{6,5},{9,10},{10,9},{13,14},{14,13},{17,18},{18,... | collective-permute-start | bytes 2850824 | tf_op jit(solution)/shard_map/mid_b/ppermute | solution.py:252
  30.4 36.5 %collective-permute-start.4 = (bf16[128,3712]{1,0:T(8,128)(2,1)}, bf16[128,3712]{1,0:T(8,128)(2,1)S(1)}, u32[]{:S(2)}, u32[]{:S(2)}) collective-permute-start(bf16[128,3712]{1,0:T(8,128)(2,1)} %collective-permute-done.3.refs_0_.refs_6_), channel_id=1, source_target_pairs={{0,8},{1,9},{2,10},{3,11},{4,12},{5,13},{6,14},{7,15},{8,0},{9,1},... | collective-permute-start | bytes 2850824 | tf_op jit(solution)/shard_map/x_pair/ppermute | solution.py:252
  32.0 34.9 %collective-permute-start.5 = (bf16[4,4,72,256]{3,2,1,0:T(8,128)(2,1)S(1)}, bf16[4,4,72,256]{3,2,1,0:T(8,128)(2,1)S(1)}, u32[]{:S(2)}, u32[]{:S(2)}) collective-permute-start(bf16[4,4,72,256]{3,2,1,0:T(8,128)(2,1)S(1)} %get-tuple-element.49), channel_id=1, source_target_pairs={{0,1},{1,0},{2,3},{3,2},{4,5},{5,4},{6,7},{7,6},{8,9},{9,8},{10,11... | collective-permute-start | bytes 1769480 | tf_op jit(solution)/shard_map/g_near/ppermute | solution.py:252
  38.5 28.4 %collective-permute-start.7 = (bf16[4,4,72,256]{3,2,1,0:T(8,128)(2,1)S(1)}, bf16[4,4,72,256]{3,2,1,0:T(8,128)(2,1)S(1)}, u32[]{:S(2)}, u32[]{:S(2)}) collective-permute-start(bf16[4,4,72,256]{3,2,1,0:T(8,128)(2,1)S(1)} %get-tuple-element.66), channel_id=1, source_target_pairs={{1,2},{2,1},{5,6},{6,5},{9,10},{10,9},{13,14},{14,13},{17,18},{18,... | collective-permute-start | bytes 1769480 | tf_op jit(solution)/shard_map/g_inner/ppermute | solution.py:252
  66.9 23.9 %collective-permute-start.11 = (bf16[128,3712]{1,0:T(8,128)(2,1)S(1)}, bf16[128,3712]{1,0:T(8,128)(2,1)S(1)}, u32[]{:S(2)}, u32[]{:S(2)}) collective-permute-start(bf16[128,3712]{1,0:T(8,128)(2,1)S(1)} %collective-permute-done.8), channel_id=1, source_target_pairs={{1,0},{2,3},{5,4},{6,7},{9,8},{10,11},{13,12},{14,15},{17,16},{18,... | collective-permute-start | bytes 2850824 | tf_op jit(solution)/shard_map/end_b/ppermute | solution.py:252
  68.2 22.7 %collective-permute-start.10 = (bf16[4,4,72,256]{3,2,1,0:T(8,128)(2,1)S(1)}, bf16[4,4,72,256]{3,2,1,0:T(8,128)(2,1)S(1)}, u32[]{:S(2)}, u32[]{:S(2)}) collective-permute-start(bf16[4,4,72,256]{3,2,1,0:T(8,128)(2,1)S(1)} %get-tuple-element.77), channel_id=1, source_target_pairs={{0,2},{3,1},{4,6},{7,5},{8,10},{11,9},{12,14},{15,13},{16,18},{19,... | collective-permute-start | bytes 1769480 | tf_op jit(solution)/shard_map/g_out/ppermute | solution.py:252
  74.8 20.2 %collective-permute-start.9 = (bf16[128,3712]{1,0:T(8,128)(2,1)S(1)}, bf16[128,3712]{1,0:T(8,128)(2,1)S(1)}, u32[]{:S(2)}, u32[]{:S(2)}) collective-permute-start(bf16[128,3712]{1,0:T(8,128)(2,1)S(1)} %broadcast_select_fusion.1.refs_0_.refs_2_), channel_id=1, source_target_pairs={{0,8},{1,9},{2,10},{3,11},{4,12},{5,13},{6,14},{7,15},{8,0},{9,1},... | collective-permute-start | bytes 2850824 | tf_op jit(solution)/shard_map/x_far_a/ppermute | solution.py:252
  75.4 19.6 %collective-permute-start.13 = (bf16[128,3712]{1,0:T(8,128)(2,1)}, bf16[128,3712]{1,0:T(8,128)(2,1)S(1)}, u32[]{:S(2)}, u32[]{:S(2)}) collective-permute-start(bf16[128,3712]{1,0:T(8,128)(2,1)} %collective-permute-done.3.refs_0_.refs_6_), channel_id=1, source_target_pairs={{0,4},{1,5},{2,6},{3,7},{4,0},{5,1},{6,2},{7,3},{8,12},{9,13},{10,... | collective-permute-start | bytes 2850824 | tf_op jit(solution)/shard_map/c_pair/ppermute | solution.py:252
  75.4 19.6 %collective-permute-start.12 = (bf16[128,3712]{1,0:T(8,128)(2,1)}, bf16[128,3712]{1,0:T(8,128)(2,1)S(1)}, u32[]{:S(2)}, u32[]{:S(2)}) collective-permute-start(bf16[128,3712]{1,0:T(8,128)(2,1)} %collective-permute-done.2.refs_2_.refs_4_), channel_id=1, source_target_pairs={{0,4},{1,5},{2,6},{3,7},{4,0},{5,1},{6,2},{7,3},{8,12},{9,13},{10,... | collective-permute-start | bytes 2850824 | tf_op jit(solution)/shard_map/c_xown/ppermute | solution.py:252
  94.9 7.9 %collective-permute-start.17 = (bf16[128,3712]{1,0:T(8,128)(2,1)S(1)}, bf16[128,3712]{1,0:T(8,128)(2,1)S(1)}, u32[]{:S(2)}, u32[]{:S(2)}) collective-permute-start(bf16[128,3712]{1,0:T(8,128)(2,1)S(1)} %collective-permute-done.4.refs_2_.refs_8_), channel_id=1, source_target_pairs={{0,4},{1,5},{2,6},{3,7},{4,0},{5,1},{6,2},{7,3},{8,12},{9,13},{10,... | collective-permute-start | bytes 2850824 | tf_op jit(solution)/shard_map/c_xpair/ppermute | solution.py:252
  95.0 32.7 %collective-permute-start.16 = (bf16[128,3712]{1,0:T(8,128)(2,1)S(1)}, bf16[128,3712]{1,0:T(8,128)(2,1)S(1)}, u32[]{:S(2)}, u32[]{:S(2)}) collective-permute-start(bf16[128,3712]{1,0:T(8,128)(2,1)S(1)} %broadcast_select_fusion.refs_4_.refs_6_), channel_id=1, source_target_pairs={{0,8},{1,9},{2,10},{3,11},{4,12},{5,13},{6,14},{7,15},{8,0},{9,1},... | collective-permute-start | bytes 2850824 | tf_op jit(solution)/shard_map/x_far_b/ppermute | solution.py:252
  95.6 32.1 %collective-permute-start.14 = (bf16[128,3712]{1,0:T(8,128)(2,1)S(1)}, bf16[128,3712]{1,0:T(8,128)(2,1)S(1)}, u32[]{:S(2)}, u32[]{:S(2)}) collective-permute-start(bf16[128,3712]{1,0:T(8,128)(2,1)S(1)} %broadcast_select_fusion.1.refs_0_.refs_2_), channel_id=1, source_target_pairs={{0,4},{1,5},{2,6},{3,7},{4,0},{5,1},{6,2},{7,3},{8,12},{9,13},{10,... | collective-permute-start | bytes 2850824 | tf_op jit(solution)/shard_map/c_far_a/ppermute | solution.py:252
  95.7 20.5 %collective-permute-start.15 = (bf16[4,4,72,256]{3,2,1,0:T(8,128)(2,1)S(1)}, bf16[4,4,72,256]{3,2,1,0:T(8,128)(2,1)S(1)}, u32[]{:S(2)}, u32[]{:S(2)}) collective-permute-start(bf16[4,4,72,256]{3,2,1,0:T(8,128)(2,1)S(1)} %get-tuple-element.66), channel_id=1, source_target_pairs={{0,3},{3,0},{4,7},{7,4},{8,11},{11,8},{12,15},{15,12},{16,19},{19,... | collective-permute-start | bytes 1769480 | tf_op jit(solution)/shard_map/g_outer/ppermute | solution.py:252
  99.4 28.2 %collective-permute-start.18 = (bf16[4,4,72,256]{3,2,1,0:T(8,128)(2,1)S(1)}, bf16[4,4,72,256]{3,2,1,0:T(8,128)(2,1)S(1)}, u32[]{:S(2)}, u32[]{:S(2)}) collective-permute-start(bf16[4,4,72,256]{3,2,1,0:T(8,128)(2,1)S(1)} %get-tuple-element.77), channel_id=1, source_target_pairs={{2,0},{1,3},{6,4},{5,7},{10,8},{9,11},{14,12},{13,15},{18,16},{17,... | collective-permute-start | bytes 1769480 | tf_op jit(solution)/shard_map/g_in/ppermute | solution.py:252
  127.6 2.5 %collective-permute-start.19 = (bf16[128,3712]{1,0:T(8,128)(2,1)S(1)}, bf16[128,3712]{1,0:T(8,128)(2,1)S(1)}, u32[]{:S(2)}, u32[]{:S(2)}) collective-permute-start(bf16[128,3712]{1,0:T(8,128)(2,1)S(1)} %collective-permute-done.9.refs_2_.refs_4_), channel_id=1, source_target_pairs={{0,4},{1,5},{2,6},{3,7},{4,0},{5,1},{6,2},{7,3},{8,12},{9,13},{10,... | collective-permute-start | bytes 2850824 | tf_op jit(solution)/shard_map/c_xfar_a/ppermute | solution.py:252
  127.7 3.9 %collective-permute-start.20 = (bf16[128,3712]{1,0:T(8,128)(2,1)S(1)}, bf16[128,3712]{1,0:T(8,128)(2,1)S(1)}, u32[]{:S(2)}, u32[]{:S(2)}) collective-permute-start(bf16[128,3712]{1,0:T(8,128)(2,1)S(1)} %broadcast_select_fusion.refs_4_.refs_6_), channel_id=1, source_target_pairs={{0,4},{1,5},{2,6},{3,7},{4,0},{5,1},{6,2},{7,3},{8,12},{9,13},{10,... | collective-permute-start | bytes 2850824 | tf_op jit(solution)/shard_map/c_far_b/ppermute | solution.py:252
  128.1 4.7 %collective-permute-start.21 = (bf16[128,3712]{1,0:T(8,128)(2,1)S(1)}, bf16[128,3712]{1,0:T(8,128)(2,1)S(1)}, u32[]{:S(2)}, u32[]{:S(2)}) collective-permute-start(bf16[128,3712]{1,0:T(8,128)(2,1)S(1)} %collective-permute-done.16.refs_6_.refs_8_), channel_id=1, source_target_pairs={{0,4},{1,5},{2,6},{3,7},{4,0},{5,1},{6,2},{7,3},{8,12},{9,13},{10,... | collective-permute-start | bytes 2850824 | tf_op jit(solution)/shard_map/c_xfar_b/ppermute | solution.py:252

commit v3 on v2

--- a/solution.py
+++ b/solution.py
@@ -113,11 +113,15 @@
         out_ref[:, q * tok : (q + 1) * tok] = rows_ref[...].astype(out_ref.dtype)
 
 
+def last_block(label, tok):
+    last = label.shape[1] // tok - 1
+    return pl.BlockSpec((tok, tok), lambda i, w: (0, last))
+
+
 def spread_call(body, where, hiddens, unit_blocks, labels, n_out):
     experts, sources, capacity = hiddens[0].shape[:3]
     tok = labels[0].shape[0]
     units = hiddens[0].shape[3] // unit_blocks
-    last = labels[0].shape[1] // tok - 1
     out = jax.ShapeDtypeStruct((units * experts, sources * tok), jnp.bfloat16)
     out_spec = pl.BlockSpec(out.shape, lambda i, w: (0, 0))
     return pl.pallas_call(
@@ -132,7 +136,7 @@
                 )
                 for _ in hiddens
             ]
-            + [pl.BlockSpec((tok, tok), lambda i, w: (0, last)) for _ in labels],
+            + [last_block(label, tok) for label in labels],
             out_specs=[out_spec] * n_out,
             scratch_shapes=[
                 pltpu.VMEM((tok, tok), jnp.float32),
@@ -157,26 +161,19 @@
     return spread_call(body, where, [hidden], unit_blocks, labels, 1)[0]
 
 
-def spread_far(where, hidden_ends, hidden_inner, labels_a, labels_b):
-    def body(where_ref, ends_a, ends_b, inner_a, inner_b, *refs):
-        *label_refs, out_a, out_b, table_ref, rows_ref = refs
-        n = len(label_refs) // 2
-
-        def both(hidden_a, hidden_b):
-            spread_rows(where_ref[0], hidden_a, label_refs[:n], out_a, table_ref, rows_ref)
-            spread_rows(where_ref[0], hidden_b, label_refs[n:], out_b, table_ref, rows_ref)
+def spread_far(where, hidden_ends, hidden_inner, labels):
+    def body(where_ref, ends_ref, inner_ref, *refs):
+        *label_refs, out_ref, table_ref, rows_ref = refs
 
         @pl.when(where_ref[2] == 1)
         def _():
-            both(ends_a, ends_b)
+            spread_rows(where_ref[0], ends_ref, label_refs, out_ref, table_ref, rows_ref)
 
         @pl.when(where_ref[2] == 0)
         def _():
-            both(inner_a, inner_b)
-
-    return spread_call(
-        body, where, [*hidden_ends, *hidden_inner], 1, [*labels_a, *labels_b], 2
-    )
+            spread_rows(where_ref[0], inner_ref, label_refs, out_ref, table_ref, rows_ref)
+
+    return spread_call(body, where, [hidden_ends, hidden_inner], 1, labels, 1)[0]
 
 
 def product(spreads, rows, width, acc=None, last=False, experts=4, tile=512):
@@ -270,15 +267,14 @@
 
     tie = lax.optimization_barrier
     h_near, h_cross, h_flip = (units_of(z ^ i) for i in range(1, 4))
-
     where = jnp.stack([e, z, jnp.where(inner, 0, 1)]).astype(jnp.int32)
 
     c_own = send("c_own", own, core, stay)
     mid_a = send("mid_a", own, same, middle)
     x_own = send("x_own", own, side, stay)
     pair = send("pair", own, same, near)
-    c_own, h_near, own, where, mid_a, h_flip, x_own, h_cross, pair = tie(
-        (c_own, h_near, own, where, mid_a, h_flip, x_own, h_cross, pair)
+    c_own, own, h_flip, h_near, mid_a, h_cross, pair, x_own, where = tie(
+        (c_own, own, h_flip, h_near, mid_a, h_cross, pair, x_own, where)
     )
 
     end_a = send("end_a", mid_a, same, outward)
@@ -286,41 +282,43 @@
     x_pair = send("x_pair", pair, side, stay)
     g_near = send("g_near", h_near, same, near)
     g_inner = send("g_inner", h_flip, same, middle)
+    c_xown = send("c_xown", x_own, core, stay)
     far_a = jnp.where(inner, mid_a, end_a)
-    x_pair, g_near, c_own, h_cross, x_own, pair, far_a, h_flip, g_inner, own, mid_b = tie(
-        (x_pair, g_near, c_own, h_cross, x_own, pair, far_a, h_flip, g_inner, own, mid_b)
+    c_own, x_pair, pair, own, g_inner, mid_b, far_a, h_flip, c_xown, h_cross, x_own, g_near = tie(
+        (c_own, x_pair, pair, own, g_inner, mid_b, far_a, h_flip, c_xown, h_cross, x_own, g_near)
     )
 
     end_b = send("end_b", mid_b, same, outward)
     g_out = send("g_out", h_cross, same, cross_out)
     x_far_a = send("x_far_a", far_a, side, stay)
-    c_xown = send("c_xown", x_own, core, stay)
+    c_xpair = send("c_xpair", x_pair, core, stay)
     c_pair = send("c_pair", pair, core, stay)
+    l_xfar_a = x_far_a[:, width:]
+    s_own = spread(where, hidden, n_replica, [own, c_own, x_own, c_xown])
     far_b = jnp.where(inner, mid_b, end_b)
-    x_far_a, g_out, far_b, h_flip, far_a, pair, x_pair, c_xown, x_own, own, c_own, c_pair, h_cross = tie(
-        (x_far_a, g_out, far_b, h_flip, far_a, pair, x_pair, c_xown, x_own, own, c_own, c_pair, h_cross)
+    c_xpair, c_pair, h_cross, h_flip, pair, x_far_a, s_own, c_xown, far_b, c_own, far_a, x_own, l_xfar_a, g_out, own, x_pair = tie(
+        (c_xpair, c_pair, h_cross, h_flip, pair, x_far_a, s_own, c_xown, far_b, c_own, far_a, x_own, l_xfar_a, g_out, own, x_pair)
     )
 
     g_outer = send("g_outer", h_flip, same, outer)
     g_in = send("g_in", h_cross, same, cross_in)
     x_far_b = send("x_far_b", far_b, side, stay)
-    c_xpair = send("c_xpair", x_pair, core, stay)
     c_far_a = send("c_far_a", far_a, core, stay)
+    c_xfar_a = send("c_xfar_a", x_far_a, core, stay)
     rows_own = [own, c_own, x_own, c_xown]
     rows_near = [pair, c_pair, x_pair, c_xpair]
-    s_own = spread(where, hidden, n_replica, rows_own)
     s_near = spread(where, g_near, 1, rows_near)
     acc = product([s_own, s_near], rows_own + rows_near, width)
-    c_far_a, g_outer, x_far_b, acc, x_far_a, far_b, g_in = tie(
-        (c_far_a, g_outer, x_far_b, acc, x_far_a, far_b, g_in)
-    )
-
-    c_xfar_a = send("c_xfar_a", x_far_a, core, stay)
     c_far_b = send("c_far_b", far_b, core, stay)
+    s_a = spread_far(where, g_in, g_inner, [far_a, c_far_a, l_xfar_a, c_xfar_a])
+    far_b, s_a, g_outer, x_far_b, acc, c_xfar_a, c_far_a, c_far_b = tie(
+        (far_b, s_a, g_outer, x_far_b, acc, c_xfar_a, c_far_a, c_far_b)
+    )
+
     c_xfar_b = send("c_xfar_b", x_far_b, core, stay)
     rows_a = [far_a, c_far_a, x_far_a, c_xfar_a]
     rows_b = [far_b, c_far_b, x_far_b, c_xfar_b]
-    s_a, s_b = spread_far(where, (g_in, g_outer), (g_inner, g_out), rows_a, rows_b)
+    s_b = spread_far(where, g_outer, g_out, rows_b)
     return product([s_a, s_b], rows_a + rows_b, width, acc, last=True, experts=per_device)
 
 

time: 149 us -> 141 us (0.946)
  waiting for transfers between devices: 80.7 us -> 69.3 us
    ppermute x22, waiting for transfers between devices: 80.7 us -> 69.3 us  [send(): return lax.ppermute(array, both, pairs)]
    pallas_call x3 -> x4, Pallas kernels: 5.86 us -> 6.62 us  [spread_call(): pl.pallas_call(body, grid_spec=pltpu.PrefetchScalarGridSpec(num_scalar_pr...]
  transfers between devices with their start and end apart: 22 -> 22, of which waited for: 10 -> 8; matrix products, arithmetic and copies ran while one was open for 1% -> 1% of each run, Pallas kernels for 10% -> 12%
where the time goes in v3:
time: 141 us; the launch traced here: 140 us
  waiting for transfers between devices  69.3 us (49%)
  Pallas kernels  34.3 us (24%)
  starting transfers between devices  33.2 us (24%)
  local copies, waits for them, and re-layouts  2.76 us (2%)
    ppermute x22, waiting for transfers between devices, send(): return lax.ppermute(array, both, pairs)  69.3 us
    ppermute x22, starting transfers between devices, send(): return lax.ppermute(array, both, pairs)  33.2 us
    pallas_call x2, Pallas kernels, product(): pl.pallas_call(body, grid=(width // tile,), in_specs=in_specs, out_specs=...  25.1 us
    pallas_call x4, Pallas kernels, spread_call(): pl.pallas_call(body, grid_spec=pltpu.PrefetchScalarGridSpec(num_scalar_pr...  6.62 us
  transfers between devices with their start and end apart: 22, of which 8 were waited for; matrix products, arithmetic and copies ran while one was open for 1% of the time, Pallas kernels for 12%

profile of v3, /device:TPU:0, one launch (start us, length us, event | category | flops | bytes accessed | tf_op | source)
XLA Modules:
  0.0 140.2 jit_solution(15941498590383179269)
XLA Ops:
  0.0 2.5 %shard_map.55.refs_0_.refs_2_ = bf16[128,3712]{1,0:T(8,128)(2,1)} custom-call(bf16[128,3584]{1,0:T(8,128)(2,1)} %rows_ref.1, f32[1,128]{1,0:T(1,128)} %bitcast.16, f32[8,128]{1,0:T(8,128)} %bitcast.14, s32[8,128]{1,0:T(8,128)} %bitcast.15), custom_call_target="tpu_custom_call" | custom-call | tf_op jit(solution)/shard_map/pallas_call | solution.py:87
  2.5 2.9 %collective-permute-start.3 = (bf16[128,3712]{1,0:T(8,128)(2,1)}, bf16[128,3712]{1,0:T(8,128)(2,1)S(1)}, u32[]{:S(2)}, u32[]{:S(2)}) collective-permute-start(bf16[128,3712]{1,0:T(8,128)(2,1)} %shard_map.55.refs_0_.refs_2_), channel_id=1, source_target_pairs={{0,8},{1,9},{2,10},{3,11},{4,12},{5,13},{6,14},{7,15},{8,0},{9,1},... | collective-permute-start | bytes 2850824 | tf_op jit(solution)/shard_map/x_own/ppermute | solution.py:249
  5.5 1.6 %collective-permute-start.2 = (bf16[128,3712]{1,0:T(8,128)(2,1)}, bf16[128,3712]{1,0:T(8,128)(2,1)}, u32[]{:S(2)}, u32[]{:S(2)}) collective-permute-start(bf16[128,3712]{1,0:T(8,128)(2,1)} %shard_map.55.refs_0_.refs_2_), channel_id=1, source_target_pairs={{0,1},{1,0},{2,3},{3,2},{4,5},{5,4},{6,7},{7,6},{8,9},{9,8},{10,11... | collective-permute-start | bytes 2850824 | tf_op jit(solution)/shard_map/pair/ppermute | solution.py:249
  7.0 1.6 %collective-permute-start.1 = (bf16[128,3712]{1,0:T(8,128)(2,1)}, bf16[128,3712]{1,0:T(8,128)(2,1)}, u32[]{:S(2)}, u32[]{:S(2)}) collective-permute-start(bf16[128,3712]{1,0:T(8,128)(2,1)} %shard_map.55.refs_0_.refs_2_), channel_id=1, source_target_pairs={{1,2},{2,1},{5,6},{6,5},{9,10},{10,9},{13,14},{14,13},{17,18},{18,... | collective-permute-start | bytes 2850824 | tf_op jit(solution)/shard_map/mid_a/ppermute | solution.py:249
  8.7 1.6 %dynamic-slice_bitcast_fusion = (bf16[4,4,72,256]{3,2,1,0:T(8,128)(2,1)S(1)}, bf16[4,4,72,256]{3,2,1,0:T(8,128)(2,1)S(1)}, bf16[4,4,72,256]{3,2,1,0:T(8,128)(2,1)S(1)}) fusion(bf16[1,4,4,72,1024]{4,3,2,1,0:T(8,128)(2,1)} %param.9, s32[]{:T(128)S(6)} %select_n.27, s32[]{:T(128)S(6)} %select_n.26, s32[]{:T(128)S(6)} %select_n.25), kind=kLoop, calls=%fused_computation.2 | loop fusion | bytes 3538956 | tf_op jit(solution)/shard_map/dynamic_slice | solution.py:264
  10.3 16.4 %collective-permute-done.3.refs_2_.refs_4_ = bf16[128,3712]{1,0:T(8,128)(2,1)S(1)} collective-permute-done((bf16[128,3712]{1,0:T(8,128)(2,1)}, bf16[128,3712]{1,0:T(8,128)(2,1)S(1)}, u32[]{:S(2)}, u32[]{:S(2)}) %collective-permute-start.3) | collective-permute-done | bytes 950304 | tf_op jit(solution)/shard_map/x_own/ppermute | solution.py:249
  26.7 1.6 %collective-permute-done.2.refs_0_.refs_6_ = bf16[128,3712]{1,0:T(8,128)(2,1)} collective-permute-done((bf16[128,3712]{1,0:T(8,128)(2,1)}, bf16[128,3712]{1,0:T(8,128)(2,1)}, u32[]{:S(2)}, u32[]{:S(2)}) %collective-permute-start.2) | collective-permute-done | bytes 950304 | tf_op jit(solution)/shard_map/pair/ppermute | solution.py:249
  28.3 1.3 collective-permute-start.7
  29.6 0.7 collective-permute-start.6
  30.8 7.7 %collective-permute-start.9 = (bf16[4,4,72,256]{3,2,1,0:T(8,128)(2,1)S(1)}, bf16[4,4,72,256]{3,2,1,0:T(8,128)(2,1)S(1)}, u32[]{:S(2)}, u32[]{:S(2)}) collective-permute-start(bf16[4,4,72,256]{3,2,1,0:T(8,128)(2,1)S(1)} %get-tuple-element.57), channel_id=1, source_target_pairs={{0,1},{1,0},{2,3},{3,2},{4,5},{5,4},{6,7},{7,6},{8,9},{9,8},{10,11... | collective-permute-start | bytes 1769480 | tf_op jit(solution)/shard_map/g_near/ppermute | solution.py:249
  38.5 0.7 collective-permute-start.5
  39.2 17.2 %collective-permute-done.7 = bf16[128,3712]{1,0:T(8,128)(2,1)S(1)} collective-permute-done((bf16[128,3712]{1,0:T(8,128)(2,1)}, bf16[128,3712]{1,0:T(8,128)(2,1)S(1)}, u32[]{:S(2)}, u32[]{:S(2)}) %collective-permute-start.7) | collective-permute-done | bytes 950304 | tf_op jit(solution)/shard_map/end_a/ppermute | solution.py:249
  56.5 10.4 %collective-permute-done.9.hidden_ref = bf16[4,4,72,256]{3,2,1,0:T(8,128)(2,1)S(1)} collective-permute-done((bf16[4,4,72,256]{3,2,1,0:T(8,128)(2,1)S(1)}, bf16[4,4,72,256]{3,2,1,0:T(8,128)(2,1)S(1)}, u32[]{:S(2)}, u32[]{:S(2)}) %collective-permute-start.9) | collective-permute-done | bytes 589856 | tf_op jit(solution)/shard_map/g_near/ppermute | solution.py:249
  66.9 0.6 collective-permute-start.12
  67.5 1.3 collective-permute-start.13
  68.8 6.6 %collective-permute-start.14 = (bf16[4,4,72,256]{3,2,1,0:T(8,128)(2,1)S(1)}, bf16[4,4,72,256]{3,2,1,0:T(8,128)(2,1)S(1)}, u32[]{:S(2)}, u32[]{:S(2)}) collective-permute-start(bf16[4,4,72,256]{3,2,1,0:T(8,128)(2,1)S(1)} %get-tuple-element.70), channel_id=1, source_target_pairs={{0,2},{3,1},{4,6},{7,5},{8,10},{11,9},{12,14},{15,13},{16,18},{19,... | collective-permute-start | bytes 1769480 | tf_op jit(solution)/shard_map/g_out/ppermute | solution.py:249
  75.5 0.5 collective-permute-start.11
  76.0 1.2 copy-done.1
  77.1 2.1 %shard_map.56.refs_0_ = bf16[1024,512]{1,0:T(8,128)(2,1)S(1)} custom-call(s32[3]{0:T(128)S(1)} %pad_add_fusion.where_ref, bf16[4,4,72,1024]{3,2,1,0:T(8,128)(2,1)S(1)} %bitcast.13, bf16[128,3712]{1,0:T(8,128)(2,1)S(1)} %copy-done.1, bf16[128,3712]{1,0:T(8,128)(2,1)} %collective-permute-done.refs_1_.refs_3_, ...), custom_call_target="tpu_custom_call" | custom-call | flops 150994944 | bytes 3407872 | tf_op jit(solution)/shard_map/pallas_call | solution.py:127
  79.2 8.7 %collective-permute-done.12.refs_4_ = bf16[128,3712]{1,0:T(8,128)(2,1)S(1)} collective-permute-done((bf16[128,3712]{1,0:T(8,128)(2,1)S(1)}, bf16[128,3712]{1,0:T(8,128)(2,1)S(1)}, u32[]{:S(2)}, u32[]{:S(2)}) %collective-permute-start.12) | collective-permute-done | bytes 950304 | tf_op jit(solution)/shard_map/x_far_a/ppermute | solution.py:249
  87.9 3.2 %collective-permute-done.13 = bf16[128,3712]{1,0:T(8,128)(2,1)S(1)} collective-permute-done((bf16[128,3712]{1,0:T(8,128)(2,1)S(1)}, bf16[128,3712]{1,0:T(8,128)(2,1)S(1)}, u32[]{:S(2)}, u32[]{:S(2)}) %collective-permute-start.13) | collective-permute-done | bytes 950304 | tf_op jit(solution)/shard_map/end_b/ppermute | solution.py:249
  91.3 1.3 collective-permute-start.15
  92.7 0.5 collective-permute-start.16
  93.3 1.5 %collective-permute-start.19 = (bf16[128,3712]{1,0:T(8,128)(2,1)S(1)}, bf16[128,3712]{1,0:T(8,128)(2,1)S(1)}, u32[]{:S(2)}, u32[]{:S(2)}) collective-permute-start(bf16[128,3712]{1,0:T(8,128)(2,1)S(1)} %broadcast_select_fusion.refs_0_.refs_6_), channel_id=1, source_target_pairs={{0,8},{1,9},{2,10},{3,11},{4,12},{5,13},{6,14},{7,15},{8,0},{9,1},... | collective-permute-start | bytes 2850824 | tf_op jit(solution)/shard_map/x_far_b/ppermute | solution.py:249
  94.8 2.0 %shard_map.58.refs_1_ = bf16[1024,512]{1,0:T(8,128)(2,1)S(1)} custom-call(s32[3]{0:T(128)S(1)} %pad_add_fusion.where_ref, bf16[4,4,72,256]{3,2,1,0:T(8,128)(2,1)S(1)} %collective-permute-done.9.hidden_ref, bf16[128,3712]{1,0:T(8,128)(2,1)} %collective-permute-done.2.refs_0_.refs_6_, bf16[128,3712]{1,0:T(8,128)(2,1)S(1)} %collective-permute-done.11.refs_1_.refs_7_, ...), custom_call_target="tpu_custom_call" | custom-call | flops 150994944 | bytes 1638400 | tf_op jit(solution)/shard_map/pallas_call | solution.py:127
  96.8 9.4 %collective-permute-done.15.ends_ref = bf16[4,4,72,256]{3,2,1,0:T(8,128)(2,1)S(1)} collective-permute-done((bf16[4,4,72,256]{3,2,1,0:T(8,128)(2,1)S(1)}, bf16[4,4,72,256]{3,2,1,0:T(8,128)(2,1)S(1)}, u32[]{:S(2)}, u32[]{:S(2)}) %collective-permute-start.15) | collective-permute-done | bytes 589856 | tf_op jit(solution)/shard_map/g_in/ppermute | solution.py:249
  106.1 3.6 %collective-permute-start.18 = (bf16[4,4,72,256]{3,2,1,0:T(8,128)(2,1)S(1)}, bf16[4,4,72,256]{3,2,1,0:T(8,128)(2,1)S(1)}, u32[]{:S(2)}, u32[]{:S(2)}) collective-permute-start(bf16[4,4,72,256]{3,2,1,0:T(8,128)(2,1)S(1)} %get-tuple-element.75), channel_id=1, source_target_pairs={{0,3},{3,0},{4,7},{7,4},{8,11},{11,8},{12,15},{15,12},{16,19},{19,... | collective-permute-start | bytes 1769480 | tf_op jit(solution)/shard_map/g_outer/ppermute | solution.py:249
  109.8 11.5 %shard_map.59.refs_10_ = bf16[1024,3584]{1,0:T(8,128)(2,1)S(1)} custom-call(bf16[1024,512]{1,0:T(8,128)(2,1)S(1)} %shard_map.56.refs_0_, bf16[1024,512]{1,0:T(8,128)(2,1)S(1)} %shard_map.58.refs_1_, bf16[128,3712]{1,0:T(8,128)(2,1)S(1)} %copy-done.2, bf16[128,3712]{1,0:T(8,128)(2,1)} %collective-permute-done.refs_1_.refs_3_, ...), custom_call_target="tpu_custom_call" | custom-call | flops 7516192768 | bytes 22020096 | tf_op jit(solution)/shard_map/pallas_call | solution.py:214
  121.3 1.3 shard_map.57.refs_0_
  122.7 2.5 %collective-permute-done.21.refs_3_.refs_9_ = bf16[128,3712]{1,0:T(8,128)(2,1)S(1)} collective-permute-done((bf16[128,3712]{1,0:T(8,128)(2,1)S(1)}, bf16[128,3712]{1,0:T(8,128)(2,1)S(1)}, u32[]{:S(2)}, u32[]{:S(2)}) %collective-permute-start.21) | collective-permute-done | bytes 950304 | tf_op jit(solution)/shard_map/c_xfar_b/ppermute | solution.py:249
  125.2 1.3 shard_map.60.refs_1_
  126.5 13.7 %shard_map.61 = bf16[256,4,3584]{2,1,0:T(4,128)(2,1)} custom-call(bf16[1024,512]{1,0:T(8,128)(2,1)S(1)} %shard_map.57.refs_0_, bf16[1024,512]{1,0:T(8,128)(2,1)S(1)} %shard_map.60.refs_1_, bf16[128,3712]{1,0:T(8,128)(2,1)S(1)} %broadcast_select_fusion.1.refs_0_.refs_2_, bf16[128,3712]{1,0:T(8,128)(2,1)S(1)} %collective-permute-done.16.refs_1_.refs_3_, ...), custom_call_target="tpu_custom_call" | custom-call | flops 7516192768 | bytes 22020096 | tf_op jit(solution)/shard_map/pallas_call | solution.py:214
  (30 shorter events, 1.2 us)
Async XLA Ops:
  0.0 75.9 %copy-start = (bf16[1,4,4,72,1024]{4,3,2,1,0:T(8,128)(2,1)S(1)}, bf16[1,4,4,72,1024]{4,3,2,1,0:T(8,128)(2,1)}, u32[]{:S(2)}) copy-start(bf16[1,4,4,72,1024]{4,3,2,1,0:T(8,128)(2,1)} %param.9) | copy-start | bytes 7077892
  2.5 24.2 %collective-permute-start.3 = (bf16[128,3712]{1,0:T(8,128)(2,1)}, bf16[128,3712]{1,0:T(8,128)(2,1)S(1)}, u32[]{:S(2)}, u32[]{:S(2)}) collective-permute-start(bf16[128,3712]{1,0:T(8,128)(2,1)} %shard_map.55.refs_0_.refs_2_), channel_id=1, source_target_pairs={{0,8},{1,9},{2,10},{3,11},{4,12},{5,13},{6,14},{7,15},{8,0},{9,1},... | collective-permute-start | bytes 2850824 | tf_op jit(solution)/shard_map/x_own/ppermute | solution.py:249
  5.5 22.8 %collective-permute-start.2 = (bf16[128,3712]{1,0:T(8,128)(2,1)}, bf16[128,3712]{1,0:T(8,128)(2,1)}, u32[]{:S(2)}, u32[]{:S(2)}) collective-permute-start(bf16[128,3712]{1,0:T(8,128)(2,1)} %shard_map.55.refs_0_.refs_2_), channel_id=1, source_target_pairs={{0,1},{1,0},{2,3},{3,2},{4,5},{5,4},{6,7},{7,6},{8,9},{9,8},{10,11... | collective-permute-start | bytes 2850824 | tf_op jit(solution)/shard_map/pair/ppermute | solution.py:249
  7.0 21.3 %collective-permute-start.1 = (bf16[128,3712]{1,0:T(8,128)(2,1)}, bf16[128,3712]{1,0:T(8,128)(2,1)}, u32[]{:S(2)}, u32[]{:S(2)}) collective-permute-start(bf16[128,3712]{1,0:T(8,128)(2,1)} %shard_map.55.refs_0_.refs_2_), channel_id=1, source_target_pairs={{1,2},{2,1},{5,6},{6,5},{9,10},{10,9},{13,14},{14,13},{17,18},{18,... | collective-permute-start | bytes 2850824 | tf_op jit(solution)/shard_map/mid_a/ppermute | solution.py:249
  8.7 19.6 %collective-permute-start = (bf16[128,3712]{1,0:T(8,128)(2,1)}, bf16[128,3712]{1,0:T(8,128)(2,1)}, u32[]{:S(2)}, u32[]{:S(2)}) collective-permute-start(bf16[128,3712]{1,0:T(8,128)(2,1)} %shard_map.55.refs_0_.refs_2_), channel_id=1, source_target_pairs={{0,4},{1,5},{2,6},{3,7},{4,0},{5,1},{6,2},{7,3},{8,12},{9,13},{10,... | collective-permute-start | bytes 2850824 | tf_op jit(solution)/shard_map/c_own/ppermute | solution.py:249
  28.3 28.0 %collective-permute-start.7 = (bf16[128,3712]{1,0:T(8,128)(2,1)}, bf16[128,3712]{1,0:T(8,128)(2,1)S(1)}, u32[]{:S(2)}, u32[]{:S(2)}) collective-permute-start(bf16[128,3712]{1,0:T(8,128)(2,1)} %collective-permute-done.1), channel_id=1, source_target_pairs={{1,0},{2,3},{5,4},{6,7},{9,8},{10,11},{13,12},{14,15},{17,16},{18,... | collective-permute-start | bytes 2850824 | tf_op jit(solution)/shard_map/end_a/ppermute | solution.py:249
  29.6 37.3 %collective-permute-start.6 = (bf16[128,3712]{1,0:T(8,128)(2,1)}, bf16[128,3712]{1,0:T(8,128)(2,1)S(1)}, u32[]{:S(2)}, u32[]{:S(2)}) collective-permute-start(bf16[128,3712]{1,0:T(8,128)(2,1)} %collective-permute-done.2.refs_0_.refs_6_), channel_id=1, source_target_pairs={{1,2},{2,1},{5,6},{6,5},{9,10},{10,9},{13,14},{14,13},{17,18},{18,... | collective-permute-start | bytes 2850824 | tf_op jit(solution)/shard_map/mid_b/ppermute | solution.py:249
  30.3 36.6 %collective-permute-start.4 = (bf16[128,3712]{1,0:T(8,128)(2,1)}, bf16[128,3712]{1,0:T(8,128)(2,1)S(1)}, u32[]{:S(2)}, u32[]{:S(2)}) collective-permute-start(bf16[128,3712]{1,0:T(8,128)(2,1)} %collective-permute-done.2.refs_0_.refs_6_), channel_id=1, source_target_pairs={{0,8},{1,9},{2,10},{3,11},{4,12},{5,13},{6,14},{7,15},{8,0},{9,1},... | collective-permute-start | bytes 2850824 | tf_op jit(solution)/shard_map/x_pair/ppermute | solution.py:249
  30.8 36.1 %collective-permute-start.9 = (bf16[4,4,72,256]{3,2,1,0:T(8,128)(2,1)S(1)}, bf16[4,4,72,256]{3,2,1,0:T(8,128)(2,1)S(1)}, u32[]{:S(2)}, u32[]{:S(2)}) collective-permute-start(bf16[4,4,72,256]{3,2,1,0:T(8,128)(2,1)S(1)} %get-tuple-element.57), channel_id=1, source_target_pairs={{0,1},{1,0},{2,3},{3,2},{4,5},{5,4},{6,7},{7,6},{8,9},{9,8},{10,11... | collective-permute-start | bytes 1769480 | tf_op jit(solution)/shard_map/g_near/ppermute | solution.py:249
  38.5 28.4 %collective-permute-start.5 = (bf16[4,4,72,256]{3,2,1,0:T(8,128)(2,1)S(1)}, bf16[4,4,72,256]{3,2,1,0:T(8,128)(2,1)S(1)}, u32[]{:S(2)}, u32[]{:S(2)}) collective-permute-start(bf16[4,4,72,256]{3,2,1,0:T(8,128)(2,1)S(1)} %get-tuple-element.75), channel_id=1, source_target_pairs={{1,2},{2,1},{5,6},{6,5},{9,10},{10,9},{13,14},{14,13},{17,18},{18,... | collective-permute-start | bytes 1769480 | tf_op jit(solution)/shard_map/g_inner/ppermute | solution.py:249
  56.3 10.5 %collective-permute-start.8 = (bf16[128,3712]{1,0:T(8,128)(2,1)S(1)}, bf16[128,3712]{1,0:T(8,128)(2,1)S(1)}, u32[]{:S(2)}, u32[]{:S(2)}) collective-permute-start(bf16[128,3712]{1,0:T(8,128)(2,1)S(1)} %collective-permute-done.3.refs_2_.refs_4_), channel_id=1, source_target_pairs={{0,4},{1,5},{2,6},{3,7},{4,0},{5,1},{6,2},{7,3},{8,12},{9,13},{10,... | collective-permute-start | bytes 2850824 | tf_op jit(solution)/shard_map/c_xown/ppermute | solution.py:249
  66.9 21.0 %collective-permute-start.12 = (bf16[128,3712]{1,0:T(8,128)(2,1)S(1)}, bf16[128,3712]{1,0:T(8,128)(2,1)S(1)}, u32[]{:S(2)}, u32[]{:S(2)}) collective-permute-start(bf16[128,3712]{1,0:T(8,128)(2,1)S(1)} %broadcast_select_fusion.1.refs_0_.refs_2_), channel_id=1, source_target_pairs={{0,8},{1,9},{2,10},{3,11},{4,12},{5,13},{6,14},{7,15},{8,0},{9,1},... | collective-permute-start | bytes 2850824 | tf_op jit(solution)/shard_map/x_far_a/ppermute | solution.py:249
  67.5 23.6 %collective-permute-start.13 = (bf16[128,3712]{1,0:T(8,128)(2,1)S(1)}, bf16[128,3712]{1,0:T(8,128)(2,1)S(1)}, u32[]{:S(2)}, u32[]{:S(2)}) collective-permute-start(bf16[128,3712]{1,0:T(8,128)(2,1)S(1)} %collective-permute-done.6), channel_id=1, source_target_pairs={{1,0},{2,3},{5,4},{6,7},{9,8},{10,11},{13,12},{14,15},{17,16},{18,... | collective-permute-start | bytes 2850824 | tf_op jit(solution)/shard_map/end_b/ppermute | solution.py:249
  68.8 22.5 %collective-permute-start.14 = (bf16[4,4,72,256]{3,2,1,0:T(8,128)(2,1)S(1)}, bf16[4,4,72,256]{3,2,1,0:T(8,128)(2,1)S(1)}, u32[]{:S(2)}, u32[]{:S(2)}) collective-permute-start(bf16[4,4,72,256]{3,2,1,0:T(8,128)(2,1)S(1)} %get-tuple-element.70), channel_id=1, source_target_pairs={{0,2},{3,1},{4,6},{7,5},{8,10},{11,9},{12,14},{15,13},{16,18},{19,... | collective-permute-start | bytes 1769480 | tf_op jit(solution)/shard_map/g_out/ppermute | solution.py:249
  75.4 15.9 %collective-permute-start.10 = (bf16[128,3712]{1,0:T(8,128)(2,1)S(1)}, bf16[128,3712]{1,0:T(8,128)(2,1)S(1)}, u32[]{:S(2)}, u32[]{:S(2)}) collective-permute-start(bf16[128,3712]{1,0:T(8,128)(2,1)S(1)} %collective-permute-done.4.refs_2_.refs_8_), channel_id=1, source_target_pairs={{0,4},{1,5},{2,6},{3,7},{4,0},{5,1},{6,2},{7,3},{8,12},{9,13},{10,... | collective-permute-start | bytes 2850824 | tf_op jit(solution)/shard_map/c_xpair/ppermute | solution.py:249
  75.5 15.8 %collective-permute-start.11 = (bf16[128,3712]{1,0:T(8,128)(2,1)}, bf16[128,3712]{1,0:T(8,128)(2,1)S(1)}, u32[]{:S(2)}, u32[]{:S(2)}) collective-permute-start(bf16[128,3712]{1,0:T(8,128)(2,1)} %collective-permute-done.2.refs_0_.refs_6_), channel_id=1, source_target_pairs={{0,4},{1,5},{2,6},{3,7},{4,0},{5,1},{6,2},{7,3},{8,12},{9,13},{10,... | collective-permute-start | bytes 2850824 | tf_op jit(solution)/shard_map/c_pair/ppermute | solution.py:249
  76.0 1.2 copy-start.1
  77.1 32.6 %copy-start.2 = (bf16[128,3712]{1,0:T(8,128)(2,1)S(1)}, bf16[128,3712]{1,0:T(8,128)(2,1)}, u32[]{:S(2)}) copy-start(bf16[128,3712]{1,0:T(8,128)(2,1)} %shard_map.55.refs_0_.refs_2_) | copy-start | bytes 2850820
  91.3 14.8 %collective-permute-start.15 = (bf16[4,4,72,256]{3,2,1,0:T(8,128)(2,1)S(1)}, bf16[4,4,72,256]{3,2,1,0:T(8,128)(2,1)S(1)}, u32[]{:S(2)}, u32[]{:S(2)}) collective-permute-start(bf16[4,4,72,256]{3,2,1,0:T(8,128)(2,1)S(1)} %get-tuple-element.70), channel_id=1, source_target_pairs={{2,0},{1,3},{6,4},{5,7},{10,8},{9,11},{14,12},{13,15},{18,16},{17,... | collective-permute-start | bytes 1769480 | tf_op jit(solution)/shard_map/g_in/ppermute | solution.py:249
  92.6 28.7 %collective-permute-start.17 = (bf16[128,3712]{1,0:T(8,128)(2,1)S(1)}, bf16[128,3712]{1,0:T(8,128)(2,1)S(1)}, u32[]{:S(2)}, u32[]{:S(2)}) collective-permute-start(bf16[128,3712]{1,0:T(8,128)(2,1)S(1)} %collective-permute-done.12.refs_4_), channel_id=1, source_target_pairs={{0,4},{1,5},{2,6},{3,7},{4,0},{5,1},{6,2},{7,3},{8,12},{9,13},{10,... | collective-permute-start | bytes 2850824 | tf_op jit(solution)/shard_map/c_xfar_a/ppermute | solution.py:249
  92.7 28.6 %collective-permute-start.16 = (bf16[128,3712]{1,0:T(8,128)(2,1)S(1)}, bf16[128,3712]{1,0:T(8,128)(2,1)S(1)}, u32[]{:S(2)}, u32[]{:S(2)}) collective-permute-start(bf16[128,3712]{1,0:T(8,128)(2,1)S(1)} %broadcast_select_fusion.1.refs_0_.refs_2_), channel_id=1, source_target_pairs={{0,4},{1,5},{2,6},{3,7},{4,0},{5,1},{6,2},{7,3},{8,12},{9,13},{10,... | collective-permute-start | bytes 2850824 | tf_op jit(solution)/shard_map/c_far_a/ppermute | solution.py:249
  93.2 29.4 %collective-permute-start.20 = (bf16[128,3712]{1,0:T(8,128)(2,1)S(1)}, bf16[128,3712]{1,0:T(8,128)(2,1)S(1)}, u32[]{:S(2)}, u32[]{:S(2)}) collective-permute-start(bf16[128,3712]{1,0:T(8,128)(2,1)S(1)} %broadcast_select_fusion.refs_0_.refs_6_), channel_id=1, source_target_pairs={{0,4},{1,5},{2,6},{3,7},{4,0},{5,1},{6,2},{7,3},{8,12},{9,13},{10,... | collective-permute-start | bytes 2850824 | tf_op jit(solution)/shard_map/c_far_b/ppermute | solution.py:249
  93.3 29.3 %collective-permute-start.19 = (bf16[128,3712]{1,0:T(8,128)(2,1)S(1)}, bf16[128,3712]{1,0:T(8,128)(2,1)S(1)}, u32[]{:S(2)}, u32[]{:S(2)}) collective-permute-start(bf16[128,3712]{1,0:T(8,128)(2,1)S(1)} %broadcast_select_fusion.refs_0_.refs_6_), channel_id=1, source_target_pairs={{0,8},{1,9},{2,10},{3,11},{4,12},{5,13},{6,14},{7,15},{8,0},{9,1},... | collective-permute-start | bytes 2850824 | tf_op jit(solution)/shard_map/x_far_b/ppermute | solution.py:249
  106.1 16.4 %collective-permute-start.18 = (bf16[4,4,72,256]{3,2,1,0:T(8,128)(2,1)S(1)}, bf16[4,4,72,256]{3,2,1,0:T(8,128)(2,1)S(1)}, u32[]{:S(2)}, u32[]{:S(2)}) collective-permute-start(bf16[4,4,72,256]{3,2,1,0:T(8,128)(2,1)S(1)} %get-tuple-element.75), channel_id=1, source_target_pairs={{0,3},{3,0},{4,7},{7,4},{8,11},{11,8},{12,15},{15,12},{16,19},{19,... | collective-permute-start | bytes 1769480 | tf_op jit(solution)/shard_map/g_outer/ppermute | solution.py:249
  122.6 2.6 %collective-permute-start.21 = (bf16[128,3712]{1,0:T(8,128)(2,1)S(1)}, bf16[128,3712]{1,0:T(8,128)(2,1)S(1)}, u32[]{:S(2)}, u32[]{:S(2)}) collective-permute-start(bf16[128,3712]{1,0:T(8,128)(2,1)S(1)} %collective-permute-done.19.refs_2_.refs_8_), channel_id=1, source_target_pairs={{0,4},{1,5},{2,6},{3,7},{4,0},{5,1},{6,2},{7,3},{8,12},{9,13},{10,... | collective-permute-start | bytes 2850824 | tf_op jit(solution)/shard_map/c_xfar_b/ppermute | solution.py:249

commit v4 on v3

--- a/solution.py
+++ b/solution.py
@@ -176,7 +176,7 @@
     return spread_call(body, where, [hidden_ends, hidden_inner], 1, labels, 1)[0]
 
 
-def product(spreads, rows, width, acc=None, last=False, experts=4, tile=512):
+def product(spreads, rows, width, acc=None, last=False, experts=4, tile=512, cost=1):
     n_tok = rows[0].shape[0]
     m = spreads[0].shape[0]
     k = sum(s.shape[1] for s in spreads)
@@ -219,8 +219,8 @@
         out_shape=out_shape,
         compiler_params=pltpu.CompilerParams(vmem_limit_bytes=20 << 20),
         cost_estimate=pl.CostEstimate(
-            flops=2 * m * k * width,
-            bytes_accessed=m * width * 4 + k * width * 2,
+            flops=cost * 2 * m * k * width,
+            bytes_accessed=cost * (m * width * 4 + k * width * 2),
             transcendentals=0,
         ),
     )(*args)
@@ -273,8 +273,8 @@
     mid_a = send("mid_a", own, same, middle)
     x_own = send("x_own", own, side, stay)
     pair = send("pair", own, same, near)
-    c_own, own, h_flip, h_near, mid_a, h_cross, pair, x_own, where = tie(
-        (c_own, own, h_flip, h_near, mid_a, h_cross, pair, x_own, where)
+    own, c_own, mid_a, x_own, pair, where, h_near, h_cross, h_flip = tie(
+        (own, c_own, mid_a, x_own, pair, where, h_near, h_cross, h_flip)
     )
 
     end_a = send("end_a", mid_a, same, outward)
@@ -284,8 +284,8 @@
     g_inner = send("g_inner", h_flip, same, middle)
     c_xown = send("c_xown", x_own, core, stay)
     far_a = jnp.where(inner, mid_a, end_a)
-    c_own, x_pair, pair, own, g_inner, mid_b, far_a, h_flip, c_xown, h_cross, x_own, g_near = tie(
-        (c_own, x_pair, pair, own, g_inner, mid_b, far_a, h_flip, c_xown, h_cross, x_own, g_near)
+    x_pair, g_near, g_inner, c_xown, far_a, mid_b, own, c_own, x_own, pair, h_cross, h_flip = tie(
+        (x_pair, g_near, g_inner, c_xown, far_a, mid_b, own, c_own, x_own, pair, h_cross, h_flip)
     )
 
     end_b = send("end_b", mid_b, same, outward)
@@ -295,31 +295,35 @@
     c_pair = send("c_pair", pair, core, stay)
     l_xfar_a = x_far_a[:, width:]
     s_own = spread(where, hidden, n_replica, [own, c_own, x_own, c_xown])
+    acc = product([s_own], [own, c_own, x_own, c_xown], width)
     far_b = jnp.where(inner, mid_b, end_b)
-    c_xpair, c_pair, h_cross, h_flip, pair, x_far_a, s_own, c_xown, far_b, c_own, far_a, x_own, l_xfar_a, g_out, own, x_pair = tie(
-        (c_xpair, c_pair, h_cross, h_flip, pair, x_far_a, s_own, c_xown, far_b, c_own, far_a, x_own, l_xfar_a, g_out, own, x_pair)
-    )
-
-    g_outer = send("g_outer", h_flip, same, outer)
+    far_b, x_far_a, l_xfar_a, g_out, c_xpair, c_pair, acc, pair, x_pair, far_a, h_cross, h_flip = tie(
+        (far_b, x_far_a, l_xfar_a, g_out, c_xpair, c_pair, acc, pair, x_pair, far_a, h_cross, h_flip)
+    )
+
+    x_far_b = send("x_far_b", far_b, side, stay)
     g_in = send("g_in", h_cross, same, cross_in)
-    x_far_b = send("x_far_b", far_b, side, stay)
     c_far_a = send("c_far_a", far_a, core, stay)
     c_xfar_a = send("c_xfar_a", x_far_a, core, stay)
-    rows_own = [own, c_own, x_own, c_xown]
     rows_near = [pair, c_pair, x_pair, c_xpair]
     s_near = spread(where, g_near, 1, rows_near)
-    acc = product([s_own, s_near], rows_own + rows_near, width)
+    acc = product([s_near], rows_near, width, acc, cost=4)
+    g_in, acc, h_flip, far_b = tie(
+        (g_in, acc, h_flip, far_b)
+    )
+
+    g_outer = send("g_outer", h_flip, same, outer)
     c_far_b = send("c_far_b", far_b, core, stay)
     s_a = spread_far(where, g_in, g_inner, [far_a, c_far_a, l_xfar_a, c_xfar_a])
-    far_b, s_a, g_outer, x_far_b, acc, c_xfar_a, c_far_a, c_far_b = tie(
-        (far_b, s_a, g_outer, x_far_b, acc, c_xfar_a, c_far_a, c_far_b)
+    acc = product([s_a], [far_a, c_far_a, x_far_a, c_xfar_a], width, acc)
+    g_outer, x_far_b, c_far_b, acc, far_b = tie(
+        (g_outer, x_far_b, c_far_b, acc, far_b)
     )
 
     c_xfar_b = send("c_xfar_b", x_far_b, core, stay)
-    rows_a = [far_a, c_far_a, x_far_a, c_xfar_a]
     rows_b = [far_b, c_far_b, x_far_b, c_xfar_b]
     s_b = spread_far(where, g_outer, g_out, rows_b)
-    return product([s_a, s_b], rows_a + rows_b, width, acc, last=True, experts=per_device)
+    return product([s_b], rows_b, width, acc, last=True, experts=per_device)
 
 
 def solution(mesh):

time: 141 us -> 139 us (0.986)
  waiting for transfers between devices: 69.3 us -> 62.5 us
  Pallas kernels: 34.3 us -> 39.5 us
    ppermute x22, waiting for transfers between devices: 69.3 us -> 62.5 us  [send(): return lax.ppermute(array, both, pairs)]
    pallas_call x2 -> x4, Pallas kernels: 25.1 us -> 30.3 us  [product(): pl.pallas_call(body, grid=(width // tile,), in_specs=in_specs, out_specs=...]
  transfers between devices with their start and end apart: 22 -> 22, of which waited for: 8 -> 9; matrix products, arithmetic and copies ran while one was open for 1% -> 1% of each run, Pallas kernels for 12% -> 19%
where the time goes in v4:
time: 139 us; the launch traced here: 138 us
  waiting for transfers between devices  62.5 us (45%)
  Pallas kernels  39.5 us (28%)
  starting transfers between devices  32.9 us (24%)
  local copies, waits for them, and re-layouts  2.76 us (2%)
    ppermute x22, waiting for transfers between devices, send(): return lax.ppermute(array, both, pairs)  62.5 us
    ppermute x22, starting transfers between devices, send(): return lax.ppermute(array, both, pairs)  32.9 us
    pallas_call x4, Pallas kernels, product(): pl.pallas_call(body, grid=(width // tile,), in_specs=in_specs, out_specs=...  30.3 us
    pallas_call x4, Pallas kernels, spread_call(): pl.pallas_call(body, grid_spec=pltpu.PrefetchScalarGridSpec(num_scalar_pr...  6.63 us
  transfers between devices with their start and end apart: 22, of which 9 were waited for; matrix products, arithmetic and copies ran while one was open for 1% of the time, Pallas kernels for 19%

profile of v4, /device:TPU:0, one launch (start us, length us, event | category | flops | bytes accessed | tf_op | source)
XLA Modules:
  0.0 138.1 jit_solution(3187199661957269903)
XLA Ops:
  0.0 2.5 %shard_map.55.refs_0_.refs_1_ = bf16[128,3712]{1,0:T(8,128)(2,1)} custom-call(bf16[128,3584]{1,0:T(8,128)(2,1)} %rows_ref.1, f32[1,128]{1,0:T(1,128)} %bitcast.16, f32[8,128]{1,0:T(8,128)} %bitcast.14, s32[8,128]{1,0:T(8,128)} %bitcast.15), custom_call_target="tpu_custom_call" | custom-call | tf_op jit(solution)/shard_map/pallas_call | solution.py:87
  2.5 3.0 %collective-permute-start.3 = (bf16[128,3712]{1,0:T(8,128)(2,1)}, bf16[128,3712]{1,0:T(8,128)(2,1)}, u32[]{:S(2)}, u32[]{:S(2)}) collective-permute-start(bf16[128,3712]{1,0:T(8,128)(2,1)} %shard_map.55.refs_0_.refs_1_), channel_id=1, source_target_pairs={{0,1},{1,0},{2,3},{3,2},{4,5},{5,4},{6,7},{7,6},{8,9},{9,8},{10,11... | collective-permute-start | bytes 2850824 | tf_op jit(solution)/shard_map/pair/ppermute | solution.py:249
  5.6 1.5 %collective-permute-start.2 = (bf16[128,3712]{1,0:T(8,128)(2,1)}, bf16[128,3712]{1,0:T(8,128)(2,1)}, u32[]{:S(2)}, u32[]{:S(2)}) collective-permute-start(bf16[128,3712]{1,0:T(8,128)(2,1)} %shard_map.55.refs_0_.refs_1_), channel_id=1, source_target_pairs={{0,8},{1,9},{2,10},{3,11},{4,12},{5,13},{6,14},{7,15},{8,0},{9,1},... | collective-permute-start | bytes 2850824 | tf_op jit(solution)/shard_map/x_own/ppermute | solution.py:249
  7.0 1.6 %collective-permute-start.1 = (bf16[128,3712]{1,0:T(8,128)(2,1)}, bf16[128,3712]{1,0:T(8,128)(2,1)}, u32[]{:S(2)}, u32[]{:S(2)}) collective-permute-start(bf16[128,3712]{1,0:T(8,128)(2,1)} %shard_map.55.refs_0_.refs_1_), channel_id=1, source_target_pairs={{1,2},{2,1},{5,6},{6,5},{9,10},{10,9},{13,14},{14,13},{17,18},{18,... | collective-permute-start | bytes 2850824 | tf_op jit(solution)/shard_map/mid_a/ppermute | solution.py:249
  8.7 1.6 %dynamic-slice_bitcast_fusion = (bf16[4,4,72,256]{3,2,1,0:T(8,128)(2,1)S(1)}, bf16[4,4,72,256]{3,2,1,0:T(8,128)(2,1)S(1)}, bf16[4,4,72,256]{3,2,1,0:T(8,128)(2,1)S(1)}) fusion(bf16[1,4,4,72,1024]{4,3,2,1,0:T(8,128)(2,1)} %param.9, s32[]{:T(128)S(6)} %select_n.28, s32[]{:T(128)S(6)} %select_n.27, s32[]{:T(128)S(6)} %select_n.26), kind=kLoop, calls=%fused_computation.2 | loop fusion | bytes 3538956 | tf_op jit(solution)/shard_map/dynamic_slice | solution.py:264
  10.3 16.7 %collective-permute-done.3.refs_0_.refs_1_ = bf16[128,3712]{1,0:T(8,128)(2,1)} collective-permute-done((bf16[128,3712]{1,0:T(8,128)(2,1)}, bf16[128,3712]{1,0:T(8,128)(2,1)}, u32[]{:S(2)}, u32[]{:S(2)}) %collective-permute-start.3) | collective-permute-done | bytes 950304 | tf_op jit(solution)/shard_map/pair/ppermute | solution.py:249
  27.0 1.4 %collective-permute-done.2.refs_2_.refs_3_ = bf16[128,3712]{1,0:T(8,128)(2,1)} collective-permute-done((bf16[128,3712]{1,0:T(8,128)(2,1)}, bf16[128,3712]{1,0:T(8,128)(2,1)}, u32[]{:S(2)}, u32[]{:S(2)}) %collective-permute-start.2) | collective-permute-done | bytes 950304 | tf_op jit(solution)/shard_map/x_own/ppermute | solution.py:249
  28.4 1.3 collective-permute-start.8
  29.7 0.7 collective-permute-start.9
  30.4 1.6 %collective-permute-start.4 = (bf16[128,3712]{1,0:T(8,128)(2,1)}, bf16[128,3712]{1,0:T(8,128)(2,1)S(1)}, u32[]{:S(2)}, u32[]{:S(2)}) collective-permute-start(bf16[128,3712]{1,0:T(8,128)(2,1)} %collective-permute-done.3.refs_0_.refs_1_), channel_id=1, source_target_pairs={{0,8},{1,9},{2,10},{3,11},{4,12},{5,13},{6,14},{7,15},{8,0},{9,1},... | collective-permute-start | bytes 2850824 | tf_op jit(solution)/shard_map/x_pair/ppermute | solution.py:249
  32.0 6.5 %collective-permute-start.5 = (bf16[4,4,72,256]{3,2,1,0:T(8,128)(2,1)S(1)}, bf16[4,4,72,256]{3,2,1,0:T(8,128)(2,1)S(1)}, u32[]{:S(2)}, u32[]{:S(2)}) collective-permute-start(bf16[4,4,72,256]{3,2,1,0:T(8,128)(2,1)S(1)} %get-tuple-element.49), channel_id=1, source_target_pairs={{0,1},{1,0},{2,3},{3,2},{4,5},{5,4},{6,7},{7,6},{8,9},{9,8},{10,11... | collective-permute-start | bytes 1769480 | tf_op jit(solution)/shard_map/g_near/ppermute | solution.py:249
  39.2 17.2 %collective-permute-done.8 = bf16[128,3712]{1,0:T(8,128)(2,1)S(1)} collective-permute-done((bf16[128,3712]{1,0:T(8,128)(2,1)}, bf16[128,3712]{1,0:T(8,128)(2,1)S(1)}, u32[]{:S(2)}, u32[]{:S(2)}) %collective-permute-start.8) | collective-permute-done | bytes 950304 | tf_op jit(solution)/shard_map/end_a/ppermute | solution.py:249
  56.5 10.4 %collective-permute-done.5.hidden_ref = bf16[4,4,72,256]{3,2,1,0:T(8,128)(2,1)S(1)} collective-permute-done((bf16[4,4,72,256]{3,2,1,0:T(8,128)(2,1)S(1)}, bf16[4,4,72,256]{3,2,1,0:T(8,128)(2,1)S(1)}, u32[]{:S(2)}, u32[]{:S(2)}) %collective-permute-start.5) | collective-permute-done | bytes 589856 | tf_op jit(solution)/shard_map/g_near/ppermute | solution.py:249
  67.5 1.3 collective-permute-start.10
  68.8 6.6 %collective-permute-start.12 = (bf16[4,4,72,256]{3,2,1,0:T(8,128)(2,1)S(1)}, bf16[4,4,72,256]{3,2,1,0:T(8,128)(2,1)S(1)}, u32[]{:S(2)}, u32[]{:S(2)}) collective-permute-start(bf16[4,4,72,256]{3,2,1,0:T(8,128)(2,1)S(1)} %get-tuple-element.66), channel_id=1, source_target_pairs={{0,2},{3,1},{4,6},{7,5},{8,10},{11,9},{12,14},{15,13},{16,18},{19,... | collective-permute-start | bytes 1769480 | tf_op jit(solution)/shard_map/g_out/ppermute | solution.py:249
  76.0 1.2 copy-done.1
  77.1 2.1 %shard_map.56.refs_0_ = bf16[1024,512]{1,0:T(8,128)(2,1)S(1)} custom-call(s32[3]{0:T(128)S(1)} %pad_add_fusion.where_ref, bf16[4,4,72,1024]{3,2,1,0:T(8,128)(2,1)S(1)} %bitcast.13, bf16[128,3712]{1,0:T(8,128)(2,1)S(1)} %copy-done.1, bf16[128,3712]{1,0:T(8,128)(2,1)} %collective-permute-done.refs_1_.refs_2_, ...), custom_call_target="tpu_custom_call" | custom-call | flops 150994944 | bytes 3407872 | tf_op jit(solution)/shard_map/pallas_call | solution.py:127
  79.2 7.2 %shard_map.57.refs_5_ = bf16[1024,3584]{1,0:T(8,128)(2,1)S(1)} custom-call(bf16[1024,512]{1,0:T(8,128)(2,1)S(1)} %shard_map.56.refs_0_, bf16[128,3712]{1,0:T(8,128)(2,1)S(1)} %copy-done.2, bf16[128,3712]{1,0:T(8,128)(2,1)} %collective-permute-done.refs_1_.refs_2_, bf16[128,3712]{1,0:T(8,128)(2,1)} %collective-permute-done.2.refs_2_.refs_3_, ...), custom_call_target="tpu_custom_call" | custom-call | flops 3758096384 | bytes 18350080 | tf_op jit(solution)/shard_map/pallas_call | solution.py:214
  86.4 1.5 %collective-permute-done.11.refs_3_ = bf16[128,3712]{1,0:T(8,128)(2,1)S(1)} collective-permute-done((bf16[128,3712]{1,0:T(8,128)(2,1)S(1)}, bf16[128,3712]{1,0:T(8,128)(2,1)S(1)}, u32[]{:S(2)}, u32[]{:S(2)}) %collective-permute-start.11) | collective-permute-done | bytes 950304 | tf_op jit(solution)/shard_map/x_far_a/ppermute | solution.py:249
  87.9 3.2 %collective-permute-done.10 = bf16[128,3712]{1,0:T(8,128)(2,1)S(1)} collective-permute-done((bf16[128,3712]{1,0:T(8,128)(2,1)S(1)}, bf16[128,3712]{1,0:T(8,128)(2,1)S(1)}, u32[]{:S(2)}, u32[]{:S(2)}) %collective-permute-start.10) | collective-permute-done | bytes 950304 | tf_op jit(solution)/shard_map/end_b/ppermute | solution.py:249
  91.3 1.3 collective-permute-start.15
  92.6 1.6 %collective-permute-start.17 = (bf16[128,3712]{1,0:T(8,128)(2,1)S(1)}, bf16[128,3712]{1,0:T(8,128)(2,1)S(1)}, u32[]{:S(2)}, u32[]{:S(2)}) collective-permute-start(bf16[128,3712]{1,0:T(8,128)(2,1)S(1)} %broadcast_select_fusion.refs_0_.refs_1_), channel_id=1, source_target_pairs={{0,8},{1,9},{2,10},{3,11},{4,12},{5,13},{6,14},{7,15},{8,0},{9,1},... | collective-permute-start | bytes 2850824 | tf_op jit(solution)/shard_map/x_far_b/ppermute | solution.py:249
  94.6 2.0 %shard_map.58.refs_0_ = bf16[1024,512]{1,0:T(8,128)(2,1)S(1)} custom-call(s32[3]{0:T(128)S(1)} %pad_add_fusion.where_ref, bf16[4,4,72,256]{3,2,1,0:T(8,128)(2,1)S(1)} %collective-permute-done.5.hidden_ref, bf16[128,3712]{1,0:T(8,128)(2,1)} %collective-permute-done.3.refs_0_.refs_1_, bf16[128,3712]{1,0:T(8,128)(2,1)S(1)} %collective-permute-done.14.refs_1_.refs_2_, ...), custom_call_target="tpu_custom_call" | custom-call | flops 150994944 | bytes 1638400 | tf_op jit(solution)/shard_map/pallas_call | solution.py:127
  96.6 7.3 %shard_map.59.refs_5_ = bf16[1024,3584]{1,0:T(8,128)(2,1)S(1)} custom-call(bf16[1024,512]{1,0:T(8,128)(2,1)S(1)} %shard_map.58.refs_0_, bf16[128,3712]{1,0:T(8,128)(2,1)} %collective-permute-done.3.refs_0_.refs_1_, bf16[128,3712]{1,0:T(8,128)(2,1)S(1)} %collective-permute-done.14.refs_1_.refs_2_, ...), custom_call_target="tpu_custom_call" | custom-call | flops 15032385536 | bytes 73400320 | tf_op jit(solution)/shard_map/pallas_call | solution.py:214
  104.0 2.1 %collective-permute-done.15.ends_ref = bf16[4,4,72,256]{3,2,1,0:T(8,128)(2,1)S(1)} collective-permute-done((bf16[4,4,72,256]{3,2,1,0:T(8,128)(2,1)S(1)}, bf16[4,4,72,256]{3,2,1,0:T(8,128)(2,1)S(1)}, u32[]{:S(2)}, u32[]{:S(2)}) %collective-permute-start.15) | collective-permute-done | bytes 589856 | tf_op jit(solution)/shard_map/g_in/ppermute | solution.py:249
  106.1 3.6 %collective-permute-start.16 = (bf16[4,4,72,256]{3,2,1,0:T(8,128)(2,1)S(1)}, bf16[4,4,72,256]{3,2,1,0:T(8,128)(2,1)S(1)}, u32[]{:S(2)}, u32[]{:S(2)}) collective-permute-start(bf16[4,4,72,256]{3,2,1,0:T(8,128)(2,1)S(1)} %get-tuple-element.75), channel_id=1, source_target_pairs={{0,3},{3,0},{4,7},{7,4},{8,11},{11,8},{12,15},{15,12},{16,19},{19,... | collective-permute-start | bytes 1769480 | tf_op jit(solution)/shard_map/g_outer/ppermute | solution.py:249
  109.8 1.3 shard_map.60.refs_0_
  111.1 7.0 %shard_map.61.refs_5_ = bf16[1024,3584]{1,0:T(8,128)(2,1)S(1)} custom-call(bf16[1024,512]{1,0:T(8,128)(2,1)S(1)} %shard_map.60.refs_0_, bf16[128,3712]{1,0:T(8,128)(2,1)S(1)} %broadcast_select_fusion.1.refs_0_.refs_1_, bf16[128,3712]{1,0:T(8,128)(2,1)S(1)} %collective-permute-done.19.refs_1_.refs_2_, bf16[128,3712]{1,0:T(8,128)(2,1)S(1)} %collective-permute-done.11.refs_3_, ...), custom_call_target="tpu_custom_call" | custom-call | flops 3758096384 | bytes 18350080 | tf_op jit(solution)/shard_map/pallas_call | solution.py:214
  118.1 7.5 %collective-permute-done.16.ends_ref = bf16[4,4,72,256]{3,2,1,0:T(8,128)(2,1)S(1)} collective-permute-done((bf16[4,4,72,256]{3,2,1,0:T(8,128)(2,1)S(1)}, bf16[4,4,72,256]{3,2,1,0:T(8,128)(2,1)S(1)}, u32[]{:S(2)}, u32[]{:S(2)}) %collective-permute-start.16) | collective-permute-done | bytes 589856 | tf_op jit(solution)/shard_map/g_outer/ppermute | solution.py:249
  125.5 2.5 %collective-permute-done.21.refs_3_.refs_4_ = bf16[128,3712]{1,0:T(8,128)(2,1)S(1)} collective-permute-done((bf16[128,3712]{1,0:T(8,128)(2,1)S(1)}, bf16[128,3712]{1,0:T(8,128)(2,1)S(1)}, u32[]{:S(2)}, u32[]{:S(2)}) %collective-permute-start.21) | collective-permute-done | bytes 950304 | tf_op jit(solution)/shard_map/c_xfar_b/ppermute | solution.py:249
  128.0 1.3 shard_map.62.refs_0_
  129.3 8.8 %shard_map.63 = bf16[256,4,3584]{2,1,0:T(4,128)(2,1)} custom-call(bf16[1024,512]{1,0:T(8,128)(2,1)S(1)} %shard_map.62.refs_0_, bf16[128,3712]{1,0:T(8,128)(2,1)S(1)} %broadcast_select_fusion.refs_0_.refs_1_, bf16[128,3712]{1,0:T(8,128)(2,1)S(1)} %collective-permute-done.18.refs_1_.refs_2_, bf16[128,3712]{1,0:T(8,128)(2,1)S(1)} %collective-permute-done.17.refs_2_.refs_3_, ...), custom_call_target="tpu_custom_call" | custom-call | flops 3758096384 | bytes 18350080 | tf_op jit(solution)/shard_map/pallas_call | solution.py:214
  (32 shorter events, 2.7 us)
Async XLA Ops:
  0.0 76.0 %copy-start = (bf16[1,4,4,72,1024]{4,3,2,1,0:T(8,128)(2,1)S(1)}, bf16[1,4,4,72,1024]{4,3,2,1,0:T(8,128)(2,1)}, u32[]{:S(2)}) copy-start(bf16[1,4,4,72,1024]{4,3,2,1,0:T(8,128)(2,1)} %param.9) | copy-start | bytes 7077892
  2.5 76.7 %copy-start.2 = (bf16[128,3712]{1,0:T(8,128)(2,1)S(1)}, bf16[128,3712]{1,0:T(8,128)(2,1)}, u32[]{:S(2)}) copy-start(bf16[128,3712]{1,0:T(8,128)(2,1)} %shard_map.55.refs_0_.refs_1_) | copy-start | bytes 2850820
  2.5 24.5 %collective-permute-start.3 = (bf16[128,3712]{1,0:T(8,128)(2,1)}, bf16[128,3712]{1,0:T(8,128)(2,1)}, u32[]{:S(2)}, u32[]{:S(2)}) collective-permute-start(bf16[128,3712]{1,0:T(8,128)(2,1)} %shard_map.55.refs_0_.refs_1_), channel_id=1, source_target_pairs={{0,1},{1,0},{2,3},{3,2},{4,5},{5,4},{6,7},{7,6},{8,9},{9,8},{10,11... | collective-permute-start | bytes 2850824 | tf_op jit(solution)/shard_map/pair/ppermute | solution.py:249
  5.6 22.8 %collective-permute-start.2 = (bf16[128,3712]{1,0:T(8,128)(2,1)}, bf16[128,3712]{1,0:T(8,128)(2,1)}, u32[]{:S(2)}, u32[]{:S(2)}) collective-permute-start(bf16[128,3712]{1,0:T(8,128)(2,1)} %shard_map.55.refs_0_.refs_1_), channel_id=1, source_target_pairs={{0,8},{1,9},{2,10},{3,11},{4,12},{5,13},{6,14},{7,15},{8,0},{9,1},... | collective-permute-start | bytes 2850824 | tf_op jit(solution)/shard_map/x_own/ppermute | solution.py:249
  7.0 21.3 %collective-permute-start.1 = (bf16[128,3712]{1,0:T(8,128)(2,1)}, bf16[128,3712]{1,0:T(8,128)(2,1)}, u32[]{:S(2)}, u32[]{:S(2)}) collective-permute-start(bf16[128,3712]{1,0:T(8,128)(2,1)} %shard_map.55.refs_0_.refs_1_), channel_id=1, source_target_pairs={{1,2},{2,1},{5,6},{6,5},{9,10},{10,9},{13,14},{14,13},{17,18},{18,... | collective-permute-start | bytes 2850824 | tf_op jit(solution)/shard_map/mid_a/ppermute | solution.py:249
  8.7 19.7 %collective-permute-start = (bf16[128,3712]{1,0:T(8,128)(2,1)}, bf16[128,3712]{1,0:T(8,128)(2,1)}, u32[]{:S(2)}, u32[]{:S(2)}) collective-permute-start(bf16[128,3712]{1,0:T(8,128)(2,1)} %shard_map.55.refs_0_.refs_1_), channel_id=1, source_target_pairs={{0,4},{1,5},{2,6},{3,7},{4,0},{5,1},{6,2},{7,3},{8,12},{9,13},{10,... | collective-permute-start | bytes 2850824 | tf_op jit(solution)/shard_map/c_own/ppermute | solution.py:249
  28.4 28.0 %collective-permute-start.8 = (bf16[128,3712]{1,0:T(8,128)(2,1)}, bf16[128,3712]{1,0:T(8,128)(2,1)S(1)}, u32[]{:S(2)}, u32[]{:S(2)}) collective-permute-start(bf16[128,3712]{1,0:T(8,128)(2,1)} %collective-permute-done.1), channel_id=1, source_target_pairs={{1,0},{2,3},{5,4},{6,7},{9,8},{10,11},{13,12},{14,15},{17,16},{18,... | collective-permute-start | bytes 2850824 | tf_op jit(solution)/shard_map/end_a/ppermute | solution.py:249
  29.7 37.2 %collective-permute-start.9 = (bf16[128,3712]{1,0:T(8,128)(2,1)}, bf16[128,3712]{1,0:T(8,128)(2,1)S(1)}, u32[]{:S(2)}, u32[]{:S(2)}) collective-permute-start(bf16[128,3712]{1,0:T(8,128)(2,1)} %collective-permute-done.3.refs_0_.refs_1_), channel_id=1, source_target_pairs={{1,2},{2,1},{5,6},{6,5},{9,10},{10,9},{13,14},{14,13},{17,18},{18,... | collective-permute-start | bytes 2850824 | tf_op jit(solution)/shard_map/mid_b/ppermute | solution.py:249
  30.4 36.5 %collective-permute-start.4 = (bf16[128,3712]{1,0:T(8,128)(2,1)}, bf16[128,3712]{1,0:T(8,128)(2,1)S(1)}, u32[]{:S(2)}, u32[]{:S(2)}) collective-permute-start(bf16[128,3712]{1,0:T(8,128)(2,1)} %collective-permute-done.3.refs_0_.refs_1_), channel_id=1, source_target_pairs={{0,8},{1,9},{2,10},{3,11},{4,12},{5,13},{6,14},{7,15},{8,0},{9,1},... | collective-permute-start | bytes 2850824 | tf_op jit(solution)/shard_map/x_pair/ppermute | solution.py:249
  32.0 34.9 %collective-permute-start.5 = (bf16[4,4,72,256]{3,2,1,0:T(8,128)(2,1)S(1)}, bf16[4,4,72,256]{3,2,1,0:T(8,128)(2,1)S(1)}, u32[]{:S(2)}, u32[]{:S(2)}) collective-permute-start(bf16[4,4,72,256]{3,2,1,0:T(8,128)(2,1)S(1)} %get-tuple-element.49), channel_id=1, source_target_pairs={{0,1},{1,0},{2,3},{3,2},{4,5},{5,4},{6,7},{7,6},{8,9},{9,8},{10,11... | collective-permute-start | bytes 1769480 | tf_op jit(solution)/shard_map/g_near/ppermute | solution.py:249
  38.5 28.4 %collective-permute-start.6 = (bf16[4,4,72,256]{3,2,1,0:T(8,128)(2,1)S(1)}, bf16[4,4,72,256]{3,2,1,0:T(8,128)(2,1)S(1)}, u32[]{:S(2)}, u32[]{:S(2)}) collective-permute-start(bf16[4,4,72,256]{3,2,1,0:T(8,128)(2,1)S(1)} %get-tuple-element.75), channel_id=1, source_target_pairs={{1,2},{2,1},{5,6},{6,5},{9,10},{10,9},{13,14},{14,13},{17,18},{18,... | collective-permute-start | bytes 1769480 | tf_op jit(solution)/shard_map/g_inner/ppermute | solution.py:249
  56.3 10.5 %collective-permute-start.7 = (bf16[128,3712]{1,0:T(8,128)(2,1)}, bf16[128,3712]{1,0:T(8,128)(2,1)S(1)}, u32[]{:S(2)}, u32[]{:S(2)}) collective-permute-start(bf16[128,3712]{1,0:T(8,128)(2,1)} %collective-permute-done.2.refs_2_.refs_3_), channel_id=1, source_target_pairs={{0,4},{1,5},{2,6},{3,7},{4,0},{5,1},{6,2},{7,3},{8,12},{9,13},{10,... | collective-permute-start | bytes 2850824 | tf_op jit(solution)/shard_map/c_xown/ppermute | solution.py:249
  66.9 21.0 %collective-permute-start.11 = (bf16[128,3712]{1,0:T(8,128)(2,1)S(1)}, bf16[128,3712]{1,0:T(8,128)(2,1)S(1)}, u32[]{:S(2)}, u32[]{:S(2)}) collective-permute-start(bf16[128,3712]{1,0:T(8,128)(2,1)S(1)} %broadcast_select_fusion.1.refs_0_.refs_1_), channel_id=1, source_target_pairs={{0,8},{1,9},{2,10},{3,11},{4,12},{5,13},{6,14},{7,15},{8,0},{9,1},... | collective-permute-start | bytes 2850824 | tf_op jit(solution)/shard_map/x_far_a/ppermute | solution.py:249
  67.5 23.6 %collective-permute-start.10 = (bf16[128,3712]{1,0:T(8,128)(2,1)S(1)}, bf16[128,3712]{1,0:T(8,128)(2,1)S(1)}, u32[]{:S(2)}, u32[]{:S(2)}) collective-permute-start(bf16[128,3712]{1,0:T(8,128)(2,1)S(1)} %collective-permute-done.9), channel_id=1, source_target_pairs={{1,0},{2,3},{5,4},{6,7},{9,8},{10,11},{13,12},{14,15},{17,16},{18,... | collective-permute-start | bytes 2850824 | tf_op jit(solution)/shard_map/end_b/ppermute | solution.py:249
  68.8 22.5 %collective-permute-start.12 = (bf16[4,4,72,256]{3,2,1,0:T(8,128)(2,1)S(1)}, bf16[4,4,72,256]{3,2,1,0:T(8,128)(2,1)S(1)}, u32[]{:S(2)}, u32[]{:S(2)}) collective-permute-start(bf16[4,4,72,256]{3,2,1,0:T(8,128)(2,1)S(1)} %get-tuple-element.66), channel_id=1, source_target_pairs={{0,2},{3,1},{4,6},{7,5},{8,10},{11,9},{12,14},{15,13},{16,18},{19,... | collective-permute-start | bytes 1769480 | tf_op jit(solution)/shard_map/g_out/ppermute | solution.py:249
  75.4 15.9 %collective-permute-start.13 = (bf16[128,3712]{1,0:T(8,128)(2,1)S(1)}, bf16[128,3712]{1,0:T(8,128)(2,1)S(1)}, u32[]{:S(2)}, u32[]{:S(2)}) collective-permute-start(bf16[128,3712]{1,0:T(8,128)(2,1)S(1)} %collective-permute-done.4.refs_2_.refs_3_), channel_id=1, source_target_pairs={{0,4},{1,5},{2,6},{3,7},{4,0},{5,1},{6,2},{7,3},{8,12},{9,13},{10,... | collective-permute-start | bytes 2850824 | tf_op jit(solution)/shard_map/c_xpair/ppermute | solution.py:249
  75.5 15.8 %collective-permute-start.14 = (bf16[128,3712]{1,0:T(8,128)(2,1)}, bf16[128,3712]{1,0:T(8,128)(2,1)S(1)}, u32[]{:S(2)}, u32[]{:S(2)}) collective-permute-start(bf16[128,3712]{1,0:T(8,128)(2,1)} %collective-permute-done.3.refs_0_.refs_1_), channel_id=1, source_target_pairs={{0,4},{1,5},{2,6},{3,7},{4,0},{5,1},{6,2},{7,3},{8,12},{9,13},{10,... | collective-permute-start | bytes 2850824 | tf_op jit(solution)/shard_map/c_pair/ppermute | solution.py:249
  76.0 1.2 copy-start.1
  91.3 14.8 %collective-permute-start.15 = (bf16[4,4,72,256]{3,2,1,0:T(8,128)(2,1)S(1)}, bf16[4,4,72,256]{3,2,1,0:T(8,128)(2,1)S(1)}, u32[]{:S(2)}, u32[]{:S(2)}) collective-permute-start(bf16[4,4,72,256]{3,2,1,0:T(8,128)(2,1)S(1)} %get-tuple-element.66), channel_id=1, source_target_pairs={{2,0},{1,3},{6,4},{5,7},{10,8},{9,11},{14,12},{13,15},{18,16},{17,... | collective-permute-start | bytes 1769480 | tf_op jit(solution)/shard_map/g_in/ppermute | solution.py:249
  92.6 25.5 %collective-permute-start.17 = (bf16[128,3712]{1,0:T(8,128)(2,1)S(1)}, bf16[128,3712]{1,0:T(8,128)(2,1)S(1)}, u32[]{:S(2)}, u32[]{:S(2)}) collective-permute-start(bf16[128,3712]{1,0:T(8,128)(2,1)S(1)} %broadcast_select_fusion.refs_0_.refs_1_), channel_id=1, source_target_pairs={{0,8},{1,9},{2,10},{3,11},{4,12},{5,13},{6,14},{7,15},{8,0},{9,1},... | collective-permute-start | bytes 2850824 | tf_op jit(solution)/shard_map/x_far_b/ppermute | solution.py:249
  94.1 15.6 %collective-permute-start.20 = (bf16[128,3712]{1,0:T(8,128)(2,1)S(1)}, bf16[128,3712]{1,0:T(8,128)(2,1)S(1)}, u32[]{:S(2)}, u32[]{:S(2)}) collective-permute-start(bf16[128,3712]{1,0:T(8,128)(2,1)S(1)} %collective-permute-done.11.refs_3_), channel_id=1, source_target_pairs={{0,4},{1,5},{2,6},{3,7},{4,0},{5,1},{6,2},{7,3},{8,12},{9,13},{10,... | collective-permute-start | bytes 2850824 | tf_op jit(solution)/shard_map/c_xfar_a/ppermute | solution.py:249
  94.1 15.6 %collective-permute-start.19 = (bf16[128,3712]{1,0:T(8,128)(2,1)S(1)}, bf16[128,3712]{1,0:T(8,128)(2,1)S(1)}, u32[]{:S(2)}, u32[]{:S(2)}) collective-permute-start(bf16[128,3712]{1,0:T(8,128)(2,1)S(1)} %broadcast_select_fusion.1.refs_0_.refs_1_), channel_id=1, source_target_pairs={{0,4},{1,5},{2,6},{3,7},{4,0},{5,1},{6,2},{7,3},{8,12},{9,13},{10,... | collective-permute-start | bytes 2850824 | tf_op jit(solution)/shard_map/c_far_a/ppermute | solution.py:249
  106.1 19.4 %collective-permute-start.18 = (bf16[128,3712]{1,0:T(8,128)(2,1)S(1)}, bf16[128,3712]{1,0:T(8,128)(2,1)S(1)}, u32[]{:S(2)}, u32[]{:S(2)}) collective-permute-start(bf16[128,3712]{1,0:T(8,128)(2,1)S(1)} %broadcast_select_fusion.refs_0_.refs_1_), channel_id=1, source_target_pairs={{0,4},{1,5},{2,6},{3,7},{4,0},{5,1},{6,2},{7,3},{8,12},{9,13},{10,... | collective-permute-start | bytes 2850824 | tf_op jit(solution)/shard_map/c_far_b/ppermute | solution.py:249
  106.1 19.4 %collective-permute-start.16 = (bf16[4,4,72,256]{3,2,1,0:T(8,128)(2,1)S(1)}, bf16[4,4,72,256]{3,2,1,0:T(8,128)(2,1)S(1)}, u32[]{:S(2)}, u32[]{:S(2)}) collective-permute-start(bf16[4,4,72,256]{3,2,1,0:T(8,128)(2,1)S(1)} %get-tuple-element.75), channel_id=1, source_target_pairs={{0,3},{3,0},{4,7},{7,4},{8,11},{11,8},{12,15},{15,12},{16,19},{19,... | collective-permute-start | bytes 1769480 | tf_op jit(solution)/shard_map/g_outer/ppermute | solution.py:249
  125.5 2.5 %collective-permute-start.21 = (bf16[128,3712]{1,0:T(8,128)(2,1)S(1)}, bf16[128,3712]{1,0:T(8,128)(2,1)S(1)}, u32[]{:S(2)}, u32[]{:S(2)}) collective-permute-start(bf16[128,3712]{1,0:T(8,128)(2,1)S(1)} %collective-permute-done.17.refs_2_.refs_3_), channel_id=1, source_target_pairs={{0,4},{1,5},{2,6},{3,7},{4,0},{5,1},{6,2},{7,3},{8,12},{9,13},{10,... | collective-permute-start | bytes 2850824 | tf_op jit(solution)/shard_map/c_xfar_b/ppermute | solution.py:249

commit v5 on v4

--- a/solution.py
+++ b/solution.py
@@ -315,12 +315,15 @@
     g_outer = send("g_outer", h_flip, same, outer)
     c_far_b = send("c_far_b", far_b, core, stay)
     s_a = spread_far(where, g_in, g_inner, [far_a, c_far_a, l_xfar_a, c_xfar_a])
-    acc = product([s_a], [far_a, c_far_a, x_far_a, c_xfar_a], width, acc)
-    g_outer, x_far_b, c_far_b, acc, far_b = tie(
-        (g_outer, x_far_b, c_far_b, acc, far_b)
-    )
-
+    x_far_b, acc = tie(
+        (x_far_b, acc)
+    )
     c_xfar_b = send("c_xfar_b", x_far_b, core, stay)
+    acc = product([s_a], [far_a, c_far_a, x_far_a, c_xfar_a], width, acc, cost=4)
+    g_outer, c_xfar_b, c_far_b, acc, far_b = tie(
+        (g_outer, c_xfar_b, c_far_b, acc, far_b)
+    )
+
     rows_b = [far_b, c_far_b, x_far_b, c_xfar_b]
     s_b = spread_far(where, g_outer, g_out, rows_b)
     return product([s_b], rows_b, width, acc, last=True, experts=per_device)

time: 139 us -> 134 us (0.964)
  waiting for transfers between devices: 62.5 us -> 57.3 us
    ppermute x22, waiting for transfers between devices: 62.5 us -> 57.3 us  [send(): return lax.ppermute(array, both, pairs)]
  transfers between devices with their start and end apart: 22 -> 22, of which waited for: 9 -> 9; matrix products, arithmetic and copies ran while one was open for 1% -> 1% of each run, Pallas kernels for 19% -> 20%
where the time goes in v5:
time: 134 us; the launch traced here: 133 us
  waiting for transfers between devices  57.3 us (43%)
  Pallas kernels  39.5 us (29%)
  starting transfers between devices  33 us (25%)
  local copies, waits for them, and re-layouts  2.76 us (2%)
    ppermute x22, waiting for transfers between devices, send(): return lax.ppermute(array, both, pairs)  57.3 us
    ppermute x22, starting transfers between devices, send(): return lax.ppermute(array, both, pairs)  33 us
    pallas_call x4, Pallas kernels, product(): pl.pallas_call(body, grid=(width // tile,), in_specs=in_specs, out_specs=...  30.3 us
    pallas_call x4, Pallas kernels, spread_call(): pl.pallas_call(body, grid_spec=pltpu.PrefetchScalarGridSpec(num_scalar_pr...  6.63 us
  transfers between devices with their start and end apart: 22, of which 9 were waited for; matrix products, arithmetic and copies ran while one was open for 1% of the time, Pallas kernels for 20%

profile of v5, /device:TPU:0, one launch (start us, length us, event | category | flops | bytes accessed | tf_op | source)
XLA Modules:
  0.0 133.0 jit_solution(1039506109067258999)
XLA Ops:
  0.0 2.5 %shard_map.55.refs_0_.refs_1_ = bf16[128,3712]{1,0:T(8,128)(2,1)} custom-call(bf16[128,3584]{1,0:T(8,128)(2,1)} %rows_ref.1, f32[1,128]{1,0:T(1,128)} %bitcast.16, f32[8,128]{1,0:T(8,128)} %bitcast.14, s32[8,128]{1,0:T(8,128)} %bitcast.15), custom_call_target="tpu_custom_call" | custom-call | tf_op jit(solution)/shard_map/pallas_call | solution.py:87
  2.5 3.0 %collective-permute-start.3 = (bf16[128,3712]{1,0:T(8,128)(2,1)}, bf16[128,3712]{1,0:T(8,128)(2,1)}, u32[]{:S(2)}, u32[]{:S(2)}) collective-permute-start(bf16[128,3712]{1,0:T(8,128)(2,1)} %shard_map.55.refs_0_.refs_1_), channel_id=1, source_target_pairs={{0,1},{1,0},{2,3},{3,2},{4,5},{5,4},{6,7},{7,6},{8,9},{9,8},{10,11... | collective-permute-start | bytes 2850824 | tf_op jit(solution)/shard_map/pair/ppermute | solution.py:249
  5.6 1.5 %collective-permute-start.2 = (bf16[128,3712]{1,0:T(8,128)(2,1)}, bf16[128,3712]{1,0:T(8,128)(2,1)}, u32[]{:S(2)}, u32[]{:S(2)}) collective-permute-start(bf16[128,3712]{1,0:T(8,128)(2,1)} %shard_map.55.refs_0_.refs_1_), channel_id=1, source_target_pairs={{0,8},{1,9},{2,10},{3,11},{4,12},{5,13},{6,14},{7,15},{8,0},{9,1},... | collective-permute-start | bytes 2850824 | tf_op jit(solution)/shard_map/x_own/ppermute | solution.py:249
  7.0 1.6 %collective-permute-start.1 = (bf16[128,3712]{1,0:T(8,128)(2,1)}, bf16[128,3712]{1,0:T(8,128)(2,1)}, u32[]{:S(2)}, u32[]{:S(2)}) collective-permute-start(bf16[128,3712]{1,0:T(8,128)(2,1)} %shard_map.55.refs_0_.refs_1_), channel_id=1, source_target_pairs={{1,2},{2,1},{5,6},{6,5},{9,10},{10,9},{13,14},{14,13},{17,18},{18,... | collective-permute-start | bytes 2850824 | tf_op jit(solution)/shard_map/mid_a/ppermute | solution.py:249
  8.7 1.6 %dynamic-slice_bitcast_fusion = (bf16[4,4,72,256]{3,2,1,0:T(8,128)(2,1)S(1)}, bf16[4,4,72,256]{3,2,1,0:T(8,128)(2,1)S(1)}, bf16[4,4,72,256]{3,2,1,0:T(8,128)(2,1)S(1)}) fusion(bf16[1,4,4,72,1024]{4,3,2,1,0:T(8,128)(2,1)} %param.9, s32[]{:T(128)S(6)} %select_n.28, s32[]{:T(128)S(6)} %select_n.27, s32[]{:T(128)S(6)} %select_n.26), kind=kLoop, calls=%fused_computation.2 | loop fusion | bytes 3538956 | tf_op jit(solution)/shard_map/dynamic_slice | solution.py:264
  10.3 16.7 %collective-permute-done.3.refs_0_.refs_1_ = bf16[128,3712]{1,0:T(8,128)(2,1)} collective-permute-done((bf16[128,3712]{1,0:T(8,128)(2,1)}, bf16[128,3712]{1,0:T(8,128)(2,1)}, u32[]{:S(2)}, u32[]{:S(2)}) %collective-permute-start.3) | collective-permute-done | bytes 950304 | tf_op jit(solution)/shard_map/pair/ppermute | solution.py:249
  27.0 1.4 %collective-permute-done.2.refs_2_.refs_3_ = bf16[128,3712]{1,0:T(8,128)(2,1)} collective-permute-done((bf16[128,3712]{1,0:T(8,128)(2,1)}, bf16[128,3712]{1,0:T(8,128)(2,1)}, u32[]{:S(2)}, u32[]{:S(2)}) %collective-permute-start.2) | collective-permute-done | bytes 950304 | tf_op jit(solution)/shard_map/x_own/ppermute | solution.py:249
  28.4 1.3 collective-permute-start.8
  29.7 0.7 collective-permute-start.9
  30.4 1.6 %collective-permute-start.4 = (bf16[128,3712]{1,0:T(8,128)(2,1)}, bf16[128,3712]{1,0:T(8,128)(2,1)S(1)}, u32[]{:S(2)}, u32[]{:S(2)}) collective-permute-start(bf16[128,3712]{1,0:T(8,128)(2,1)} %collective-permute-done.3.refs_0_.refs_1_), channel_id=1, source_target_pairs={{0,8},{1,9},{2,10},{3,11},{4,12},{5,13},{6,14},{7,15},{8,0},{9,1},... | collective-permute-start | bytes 2850824 | tf_op jit(solution)/shard_map/x_pair/ppermute | solution.py:249
  32.0 6.5 %collective-permute-start.5 = (bf16[4,4,72,256]{3,2,1,0:T(8,128)(2,1)S(1)}, bf16[4,4,72,256]{3,2,1,0:T(8,128)(2,1)S(1)}, u32[]{:S(2)}, u32[]{:S(2)}) collective-permute-start(bf16[4,4,72,256]{3,2,1,0:T(8,128)(2,1)S(1)} %get-tuple-element.51), channel_id=1, source_target_pairs={{0,1},{1,0},{2,3},{3,2},{4,5},{5,4},{6,7},{7,6},{8,9},{9,8},{10,11... | collective-permute-start | bytes 1769480 | tf_op jit(solution)/shard_map/g_near/ppermute | solution.py:249
  39.2 17.2 %collective-permute-done.8 = bf16[128,3712]{1,0:T(8,128)(2,1)S(1)} collective-permute-done((bf16[128,3712]{1,0:T(8,128)(2,1)}, bf16[128,3712]{1,0:T(8,128)(2,1)S(1)}, u32[]{:S(2)}, u32[]{:S(2)}) %collective-permute-start.8) | collective-permute-done | bytes 950304 | tf_op jit(solution)/shard_map/end_a/ppermute | solution.py:249
  56.5 10.4 %collective-permute-done.5.hidden_ref = bf16[4,4,72,256]{3,2,1,0:T(8,128)(2,1)S(1)} collective-permute-done((bf16[4,4,72,256]{3,2,1,0:T(8,128)(2,1)S(1)}, bf16[4,4,72,256]{3,2,1,0:T(8,128)(2,1)S(1)}, u32[]{:S(2)}, u32[]{:S(2)}) %collective-permute-start.5) | collective-permute-done | bytes 589856 | tf_op jit(solution)/shard_map/g_near/ppermute | solution.py:249
  67.5 1.3 collective-permute-start.10
  68.8 6.6 %collective-permute-start.12 = (bf16[4,4,72,256]{3,2,1,0:T(8,128)(2,1)S(1)}, bf16[4,4,72,256]{3,2,1,0:T(8,128)(2,1)S(1)}, u32[]{:S(2)}, u32[]{:S(2)}) collective-permute-start(bf16[4,4,72,256]{3,2,1,0:T(8,128)(2,1)S(1)} %get-tuple-element.68), channel_id=1, source_target_pairs={{0,2},{3,1},{4,6},{7,5},{8,10},{11,9},{12,14},{15,13},{16,18},{19,... | collective-permute-start | bytes 1769480 | tf_op jit(solution)/shard_map/g_out/ppermute | solution.py:249
  76.0 1.2 copy-done.1
  77.1 2.1 %shard_map.56.refs_0_ = bf16[1024,512]{1,0:T(8,128)(2,1)S(1)} custom-call(s32[3]{0:T(128)S(1)} %pad_add_fusion.where_ref, bf16[4,4,72,1024]{3,2,1,0:T(8,128)(2,1)S(1)} %bitcast.13, bf16[128,3712]{1,0:T(8,128)(2,1)S(1)} %copy-done.1, bf16[128,3712]{1,0:T(8,128)(2,1)} %collective-permute-done.refs_1_.refs_2_, ...), custom_call_target="tpu_custom_call" | custom-call | flops 150994944 | bytes 3407872 | tf_op jit(solution)/shard_map/pallas_call | solution.py:127
  79.2 7.2 %shard_map.57.refs_5_ = bf16[1024,3584]{1,0:T(8,128)(2,1)S(1)} custom-call(bf16[1024,512]{1,0:T(8,128)(2,1)S(1)} %shard_map.56.refs_0_, bf16[128,3712]{1,0:T(8,128)(2,1)S(1)} %copy-done.2, bf16[128,3712]{1,0:T(8,128)(2,1)} %collective-permute-done.refs_1_.refs_2_, bf16[128,3712]{1,0:T(8,128)(2,1)} %collective-permute-done.2.refs_2_.refs_3_, ...), custom_call_target="tpu_custom_call" | custom-call | flops 3758096384 | bytes 18350080 | tf_op jit(solution)/shard_map/pallas_call | solution.py:214
  86.4 1.5 %collective-permute-done.11.refs_3_ = bf16[128,3712]{1,0:T(8,128)(2,1)S(1)} collective-permute-done((bf16[128,3712]{1,0:T(8,128)(2,1)S(1)}, bf16[128,3712]{1,0:T(8,128)(2,1)S(1)}, u32[]{:S(2)}, u32[]{:S(2)}) %collective-permute-start.11) | collective-permute-done | bytes 950304 | tf_op jit(solution)/shard_map/x_far_a/ppermute | solution.py:249
  87.9 3.2 %collective-permute-done.10 = bf16[128,3712]{1,0:T(8,128)(2,1)S(1)} collective-permute-done((bf16[128,3712]{1,0:T(8,128)(2,1)S(1)}, bf16[128,3712]{1,0:T(8,128)(2,1)S(1)}, u32[]{:S(2)}, u32[]{:S(2)}) %collective-permute-start.10) | collective-permute-done | bytes 950304 | tf_op jit(solution)/shard_map/end_b/ppermute | solution.py:249
  91.3 1.3 collective-permute-start.15
  92.6 1.6 %collective-permute-start.17 = (bf16[128,3712]{1,0:T(8,128)(2,1)S(1)}, bf16[128,3712]{1,0:T(8,128)(2,1)S(1)}, u32[]{:S(2)}, u32[]{:S(2)}) collective-permute-start(bf16[128,3712]{1,0:T(8,128)(2,1)S(1)} %broadcast_select_fusion.refs_0_.refs_1_), channel_id=1, source_target_pairs={{0,8},{1,9},{2,10},{3,11},{4,12},{5,13},{6,14},{7,15},{8,0},{9,1},... | collective-permute-start | bytes 2850824 | tf_op jit(solution)/shard_map/x_far_b/ppermute | solution.py:249
  94.6 2.0 %shard_map.58.refs_0_ = bf16[1024,512]{1,0:T(8,128)(2,1)S(1)} custom-call(s32[3]{0:T(128)S(1)} %pad_add_fusion.where_ref, bf16[4,4,72,256]{3,2,1,0:T(8,128)(2,1)S(1)} %collective-permute-done.5.hidden_ref, bf16[128,3712]{1,0:T(8,128)(2,1)} %collective-permute-done.3.refs_0_.refs_1_, bf16[128,3712]{1,0:T(8,128)(2,1)S(1)} %collective-permute-done.14.refs_1_.refs_2_, ...), custom_call_target="tpu_custom_call" | custom-call | flops 150994944 | bytes 1638400 | tf_op jit(solution)/shard_map/pallas_call | solution.py:127
  96.6 7.3 %shard_map.59.refs_5_ = bf16[1024,3584]{1,0:T(8,128)(2,1)S(1)} custom-call(bf16[1024,512]{1,0:T(8,128)(2,1)S(1)} %shard_map.58.refs_0_, bf16[128,3712]{1,0:T(8,128)(2,1)} %collective-permute-done.3.refs_0_.refs_1_, bf16[128,3712]{1,0:T(8,128)(2,1)S(1)} %collective-permute-done.14.refs_1_.refs_2_, ...), custom_call_target="tpu_custom_call" | custom-call | flops 15032385536 | bytes 73400320 | tf_op jit(solution)/shard_map/pallas_call | solution.py:214
  104.0 2.1 %collective-permute-done.15.ends_ref = bf16[4,4,72,256]{3,2,1,0:T(8,128)(2,1)S(1)} collective-permute-done((bf16[4,4,72,256]{3,2,1,0:T(8,128)(2,1)S(1)}, bf16[4,4,72,256]{3,2,1,0:T(8,128)(2,1)S(1)}, u32[]{:S(2)}, u32[]{:S(2)}) %collective-permute-start.15) | collective-permute-done | bytes 589856 | tf_op jit(solution)/shard_map/g_in/ppermute | solution.py:249
  106.1 3.6 %collective-permute-start.16 = (bf16[4,4,72,256]{3,2,1,0:T(8,128)(2,1)S(1)}, bf16[4,4,72,256]{3,2,1,0:T(8,128)(2,1)S(1)}, u32[]{:S(2)}, u32[]{:S(2)}) collective-permute-start(bf16[4,4,72,256]{3,2,1,0:T(8,128)(2,1)S(1)} %get-tuple-element.77), channel_id=1, source_target_pairs={{0,3},{3,0},{4,7},{7,4},{8,11},{11,8},{12,15},{15,12},{16,19},{19,... | collective-permute-start | bytes 1769480 | tf_op jit(solution)/shard_map/g_outer/ppermute | solution.py:249
  109.8 2.6 %collective-permute-done.17.refs_2_.refs_3_ = bf16[128,3712]{1,0:T(8,128)(2,1)S(1)} collective-permute-done((bf16[128,3712]{1,0:T(8,128)(2,1)S(1)}, bf16[128,3712]{1,0:T(8,128)(2,1)S(1)}, u32[]{:S(2)}, u32[]{:S(2)}) %collective-permute-start.17) | collective-permute-done | bytes 950304 | tf_op jit(solution)/shard_map/x_far_b/ppermute | solution.py:249
  112.4 1.3 shard_map.60.refs_0_
  113.7 7.0 %shard_map.61.refs_5_ = bf16[1024,3584]{1,0:T(8,128)(2,1)S(1)} custom-call(bf16[1024,512]{1,0:T(8,128)(2,1)S(1)} %shard_map.60.refs_0_, bf16[128,3712]{1,0:T(8,128)(2,1)S(1)} %broadcast_select_fusion.1.refs_0_.refs_1_, bf16[128,3712]{1,0:T(8,128)(2,1)S(1)} %collective-permute-done.20.refs_1_.refs_2_, bf16[128,3712]{1,0:T(8,128)(2,1)S(1)} %collective-permute-done.11.refs_3_, ...), custom_call_target="tpu_custom_call" | custom-call | flops 15032385536 | bytes 73400320 | tf_op jit(solution)/shard_map/pallas_call | solution.py:214
  120.7 2.2 %collective-permute-done.16.ends_ref = bf16[4,4,72,256]{3,2,1,0:T(8,128)(2,1)S(1)} collective-permute-done((bf16[4,4,72,256]{3,2,1,0:T(8,128)(2,1)S(1)}, bf16[4,4,72,256]{3,2,1,0:T(8,128)(2,1)S(1)}, u32[]{:S(2)}, u32[]{:S(2)}) %collective-permute-start.16) | collective-permute-done | bytes 589856 | tf_op jit(solution)/shard_map/g_outer/ppermute | solution.py:249
  122.9 1.3 shard_map.62.refs_0_
  124.2 8.8 %shard_map.63 = bf16[256,4,3584]{2,1,0:T(4,128)(2,1)} custom-call(bf16[1024,512]{1,0:T(8,128)(2,1)S(1)} %shard_map.62.refs_0_, bf16[128,3712]{1,0:T(8,128)(2,1)S(1)} %broadcast_select_fusion.refs_0_.refs_1_, bf16[128,3712]{1,0:T(8,128)(2,1)S(1)} %collective-permute-done.19.refs_1_.refs_2_, bf16[128,3712]{1,0:T(8,128)(2,1)S(1)} %collective-permute-done.17.refs_2_.refs_3_, ...), custom_call_target="tpu_custom_call" | custom-call | flops 3758096384 | bytes 18350080 | tf_op jit(solution)/shard_map/pallas_call | solution.py:214
  (32 shorter events, 2.8 us)
Async XLA Ops:
  0.0 76.0 %copy-start = (bf16[1,4,4,72,1024]{4,3,2,1,0:T(8,128)(2,1)S(1)}, bf16[1,4,4,72,1024]{4,3,2,1,0:T(8,128)(2,1)}, u32[]{:S(2)}) copy-start(bf16[1,4,4,72,1024]{4,3,2,1,0:T(8,128)(2,1)} %param.9) | copy-start | bytes 7077892
  2.5 76.7 %copy-start.2 = (bf16[128,3712]{1,0:T(8,128)(2,1)S(1)}, bf16[128,3712]{1,0:T(8,128)(2,1)}, u32[]{:S(2)}) copy-start(bf16[128,3712]{1,0:T(8,128)(2,1)} %shard_map.55.refs_0_.refs_1_) | copy-start | bytes 2850820
  2.5 24.5 %collective-permute-start.3 = (bf16[128,3712]{1,0:T(8,128)(2,1)}, bf16[128,3712]{1,0:T(8,128)(2,1)}, u32[]{:S(2)}, u32[]{:S(2)}) collective-permute-start(bf16[128,3712]{1,0:T(8,128)(2,1)} %shard_map.55.refs_0_.refs_1_), channel_id=1, source_target_pairs={{0,1},{1,0},{2,3},{3,2},{4,5},{5,4},{6,7},{7,6},{8,9},{9,8},{10,11... | collective-permute-start | bytes 2850824 | tf_op jit(solution)/shard_map/pair/ppermute | solution.py:249
  5.6 22.8 %collective-permute-start.2 = (bf16[128,3712]{1,0:T(8,128)(2,1)}, bf16[128,3712]{1,0:T(8,128)(2,1)}, u32[]{:S(2)}, u32[]{:S(2)}) collective-permute-start(bf16[128,3712]{1,0:T(8,128)(2,1)} %shard_map.55.refs_0_.refs_1_), channel_id=1, source_target_pairs={{0,8},{1,9},{2,10},{3,11},{4,12},{5,13},{6,14},{7,15},{8,0},{9,1},... | collective-permute-start | bytes 2850824 | tf_op jit(solution)/shard_map/x_own/ppermute | solution.py:249
  7.0 21.3 %collective-permute-start.1 = (bf16[128,3712]{1,0:T(8,128)(2,1)}, bf16[128,3712]{1,0:T(8,128)(2,1)}, u32[]{:S(2)}, u32[]{:S(2)}) collective-permute-start(bf16[128,3712]{1,0:T(8,128)(2,1)} %shard_map.55.refs_0_.refs_1_), channel_id=1, source_target_pairs={{1,2},{2,1},{5,6},{6,5},{9,10},{10,9},{13,14},{14,13},{17,18},{18,... | collective-permute-start | bytes 2850824 | tf_op jit(solution)/shard_map/mid_a/ppermute | solution.py:249
  8.7 19.7 %collective-permute-start = (bf16[128,3712]{1,0:T(8,128)(2,1)}, bf16[128,3712]{1,0:T(8,128)(2,1)}, u32[]{:S(2)}, u32[]{:S(2)}) collective-permute-start(bf16[128,3712]{1,0:T(8,128)(2,1)} %shard_map.55.refs_0_.refs_1_), channel_id=1, source_target_pairs={{0,4},{1,5},{2,6},{3,7},{4,0},{5,1},{6,2},{7,3},{8,12},{9,13},{10,... | collective-permute-start | bytes 2850824 | tf_op jit(solution)/shard_map/c_own/ppermute | solution.py:249
  28.4 28.0 %collective-permute-start.8 = (bf16[128,3712]{1,0:T(8,128)(2,1)}, bf16[128,3712]{1,0:T(8,128)(2,1)S(1)}, u32[]{:S(2)}, u32[]{:S(2)}) collective-permute-start(bf16[128,3712]{1,0:T(8,128)(2,1)} %collective-permute-done.1), channel_id=1, source_target_pairs={{1,0},{2,3},{5,4},{6,7},{9,8},{10,11},{13,12},{14,15},{17,16},{18,... | collective-permute-start | bytes 2850824 | tf_op jit(solution)/shard_map/end_a/ppermute | solution.py:249
  29.7 37.2 %collective-permute-start.9 = (bf16[128,3712]{1,0:T(8,128)(2,1)}, bf16[128,3712]{1,0:T(8,128)(2,1)S(1)}, u32[]{:S(2)}, u32[]{:S(2)}) collective-permute-start(bf16[128,3712]{1,0:T(8,128)(2,1)} %collective-permute-done.3.refs_0_.refs_1_), channel_id=1, source_target_pairs={{1,2},{2,1},{5,6},{6,5},{9,10},{10,9},{13,14},{14,13},{17,18},{18,... | collective-permute-start | bytes 2850824 | tf_op jit(solution)/shard_map/mid_b/ppermute | solution.py:249
  30.4 36.5 %collective-permute-start.4 = (bf16[128,3712]{1,0:T(8,128)(2,1)}, bf16[128,3712]{1,0:T(8,128)(2,1)S(1)}, u32[]{:S(2)}, u32[]{:S(2)}) collective-permute-start(bf16[128,3712]{1,0:T(8,128)(2,1)} %collective-permute-done.3.refs_0_.refs_1_), channel_id=1, source_target_pairs={{0,8},{1,9},{2,10},{3,11},{4,12},{5,13},{6,14},{7,15},{8,0},{9,1},... | collective-permute-start | bytes 2850824 | tf_op jit(solution)/shard_map/x_pair/ppermute | solution.py:249
  32.0 34.9 %collective-permute-start.5 = (bf16[4,4,72,256]{3,2,1,0:T(8,128)(2,1)S(1)}, bf16[4,4,72,256]{3,2,1,0:T(8,128)(2,1)S(1)}, u32[]{:S(2)}, u32[]{:S(2)}) collective-permute-start(bf16[4,4,72,256]{3,2,1,0:T(8,128)(2,1)S(1)} %get-tuple-element.51), channel_id=1, source_target_pairs={{0,1},{1,0},{2,3},{3,2},{4,5},{5,4},{6,7},{7,6},{8,9},{9,8},{10,11... | collective-permute-start | bytes 1769480 | tf_op jit(solution)/shard_map/g_near/ppermute | solution.py:249
  38.5 28.4 %collective-permute-start.6 = (bf16[4,4,72,256]{3,2,1,0:T(8,128)(2,1)S(1)}, bf16[4,4,72,256]{3,2,1,0:T(8,128)(2,1)S(1)}, u32[]{:S(2)}, u32[]{:S(2)}) collective-permute-start(bf16[4,4,72,256]{3,2,1,0:T(8,128)(2,1)S(1)} %get-tuple-element.77), channel_id=1, source_target_pairs={{1,2},{2,1},{5,6},{6,5},{9,10},{10,9},{13,14},{14,13},{17,18},{18,... | collective-permute-start | bytes 1769480 | tf_op jit(solution)/shard_map/g_inner/ppermute | solution.py:249
  56.3 10.5 %collective-permute-start.7 = (bf16[128,3712]{1,0:T(8,128)(2,1)}, bf16[128,3712]{1,0:T(8,128)(2,1)S(1)}, u32[]{:S(2)}, u32[]{:S(2)}) collective-permute-start(bf16[128,3712]{1,0:T(8,128)(2,1)} %collective-permute-done.2.refs_2_.refs_3_), channel_id=1, source_target_pairs={{0,4},{1,5},{2,6},{3,7},{4,0},{5,1},{6,2},{7,3},{8,12},{9,13},{10,... | collective-permute-start | bytes 2850824 | tf_op jit(solution)/shard_map/c_xown/ppermute | solution.py:249
  66.9 21.0 %collective-permute-start.11 = (bf16[128,3712]{1,0:T(8,128)(2,1)S(1)}, bf16[128,3712]{1,0:T(8,128)(2,1)S(1)}, u32[]{:S(2)}, u32[]{:S(2)}) collective-permute-start(bf16[128,3712]{1,0:T(8,128)(2,1)S(1)} %broadcast_select_fusion.1.refs_0_.refs_1_), channel_id=1, source_target_pairs={{0,8},{1,9},{2,10},{3,11},{4,12},{5,13},{6,14},{7,15},{8,0},{9,1},... | collective-permute-start | bytes 2850824 | tf_op jit(solution)/shard_map/x_far_a/ppermute | solution.py:249
  67.5 23.6 %collective-permute-start.10 = (bf16[128,3712]{1,0:T(8,128)(2,1)S(1)}, bf16[128,3712]{1,0:T(8,128)(2,1)S(1)}, u32[]{:S(2)}, u32[]{:S(2)}) collective-permute-start(bf16[128,3712]{1,0:T(8,128)(2,1)S(1)} %collective-permute-done.9), channel_id=1, source_target_pairs={{1,0},{2,3},{5,4},{6,7},{9,8},{10,11},{13,12},{14,15},{17,16},{18,... | collective-permute-start | bytes 2850824 | tf_op jit(solution)/shard_map/end_b/ppermute | solution.py:249
  68.8 22.5 %collective-permute-start.12 = (bf16[4,4,72,256]{3,2,1,0:T(8,128)(2,1)S(1)}, bf16[4,4,72,256]{3,2,1,0:T(8,128)(2,1)S(1)}, u32[]{:S(2)}, u32[]{:S(2)}) collective-permute-start(bf16[4,4,72,256]{3,2,1,0:T(8,128)(2,1)S(1)} %get-tuple-element.68), channel_id=1, source_target_pairs={{0,2},{3,1},{4,6},{7,5},{8,10},{11,9},{12,14},{15,13},{16,18},{19,... | collective-permute-start | bytes 1769480 | tf_op jit(solution)/shard_map/g_out/ppermute | solution.py:249
  75.4 15.9 %collective-permute-start.13 = (bf16[128,3712]{1,0:T(8,128)(2,1)S(1)}, bf16[128,3712]{1,0:T(8,128)(2,1)S(1)}, u32[]{:S(2)}, u32[]{:S(2)}) collective-permute-start(bf16[128,3712]{1,0:T(8,128)(2,1)S(1)} %collective-permute-done.4.refs_2_.refs_3_), channel_id=1, source_target_pairs={{0,4},{1,5},{2,6},{3,7},{4,0},{5,1},{6,2},{7,3},{8,12},{9,13},{10,... | collective-permute-start | bytes 2850824 | tf_op jit(solution)/shard_map/c_xpair/ppermute | solution.py:249
  75.5 15.8 %collective-permute-start.14 = (bf16[128,3712]{1,0:T(8,128)(2,1)}, bf16[128,3712]{1,0:T(8,128)(2,1)S(1)}, u32[]{:S(2)}, u32[]{:S(2)}) collective-permute-start(bf16[128,3712]{1,0:T(8,128)(2,1)} %collective-permute-done.3.refs_0_.refs_1_), channel_id=1, source_target_pairs={{0,4},{1,5},{2,6},{3,7},{4,0},{5,1},{6,2},{7,3},{8,12},{9,13},{10,... | collective-permute-start | bytes 2850824 | tf_op jit(solution)/shard_map/c_pair/ppermute | solution.py:249
  76.0 1.2 copy-start.1
  91.3 14.8 %collective-permute-start.15 = (bf16[4,4,72,256]{3,2,1,0:T(8,128)(2,1)S(1)}, bf16[4,4,72,256]{3,2,1,0:T(8,128)(2,1)S(1)}, u32[]{:S(2)}, u32[]{:S(2)}) collective-permute-start(bf16[4,4,72,256]{3,2,1,0:T(8,128)(2,1)S(1)} %get-tuple-element.68), channel_id=1, source_target_pairs={{2,0},{1,3},{6,4},{5,7},{10,8},{9,11},{14,12},{13,15},{18,16},{17,... | collective-permute-start | bytes 1769480 | tf_op jit(solution)/shard_map/g_in/ppermute | solution.py:249
  92.6 19.8 %collective-permute-start.17 = (bf16[128,3712]{1,0:T(8,128)(2,1)S(1)}, bf16[128,3712]{1,0:T(8,128)(2,1)S(1)}, u32[]{:S(2)}, u32[]{:S(2)}) collective-permute-start(bf16[128,3712]{1,0:T(8,128)(2,1)S(1)} %broadcast_select_fusion.refs_0_.refs_1_), channel_id=1, source_target_pairs={{0,8},{1,9},{2,10},{3,11},{4,12},{5,13},{6,14},{7,15},{8,0},{9,1},... | collective-permute-start | bytes 2850824 | tf_op jit(solution)/shard_map/x_far_b/ppermute | solution.py:249
  94.1 18.3 %collective-permute-start.21 = (bf16[128,3712]{1,0:T(8,128)(2,1)S(1)}, bf16[128,3712]{1,0:T(8,128)(2,1)S(1)}, u32[]{:S(2)}, u32[]{:S(2)}) collective-permute-start(bf16[128,3712]{1,0:T(8,128)(2,1)S(1)} %collective-permute-done.11.refs_3_), channel_id=1, source_target_pairs={{0,4},{1,5},{2,6},{3,7},{4,0},{5,1},{6,2},{7,3},{8,12},{9,13},{10,... | collective-permute-start | bytes 2850824 | tf_op jit(solution)/shard_map/c_xfar_a/ppermute | solution.py:249
  94.1 18.3 %collective-permute-start.20 = (bf16[128,3712]{1,0:T(8,128)(2,1)S(1)}, bf16[128,3712]{1,0:T(8,128)(2,1)S(1)}, u32[]{:S(2)}, u32[]{:S(2)}) collective-permute-start(bf16[128,3712]{1,0:T(8,128)(2,1)S(1)} %broadcast_select_fusion.1.refs_0_.refs_1_), channel_id=1, source_target_pairs={{0,4},{1,5},{2,6},{3,7},{4,0},{5,1},{6,2},{7,3},{8,12},{9,13},{10,... | collective-permute-start | bytes 2850824 | tf_op jit(solution)/shard_map/c_far_a/ppermute | solution.py:249
  106.1 16.8 %collective-permute-start.16 = (bf16[4,4,72,256]{3,2,1,0:T(8,128)(2,1)S(1)}, bf16[4,4,72,256]{3,2,1,0:T(8,128)(2,1)S(1)}, u32[]{:S(2)}, u32[]{:S(2)}) collective-permute-start(bf16[4,4,72,256]{3,2,1,0:T(8,128)(2,1)S(1)} %get-tuple-element.77), channel_id=1, source_target_pairs={{0,3},{3,0},{4,7},{7,4},{8,11},{11,8},{12,15},{15,12},{16,19},{19,... | collective-permute-start | bytes 1769480 | tf_op jit(solution)/shard_map/g_outer/ppermute | solution.py:249
  109.7 13.2 %collective-permute-start.19 = (bf16[128,3712]{1,0:T(8,128)(2,1)S(1)}, bf16[128,3712]{1,0:T(8,128)(2,1)S(1)}, u32[]{:S(2)}, u32[]{:S(2)}) collective-permute-start(bf16[128,3712]{1,0:T(8,128)(2,1)S(1)} %broadcast_select_fusion.refs_0_.refs_1_), channel_id=1, source_target_pairs={{0,4},{1,5},{2,6},{3,7},{4,0},{5,1},{6,2},{7,3},{8,12},{9,13},{10,... | collective-permute-start | bytes 2850824 | tf_op jit(solution)/shard_map/c_far_b/ppermute | solution.py:249
  112.4 10.5 %collective-permute-start.18 = (bf16[128,3712]{1,0:T(8,128)(2,1)S(1)}, bf16[128,3712]{1,0:T(8,128)(2,1)S(1)}, u32[]{:S(2)}, u32[]{:S(2)}) collective-permute-start(bf16[128,3712]{1,0:T(8,128)(2,1)S(1)} %collective-permute-done.17.refs_2_.refs_3_), channel_id=1, source_target_pairs={{0,4},{1,5},{2,6},{3,7},{4,0},{5,1},{6,2},{7,3},{8,12},{9,13},{10,... | collective-permute-start | bytes 2850824 | tf_op jit(solution)/shard_map/c_xfar_b/ppermute | solution.py:249

commit v6 on v5

--- a/solution.py
+++ b/solution.py
@@ -176,7 +176,7 @@
     return spread_call(body, where, [hidden_ends, hidden_inner], 1, labels, 1)[0]
 
 
-def product(spreads, rows, width, acc=None, last=False, experts=4, tile=512, cost=1):
+def product(spreads, rows, width, acc=None, last=False, experts=4, tile=896, cost=1):
     n_tok = rows[0].shape[0]
     m = spreads[0].shape[0]
     k = sum(s.shape[1] for s in spreads)

time: 134 us -> 133 us (level)
  no operation moved by 1% of the time
where the time goes in v6:
time: 133 us; the launch traced here: 132 us
  waiting for transfers between devices  57.5 us (43%)
  Pallas kernels  38.7 us (29%)
  starting transfers between devices  33 us (25%)
  local copies, waits for them, and re-layouts  2.76 us (2%)
    ppermute x22, waiting for transfers between devices, send(): return lax.ppermute(array, both, pairs)  57.5 us
    ppermute x22, starting transfers between devices, send(): return lax.ppermute(array, both, pairs)  33 us
    pallas_call x4, Pallas kernels, product(): pl.pallas_call(body, grid=(width // tile,), in_specs=in_specs, out_specs=...  29.5 us
    pallas_call x4, Pallas kernels, spread_call(): pl.pallas_call(body, grid_spec=pltpu.PrefetchScalarGridSpec(num_scalar_pr...  6.63 us
  transfers between devices with their start and end apart: 22, of which 9 were waited for; matrix products, arithmetic and copies ran while one was open for 1% of the time, Pallas kernels for 20%

profile of v6, /device:TPU:0, one launch (start us, length us, event | category | flops | bytes accessed | tf_op | source)
XLA Modules:
  0.0 132.4 jit_solution(7223655641108644809)
XLA Ops:
  0.0 2.5 %shard_map.55.refs_0_.refs_1_ = bf16[128,3712]{1,0:T(8,128)(2,1)} custom-call(bf16[128,3584]{1,0:T(8,128)(2,1)} %rows_ref.1, f32[1,128]{1,0:T(1,128)} %bitcast.16, f32[8,128]{1,0:T(8,128)} %bitcast.14, s32[8,128]{1,0:T(8,128)} %bitcast.15), custom_call_target="tpu_custom_call" | custom-call | tf_op jit(solution)/shard_map/pallas_call | solution.py:87
  2.5 3.0 %collective-permute-start.3 = (bf16[128,3712]{1,0:T(8,128)(2,1)}, bf16[128,3712]{1,0:T(8,128)(2,1)}, u32[]{:S(2)}, u32[]{:S(2)}) collective-permute-start(bf16[128,3712]{1,0:T(8,128)(2,1)} %shard_map.55.refs_0_.refs_1_), channel_id=1, source_target_pairs={{0,1},{1,0},{2,3},{3,2},{4,5},{5,4},{6,7},{7,6},{8,9},{9,8},{10,11... | collective-permute-start | bytes 2850824 | tf_op jit(solution)/shard_map/pair/ppermute | solution.py:249
  5.6 1.5 %collective-permute-start.2 = (bf16[128,3712]{1,0:T(8,128)(2,1)}, bf16[128,3712]{1,0:T(8,128)(2,1)}, u32[]{:S(2)}, u32[]{:S(2)}) collective-permute-start(bf16[128,3712]{1,0:T(8,128)(2,1)} %shard_map.55.refs_0_.refs_1_), channel_id=1, source_target_pairs={{0,8},{1,9},{2,10},{3,11},{4,12},{5,13},{6,14},{7,15},{8,0},{9,1},... | collective-permute-start | bytes 2850824 | tf_op jit(solution)/shard_map/x_own/ppermute | solution.py:249
  7.0 1.6 %collective-permute-start.1 = (bf16[128,3712]{1,0:T(8,128)(2,1)}, bf16[128,3712]{1,0:T(8,128)(2,1)}, u32[]{:S(2)}, u32[]{:S(2)}) collective-permute-start(bf16[128,3712]{1,0:T(8,128)(2,1)} %shard_map.55.refs_0_.refs_1_), channel_id=1, source_target_pairs={{1,2},{2,1},{5,6},{6,5},{9,10},{10,9},{13,14},{14,13},{17,18},{18,... | collective-permute-start | bytes 2850824 | tf_op jit(solution)/shard_map/mid_a/ppermute | solution.py:249
  8.7 1.6 %dynamic-slice_bitcast_fusion = (bf16[4,4,72,256]{3,2,1,0:T(8,128)(2,1)S(1)}, bf16[4,4,72,256]{3,2,1,0:T(8,128)(2,1)S(1)}, bf16[4,4,72,256]{3,2,1,0:T(8,128)(2,1)S(1)}) fusion(bf16[1,4,4,72,1024]{4,3,2,1,0:T(8,128)(2,1)} %param.9, s32[]{:T(128)S(6)} %select_n.28, s32[]{:T(128)S(6)} %select_n.27, s32[]{:T(128)S(6)} %select_n.26), kind=kLoop, calls=%fused_computation.2 | loop fusion | bytes 3538956 | tf_op jit(solution)/shard_map/dynamic_slice | solution.py:264
  10.3 16.7 %collective-permute-done.3.refs_0_.refs_1_ = bf16[128,3712]{1,0:T(8,128)(2,1)} collective-permute-done((bf16[128,3712]{1,0:T(8,128)(2,1)}, bf16[128,3712]{1,0:T(8,128)(2,1)}, u32[]{:S(2)}, u32[]{:S(2)}) %collective-permute-start.3) | collective-permute-done | bytes 950304 | tf_op jit(solution)/shard_map/pair/ppermute | solution.py:249
  27.0 1.4 %collective-permute-done.2.refs_2_.refs_3_ = bf16[128,3712]{1,0:T(8,128)(2,1)} collective-permute-done((bf16[128,3712]{1,0:T(8,128)(2,1)}, bf16[128,3712]{1,0:T(8,128)(2,1)}, u32[]{:S(2)}, u32[]{:S(2)}) %collective-permute-start.2) | collective-permute-done | bytes 950304 | tf_op jit(solution)/shard_map/x_own/ppermute | solution.py:249
  28.4 1.3 collective-permute-start.8
  29.7 0.7 collective-permute-start.9
  30.4 1.6 %collective-permute-start.4 = (bf16[128,3712]{1,0:T(8,128)(2,1)}, bf16[128,3712]{1,0:T(8,128)(2,1)S(1)}, u32[]{:S(2)}, u32[]{:S(2)}) collective-permute-start(bf16[128,3712]{1,0:T(8,128)(2,1)} %collective-permute-done.3.refs_0_.refs_1_), channel_id=1, source_target_pairs={{0,8},{1,9},{2,10},{3,11},{4,12},{5,13},{6,14},{7,15},{8,0},{9,1},... | collective-permute-start | bytes 2850824 | tf_op jit(solution)/shard_map/x_pair/ppermute | solution.py:249
  32.0 6.5 %collective-permute-start.5 = (bf16[4,4,72,256]{3,2,1,0:T(8,128)(2,1)S(1)}, bf16[4,4,72,256]{3,2,1,0:T(8,128)(2,1)S(1)}, u32[]{:S(2)}, u32[]{:S(2)}) collective-permute-start(bf16[4,4,72,256]{3,2,1,0:T(8,128)(2,1)S(1)} %get-tuple-element.51), channel_id=1, source_target_pairs={{0,1},{1,0},{2,3},{3,2},{4,5},{5,4},{6,7},{7,6},{8,9},{9,8},{10,11... | collective-permute-start | bytes 1769480 | tf_op jit(solution)/shard_map/g_near/ppermute | solution.py:249
  39.2 17.2 %collective-permute-done.8 = bf16[128,3712]{1,0:T(8,128)(2,1)S(1)} collective-permute-done((bf16[128,3712]{1,0:T(8,128)(2,1)}, bf16[128,3712]{1,0:T(8,128)(2,1)S(1)}, u32[]{:S(2)}, u32[]{:S(2)}) %collective-permute-start.8) | collective-permute-done | bytes 950304 | tf_op jit(solution)/shard_map/end_a/ppermute | solution.py:249
  56.5 10.4 %collective-permute-done.5.hidden_ref = bf16[4,4,72,256]{3,2,1,0:T(8,128)(2,1)S(1)} collective-permute-done((bf16[4,4,72,256]{3,2,1,0:T(8,128)(2,1)S(1)}, bf16[4,4,72,256]{3,2,1,0:T(8,128)(2,1)S(1)}, u32[]{:S(2)}, u32[]{:S(2)}) %collective-permute-start.5) | collective-permute-done | bytes 589856 | tf_op jit(solution)/shard_map/g_near/ppermute | solution.py:249
  67.5 1.3 collective-permute-start.10
  68.8 6.6 %collective-permute-start.12 = (bf16[4,4,72,256]{3,2,1,0:T(8,128)(2,1)S(1)}, bf16[4,4,72,256]{3,2,1,0:T(8,128)(2,1)S(1)}, u32[]{:S(2)}, u32[]{:S(2)}) collective-permute-start(bf16[4,4,72,256]{3,2,1,0:T(8,128)(2,1)S(1)} %get-tuple-element.68), channel_id=1, source_target_pairs={{0,2},{3,1},{4,6},{7,5},{8,10},{11,9},{12,14},{15,13},{16,18},{19,... | collective-permute-start | bytes 1769480 | tf_op jit(solution)/shard_map/g_out/ppermute | solution.py:249
  76.0 1.2 copy-done.1
  77.1 2.1 %shard_map.56.refs_0_ = bf16[1024,512]{1,0:T(8,128)(2,1)S(1)} custom-call(s32[3]{0:T(128)S(1)} %pad_add_fusion.where_ref, bf16[4,4,72,1024]{3,2,1,0:T(8,128)(2,1)S(1)} %bitcast.13, bf16[128,3712]{1,0:T(8,128)(2,1)S(1)} %copy-done.1, bf16[128,3712]{1,0:T(8,128)(2,1)} %collective-permute-done.refs_1_.refs_2_, ...), custom_call_target="tpu_custom_call" | custom-call | flops 150994944 | bytes 3407872 | tf_op jit(solution)/shard_map/pallas_call | solution.py:127
  79.2 7.0 %shard_map.57.refs_5_ = bf16[1024,3584]{1,0:T(8,128)(2,1)S(1)} custom-call(bf16[1024,512]{1,0:T(8,128)(2,1)S(1)} %shard_map.56.refs_0_, bf16[128,3712]{1,0:T(8,128)(2,1)S(1)} %copy-done.2, bf16[128,3712]{1,0:T(8,128)(2,1)} %collective-permute-done.refs_1_.refs_2_, bf16[128,3712]{1,0:T(8,128)(2,1)} %collective-permute-done.2.refs_2_.refs_3_, ...), custom_call_target="tpu_custom_call" | custom-call | flops 3758096384 | bytes 18350080 | tf_op jit(solution)/shard_map/pallas_call | solution.py:214
  86.2 1.7 %collective-permute-done.11.refs_3_ = bf16[128,3712]{1,0:T(8,128)(2,1)S(1)} collective-permute-done((bf16[128,3712]{1,0:T(8,128)(2,1)S(1)}, bf16[128,3712]{1,0:T(8,128)(2,1)S(1)}, u32[]{:S(2)}, u32[]{:S(2)}) %collective-permute-start.11) | collective-permute-done | bytes 950304 | tf_op jit(solution)/shard_map/x_far_a/ppermute | solution.py:249
  87.9 3.2 %collective-permute-done.10 = bf16[128,3712]{1,0:T(8,128)(2,1)S(1)} collective-permute-done((bf16[128,3712]{1,0:T(8,128)(2,1)S(1)}, bf16[128,3712]{1,0:T(8,128)(2,1)S(1)}, u32[]{:S(2)}, u32[]{:S(2)}) %collective-permute-start.10) | collective-permute-done | bytes 950304 | tf_op jit(solution)/shard_map/end_b/ppermute | solution.py:249
  91.3 1.3 collective-permute-start.15
  92.6 1.6 %collective-permute-start.17 = (bf16[128,3712]{1,0:T(8,128)(2,1)S(1)}, bf16[128,3712]{1,0:T(8,128)(2,1)S(1)}, u32[]{:S(2)}, u32[]{:S(2)}) collective-permute-start(bf16[128,3712]{1,0:T(8,128)(2,1)S(1)} %broadcast_select_fusion.refs_0_.refs_1_), channel_id=1, source_target_pairs={{0,8},{1,9},{2,10},{3,11},{4,12},{5,13},{6,14},{7,15},{8,0},{9,1},... | collective-permute-start | bytes 2850824 | tf_op jit(solution)/shard_map/x_far_b/ppermute | solution.py:249
  94.6 2.0 %shard_map.58.refs_0_ = bf16[1024,512]{1,0:T(8,128)(2,1)S(1)} custom-call(s32[3]{0:T(128)S(1)} %pad_add_fusion.where_ref, bf16[4,4,72,256]{3,2,1,0:T(8,128)(2,1)S(1)} %collective-permute-done.5.hidden_ref, bf16[128,3712]{1,0:T(8,128)(2,1)} %collective-permute-done.3.refs_0_.refs_1_, bf16[128,3712]{1,0:T(8,128)(2,1)S(1)} %collective-permute-done.14.refs_1_.refs_2_, ...), custom_call_target="tpu_custom_call" | custom-call | flops 150994944 | bytes 1638400 | tf_op jit(solution)/shard_map/pallas_call | solution.py:127
  96.6 7.2 %shard_map.59.refs_5_ = bf16[1024,3584]{1,0:T(8,128)(2,1)S(1)} custom-call(bf16[1024,512]{1,0:T(8,128)(2,1)S(1)} %shard_map.58.refs_0_, bf16[128,3712]{1,0:T(8,128)(2,1)} %collective-permute-done.3.refs_0_.refs_1_, bf16[128,3712]{1,0:T(8,128)(2,1)S(1)} %collective-permute-done.14.refs_1_.refs_2_, ...), custom_call_target="tpu_custom_call" | custom-call | flops 15032385536 | bytes 73400320 | tf_op jit(solution)/shard_map/pallas_call | solution.py:214
  103.8 2.3 %collective-permute-done.15.ends_ref = bf16[4,4,72,256]{3,2,1,0:T(8,128)(2,1)S(1)} collective-permute-done((bf16[4,4,72,256]{3,2,1,0:T(8,128)(2,1)S(1)}, bf16[4,4,72,256]{3,2,1,0:T(8,128)(2,1)S(1)}, u32[]{:S(2)}, u32[]{:S(2)}) %collective-permute-start.15) | collective-permute-done | bytes 589856 | tf_op jit(solution)/shard_map/g_in/ppermute | solution.py:249
  106.1 3.6 %collective-permute-start.16 = (bf16[4,4,72,256]{3,2,1,0:T(8,128)(2,1)S(1)}, bf16[4,4,72,256]{3,2,1,0:T(8,128)(2,1)S(1)}, u32[]{:S(2)}, u32[]{:S(2)}) collective-permute-start(bf16[4,4,72,256]{3,2,1,0:T(8,128)(2,1)S(1)} %get-tuple-element.77), channel_id=1, source_target_pairs={{0,3},{3,0},{4,7},{7,4},{8,11},{11,8},{12,15},{15,12},{16,19},{19,... | collective-permute-start | bytes 1769480 | tf_op jit(solution)/shard_map/g_outer/ppermute | solution.py:249
  109.8 2.6 %collective-permute-done.17.refs_2_.refs_3_ = bf16[128,3712]{1,0:T(8,128)(2,1)S(1)} collective-permute-done((bf16[128,3712]{1,0:T(8,128)(2,1)S(1)}, bf16[128,3712]{1,0:T(8,128)(2,1)S(1)}, u32[]{:S(2)}, u32[]{:S(2)}) %collective-permute-start.17) | collective-permute-done | bytes 950304 | tf_op jit(solution)/shard_map/x_far_b/ppermute | solution.py:249
  112.4 1.3 shard_map.60.refs_0_
  113.7 7.1 %shard_map.61.refs_5_ = bf16[1024,3584]{1,0:T(8,128)(2,1)S(1)} custom-call(bf16[1024,512]{1,0:T(8,128)(2,1)S(1)} %shard_map.60.refs_0_, bf16[128,3712]{1,0:T(8,128)(2,1)S(1)} %broadcast_select_fusion.1.refs_0_.refs_1_, bf16[128,3712]{1,0:T(8,128)(2,1)S(1)} %collective-permute-done.20.refs_1_.refs_2_, bf16[128,3712]{1,0:T(8,128)(2,1)S(1)} %collective-permute-done.11.refs_3_, ...), custom_call_target="tpu_custom_call" | custom-call | flops 15032385536 | bytes 73400320 | tf_op jit(solution)/shard_map/pallas_call | solution.py:214
  120.8 2.0 %collective-permute-done.16.ends_ref = bf16[4,4,72,256]{3,2,1,0:T(8,128)(2,1)S(1)} collective-permute-done((bf16[4,4,72,256]{3,2,1,0:T(8,128)(2,1)S(1)}, bf16[4,4,72,256]{3,2,1,0:T(8,128)(2,1)S(1)}, u32[]{:S(2)}, u32[]{:S(2)}) %collective-permute-start.16) | collective-permute-done | bytes 589856 | tf_op jit(solution)/shard_map/g_outer/ppermute | solution.py:249
  122.8 1.3 shard_map.62.refs_0_
  124.1 8.3 %shard_map.63 = bf16[256,4,3584]{2,1,0:T(4,128)(2,1)} custom-call(bf16[1024,512]{1,0:T(8,128)(2,1)S(1)} %shard_map.62.refs_0_, bf16[128,3712]{1,0:T(8,128)(2,1)S(1)} %broadcast_select_fusion.refs_0_.refs_1_, bf16[128,3712]{1,0:T(8,128)(2,1)S(1)} %collective-permute-done.19.refs_1_.refs_2_, bf16[128,3712]{1,0:T(8,128)(2,1)S(1)} %collective-permute-done.17.refs_2_.refs_3_, ...), custom_call_target="tpu_custom_call" | custom-call | flops 3758096384 | bytes 18350080 | tf_op jit(solution)/shard_map/pallas_call | solution.py:214
  (32 shorter events, 2.8 us)
Async XLA Ops:
  0.0 76.0 %copy-start = (bf16[1,4,4,72,1024]{4,3,2,1,0:T(8,128)(2,1)S(1)}, bf16[1,4,4,72,1024]{4,3,2,1,0:T(8,128)(2,1)}, u32[]{:S(2)}) copy-start(bf16[1,4,4,72,1024]{4,3,2,1,0:T(8,128)(2,1)} %param.9) | copy-start | bytes 7077892
  2.5 76.7 %copy-start.2 = (bf16[128,3712]{1,0:T(8,128)(2,1)S(1)}, bf16[128,3712]{1,0:T(8,128)(2,1)}, u32[]{:S(2)}) copy-start(bf16[128,3712]{1,0:T(8,128)(2,1)} %shard_map.55.refs_0_.refs_1_) | copy-start | bytes 2850820
  2.5 24.5 %collective-permute-start.3 = (bf16[128,3712]{1,0:T(8,128)(2,1)}, bf16[128,3712]{1,0:T(8,128)(2,1)}, u32[]{:S(2)}, u32[]{:S(2)}) collective-permute-start(bf16[128,3712]{1,0:T(8,128)(2,1)} %shard_map.55.refs_0_.refs_1_), channel_id=1, source_target_pairs={{0,1},{1,0},{2,3},{3,2},{4,5},{5,4},{6,7},{7,6},{8,9},{9,8},{10,11... | collective-permute-start | bytes 2850824 | tf_op jit(solution)/shard_map/pair/ppermute | solution.py:249
  5.6 22.8 %collective-permute-start.2 = (bf16[128,3712]{1,0:T(8,128)(2,1)}, bf16[128,3712]{1,0:T(8,128)(2,1)}, u32[]{:S(2)}, u32[]{:S(2)}) collective-permute-start(bf16[128,3712]{1,0:T(8,128)(2,1)} %shard_map.55.refs_0_.refs_1_), channel_id=1, source_target_pairs={{0,8},{1,9},{2,10},{3,11},{4,12},{5,13},{6,14},{7,15},{8,0},{9,1},... | collective-permute-start | bytes 2850824 | tf_op jit(solution)/shard_map/x_own/ppermute | solution.py:249
  7.0 21.3 %collective-permute-start.1 = (bf16[128,3712]{1,0:T(8,128)(2,1)}, bf16[128,3712]{1,0:T(8,128)(2,1)}, u32[]{:S(2)}, u32[]{:S(2)}) collective-permute-start(bf16[128,3712]{1,0:T(8,128)(2,1)} %shard_map.55.refs_0_.refs_1_), channel_id=1, source_target_pairs={{1,2},{2,1},{5,6},{6,5},{9,10},{10,9},{13,14},{14,13},{17,18},{18,... | collective-permute-start | bytes 2850824 | tf_op jit(solution)/shard_map/mid_a/ppermute | solution.py:249
  8.7 19.7 %collective-permute-start = (bf16[128,3712]{1,0:T(8,128)(2,1)}, bf16[128,3712]{1,0:T(8,128)(2,1)}, u32[]{:S(2)}, u32[]{:S(2)}) collective-permute-start(bf16[128,3712]{1,0:T(8,128)(2,1)} %shard_map.55.refs_0_.refs_1_), channel_id=1, source_target_pairs={{0,4},{1,5},{2,6},{3,7},{4,0},{5,1},{6,2},{7,3},{8,12},{9,13},{10,... | collective-permute-start | bytes 2850824 | tf_op jit(solution)/shard_map/c_own/ppermute | solution.py:249
  28.4 28.0 %collective-permute-start.8 = (bf16[128,3712]{1,0:T(8,128)(2,1)}, bf16[128,3712]{1,0:T(8,128)(2,1)S(1)}, u32[]{:S(2)}, u32[]{:S(2)}) collective-permute-start(bf16[128,3712]{1,0:T(8,128)(2,1)} %collective-permute-done.1), channel_id=1, source_target_pairs={{1,0},{2,3},{5,4},{6,7},{9,8},{10,11},{13,12},{14,15},{17,16},{18,... | collective-permute-start | bytes 2850824 | tf_op jit(solution)/shard_map/end_a/ppermute | solution.py:249
  29.7 37.2 %collective-permute-start.9 = (bf16[128,3712]{1,0:T(8,128)(2,1)}, bf16[128,3712]{1,0:T(8,128)(2,1)S(1)}, u32[]{:S(2)}, u32[]{:S(2)}) collective-permute-start(bf16[128,3712]{1,0:T(8,128)(2,1)} %collective-permute-done.3.refs_0_.refs_1_), channel_id=1, source_target_pairs={{1,2},{2,1},{5,6},{6,5},{9,10},{10,9},{13,14},{14,13},{17,18},{18,... | collective-permute-start | bytes 2850824 | tf_op jit(solution)/shard_map/mid_b/ppermute | solution.py:249
  30.4 36.5 %collective-permute-start.4 = (bf16[128,3712]{1,0:T(8,128)(2,1)}, bf16[128,3712]{1,0:T(8,128)(2,1)S(1)}, u32[]{:S(2)}, u32[]{:S(2)}) collective-permute-start(bf16[128,3712]{1,0:T(8,128)(2,1)} %collective-permute-done.3.refs_0_.refs_1_), channel_id=1, source_target_pairs={{0,8},{1,9},{2,10},{3,11},{4,12},{5,13},{6,14},{7,15},{8,0},{9,1},... | collective-permute-start | bytes 2850824 | tf_op jit(solution)/shard_map/x_pair/ppermute | solution.py:249
  32.0 34.9 %collective-permute-start.5 = (bf16[4,4,72,256]{3,2,1,0:T(8,128)(2,1)S(1)}, bf16[4,4,72,256]{3,2,1,0:T(8,128)(2,1)S(1)}, u32[]{:S(2)}, u32[]{:S(2)}) collective-permute-start(bf16[4,4,72,256]{3,2,1,0:T(8,128)(2,1)S(1)} %get-tuple-element.51), channel_id=1, source_target_pairs={{0,1},{1,0},{2,3},{3,2},{4,5},{5,4},{6,7},{7,6},{8,9},{9,8},{10,11... | collective-permute-start | bytes 1769480 | tf_op jit(solution)/shard_map/g_near/ppermute | solution.py:249
  38.5 28.4 %collective-permute-start.6 = (bf16[4,4,72,256]{3,2,1,0:T(8,128)(2,1)S(1)}, bf16[4,4,72,256]{3,2,1,0:T(8,128)(2,1)S(1)}, u32[]{:S(2)}, u32[]{:S(2)}) collective-permute-start(bf16[4,4,72,256]{3,2,1,0:T(8,128)(2,1)S(1)} %get-tuple-element.77), channel_id=1, source_target_pairs={{1,2},{2,1},{5,6},{6,5},{9,10},{10,9},{13,14},{14,13},{17,18},{18,... | collective-permute-start | bytes 1769480 | tf_op jit(solution)/shard_map/g_inner/ppermute | solution.py:249
  56.3 10.5 %collective-permute-start.7 = (bf16[128,3712]{1,0:T(8,128)(2,1)}, bf16[128,3712]{1,0:T(8,128)(2,1)S(1)}, u32[]{:S(2)}, u32[]{:S(2)}) collective-permute-start(bf16[128,3712]{1,0:T(8,128)(2,1)} %collective-permute-done.2.refs_2_.refs_3_), channel_id=1, source_target_pairs={{0,4},{1,5},{2,6},{3,7},{4,0},{5,1},{6,2},{7,3},{8,12},{9,13},{10,... | collective-permute-start | bytes 2850824 | tf_op jit(solution)/shard_map/c_xown/ppermute | solution.py:249
  66.9 21.0 %collective-permute-start.11 = (bf16[128,3712]{1,0:T(8,128)(2,1)S(1)}, bf16[128,3712]{1,0:T(8,128)(2,1)S(1)}, u32[]{:S(2)}, u32[]{:S(2)}) collective-permute-start(bf16[128,3712]{1,0:T(8,128)(2,1)S(1)} %broadcast_select_fusion.1.refs_0_.refs_1_), channel_id=1, source_target_pairs={{0,8},{1,9},{2,10},{3,11},{4,12},{5,13},{6,14},{7,15},{8,0},{9,1},... | collective-permute-start | bytes 2850824 | tf_op jit(solution)/shard_map/x_far_a/ppermute | solution.py:249
  67.5 23.6 %collective-permute-start.10 = (bf16[128,3712]{1,0:T(8,128)(2,1)S(1)}, bf16[128,3712]{1,0:T(8,128)(2,1)S(1)}, u32[]{:S(2)}, u32[]{:S(2)}) collective-permute-start(bf16[128,3712]{1,0:T(8,128)(2,1)S(1)} %collective-permute-done.9), channel_id=1, source_target_pairs={{1,0},{2,3},{5,4},{6,7},{9,8},{10,11},{13,12},{14,15},{17,16},{18,... | collective-permute-start | bytes 2850824 | tf_op jit(solution)/shard_map/end_b/ppermute | solution.py:249
  68.8 22.5 %collective-permute-start.12 = (bf16[4,4,72,256]{3,2,1,0:T(8,128)(2,1)S(1)}, bf16[4,4,72,256]{3,2,1,0:T(8,128)(2,1)S(1)}, u32[]{:S(2)}, u32[]{:S(2)}) collective-permute-start(bf16[4,4,72,256]{3,2,1,0:T(8,128)(2,1)S(1)} %get-tuple-element.68), channel_id=1, source_target_pairs={{0,2},{3,1},{4,6},{7,5},{8,10},{11,9},{12,14},{15,13},{16,18},{19,... | collective-permute-start | bytes 1769480 | tf_op jit(solution)/shard_map/g_out/ppermute | solution.py:249
  75.4 15.9 %collective-permute-start.13 = (bf16[128,3712]{1,0:T(8,128)(2,1)S(1)}, bf16[128,3712]{1,0:T(8,128)(2,1)S(1)}, u32[]{:S(2)}, u32[]{:S(2)}) collective-permute-start(bf16[128,3712]{1,0:T(8,128)(2,1)S(1)} %collective-permute-done.4.refs_2_.refs_3_), channel_id=1, source_target_pairs={{0,4},{1,5},{2,6},{3,7},{4,0},{5,1},{6,2},{7,3},{8,12},{9,13},{10,... | collective-permute-start | bytes 2850824 | tf_op jit(solution)/shard_map/c_xpair/ppermute | solution.py:249
  75.5 15.8 %collective-permute-start.14 = (bf16[128,3712]{1,0:T(8,128)(2,1)}, bf16[128,3712]{1,0:T(8,128)(2,1)S(1)}, u32[]{:S(2)}, u32[]{:S(2)}) collective-permute-start(bf16[128,3712]{1,0:T(8,128)(2,1)} %collective-permute-done.3.refs_0_.refs_1_), channel_id=1, source_target_pairs={{0,4},{1,5},{2,6},{3,7},{4,0},{5,1},{6,2},{7,3},{8,12},{9,13},{10,... | collective-permute-start | bytes 2850824 | tf_op jit(solution)/shard_map/c_pair/ppermute | solution.py:249
  76.0 1.2 copy-start.1
  91.3 14.8 %collective-permute-start.15 = (bf16[4,4,72,256]{3,2,1,0:T(8,128)(2,1)S(1)}, bf16[4,4,72,256]{3,2,1,0:T(8,128)(2,1)S(1)}, u32[]{:S(2)}, u32[]{:S(2)}) collective-permute-start(bf16[4,4,72,256]{3,2,1,0:T(8,128)(2,1)S(1)} %get-tuple-element.68), channel_id=1, source_target_pairs={{2,0},{1,3},{6,4},{5,7},{10,8},{9,11},{14,12},{13,15},{18,16},{17,... | collective-permute-start | bytes 1769480 | tf_op jit(solution)/shard_map/g_in/ppermute | solution.py:249
  92.6 19.8 %collective-permute-start.17 = (bf16[128,3712]{1,0:T(8,128)(2,1)S(1)}, bf16[128,3712]{1,0:T(8,128)(2,1)S(1)}, u32[]{:S(2)}, u32[]{:S(2)}) collective-permute-start(bf16[128,3712]{1,0:T(8,128)(2,1)S(1)} %broadcast_select_fusion.refs_0_.refs_1_), channel_id=1, source_target_pairs={{0,8},{1,9},{2,10},{3,11},{4,12},{5,13},{6,14},{7,15},{8,0},{9,1},... | collective-permute-start | bytes 2850824 | tf_op jit(solution)/shard_map/x_far_b/ppermute | solution.py:249
  94.1 18.3 %collective-permute-start.21 = (bf16[128,3712]{1,0:T(8,128)(2,1)S(1)}, bf16[128,3712]{1,0:T(8,128)(2,1)S(1)}, u32[]{:S(2)}, u32[]{:S(2)}) collective-permute-start(bf16[128,3712]{1,0:T(8,128)(2,1)S(1)} %collective-permute-done.11.refs_3_), channel_id=1, source_target_pairs={{0,4},{1,5},{2,6},{3,7},{4,0},{5,1},{6,2},{7,3},{8,12},{9,13},{10,... | collective-permute-start | bytes 2850824 | tf_op jit(solution)/shard_map/c_xfar_a/ppermute | solution.py:249
  94.1 18.3 %collective-permute-start.20 = (bf16[128,3712]{1,0:T(8,128)(2,1)S(1)}, bf16[128,3712]{1,0:T(8,128)(2,1)S(1)}, u32[]{:S(2)}, u32[]{:S(2)}) collective-permute-start(bf16[128,3712]{1,0:T(8,128)(2,1)S(1)} %broadcast_select_fusion.1.refs_0_.refs_1_), channel_id=1, source_target_pairs={{0,4},{1,5},{2,6},{3,7},{4,0},{5,1},{6,2},{7,3},{8,12},{9,13},{10,... | collective-permute-start | bytes 2850824 | tf_op jit(solution)/shard_map/c_far_a/ppermute | solution.py:249
  106.1 16.7 %collective-permute-start.16 = (bf16[4,4,72,256]{3,2,1,0:T(8,128)(2,1)S(1)}, bf16[4,4,72,256]{3,2,1,0:T(8,128)(2,1)S(1)}, u32[]{:S(2)}, u32[]{:S(2)}) collective-permute-start(bf16[4,4,72,256]{3,2,1,0:T(8,128)(2,1)S(1)} %get-tuple-element.77), channel_id=1, source_target_pairs={{0,3},{3,0},{4,7},{7,4},{8,11},{11,8},{12,15},{15,12},{16,19},{19,... | collective-permute-start | bytes 1769480 | tf_op jit(solution)/shard_map/g_outer/ppermute | solution.py:249
  109.7 13.0 %collective-permute-start.19 = (bf16[128,3712]{1,0:T(8,128)(2,1)S(1)}, bf16[128,3712]{1,0:T(8,128)(2,1)S(1)}, u32[]{:S(2)}, u32[]{:S(2)}) collective-permute-start(bf16[128,3712]{1,0:T(8,128)(2,1)S(1)} %broadcast_select_fusion.refs_0_.refs_1_), channel_id=1, source_target_pairs={{0,4},{1,5},{2,6},{3,7},{4,0},{5,1},{6,2},{7,3},{8,12},{9,13},{10,... | collective-permute-start | bytes 2850824 | tf_op jit(solution)/shard_map/c_far_b/ppermute | solution.py:249
  112.4 10.4 %collective-permute-start.18 = (bf16[128,3712]{1,0:T(8,128)(2,1)S(1)}, bf16[128,3712]{1,0:T(8,128)(2,1)S(1)}, u32[]{:S(2)}, u32[]{:S(2)}) collective-permute-start(bf16[128,3712]{1,0:T(8,128)(2,1)S(1)} %collective-permute-done.17.refs_2_.refs_3_), channel_id=1, source_target_pairs={{0,4},{1,5},{2,6},{3,7},{4,0},{5,1},{6,2},{7,3},{8,12},{9,13},{10,... | collective-permute-start | bytes 2850824 | tf_op jit(solution)/shard_map/c_xfar_b/ppermute | solution.py:249
